TPU v7x, 32 devices: a whole 2x2x4 slice. The times are simulated.
32 devices in a mesh: freq: 4 (over y, core), slab: 8 (over z, x).
Axes of the slice: x: 2, y: 2, z: 4, core: 2. Of those that a mesh axis runs over, the one named last changes fastest.
Arguments:
- inverse_permittivity: float32 [64, 24, 512], P('slab'), may hold values from 0.083 to 1
- forward_fields: float32 [4, 6, 64, 24, 512], P('freq', None, 'slab'), may hold values from -6 to 6
- adjoint_fields: float32 [4, 6, 64, 24, 512], P('freq', None, 'slab'), may hold values from -6 to 6
- source_wave: float32 [4, 3], P('freq'), may hold values from -4 to 4
- source_profile: float32 [4, 512], P('freq'), may hold values from -4 to 4
- adjoint_wave: float32 [4, 3], P('freq'), may hold values from -4 to 4
- adjoint_profile: float32 [4, 512], P('freq'), may hold values from -4 to 4
- source_plane: int32 [4], P('freq'), may hold values from 0 to 23
- monitor_plane: int32 [4], P('freq'), may hold values from 0 to 23
- radius_map: int32 [8, 8], P('slab'), may hold values from 1 to 4
- design_mask: int32 [8, 8], P('slab'), may hold values 0 or 1
- design_density: float32 [512, 64], P('slab'), may hold values from 0 to 1
Outputs:
- forward_out: float32 [4, 6, 64, 24, 512], P('freq', None, 'slab')
- adjoint_out: float32 [4, 6, 64, 24, 512], P('freq', None, 'slab')
- projected: float32 [512, 64], P('slab')
Inputs may be any that keep to these rules, and one draw needn't show every extreme that they name: `radius_map`: filter radius of a tile in cells.
All inputs are finite; a program needn't handle non-finite values. No bound on the sum of `design_mask` on one device may be relied on, other than what follows from the above.
Results may differ from a plain program's by a relative error of at most 0.0003.
Values sent between devices are 32-bit elements; how exact they have to be, the bound alone decides.
No kernel may reach another device: no remote copies, remote signals or barrier semaphores. Data moves between devices by JAX's collectives and lax.ppermute only.
A program may use at most 64 MiB of HBM per device.

v0:
```python
import math

import jax
import jax.numpy as jnp
from jax import lax
from jax.sharding import PartitionSpec as P

NY = 512
NZ = 24
FREQS = 4
STEPS = 3
RMAX = 4


courant = 0.5
sharpness = 4.0
midpoint = 0.5
step_size = 0.3


def shifted(shard, axis, by):
    length = lax.axis_size(axis)
    pairs = [(i, i + by) for i in range(length) if 0 <= i + by < length]
    return lax.ppermute(shard, axis, pairs)


def padded_2(cells, sides, width):
    for axis, dim in sides:
        count = lax.axis_size(axis)
        ends = count - 1
        head = lax.slice_in_dim(cells, 0, width, axis=dim)
        tail = lax.slice_in_dim(cells, cells.shape[dim] - width, cells.shape[dim], axis=dim)
        cells = jnp.concatenate(
            [
                lax.ppermute(tail, axis, [(i, (i + 1) % count) for i in range(ends)]),
                cells,
                lax.ppermute(head, axis, [((i + 1) % count, i) for i in range(ends)]),
            ],
            axis=dim,
        )
    return cells


def forward_cell(field, axis):
    axis = field.ndim + axis
    size = field.shape[axis]
    inner = lax.slice_in_dim(field, 1, size, axis=axis)
    edge = jnp.zeros_like(lax.slice_in_dim(field, 0, 1, axis=axis))
    return jnp.concatenate([inner, edge], axis=axis)


def backward_cell(field, axis):
    axis = field.ndim + axis
    size = field.shape[axis]
    inner = lax.slice_in_dim(field, 0, size - 1, axis=axis)
    edge = jnp.zeros_like(lax.slice_in_dim(field, 0, 1, axis=axis))
    return jnp.concatenate([edge, inner], axis=axis)


def next_rows(field, plane):
    return jnp.concatenate([field[:, :, 1:], plane[:, :, None]], axis=2)


def prior_rows(field, plane):
    return jnp.concatenate([plane[:, :, None], field[:, :, :-1]], axis=2)


def send_electric(first, second):
    planes = shifted(jnp.stack([first[:, :, 0], second[:, :, 0]]), "slab", -1)
    return (planes[0], planes[1])


def send_magnetic(first, second):
    planes = shifted(jnp.stack([first[:, :, -1], second[:, :, -1]]), "slab", 1)
    return (planes[0], planes[1])


def yee_update(fields, inverse, source, electric_planes, magnetic_planes):
    elec_x, elec_y, elec_z, magn_x, magn_y, magn_z = fields
    next_y, next_z = electric_planes(elec_y, elec_z)
    magn_x = magn_x - courant * (
        forward_cell(elec_z, -1) - elec_z - (forward_cell(elec_y, -2) - elec_y)
    )
    magn_y = magn_y - courant * (
        forward_cell(elec_x, -2) - elec_x - (next_rows(elec_z, next_z) - elec_z)
    )
    magn_z = magn_z - courant * (
        next_rows(elec_y, next_y) - elec_y - (forward_cell(elec_x, -1) - elec_x)
    )
    prior_y, prior_z = magnetic_planes(magn_y, magn_z)
    elec_x = (
        elec_x
        + courant
        * inverse
        * (magn_z - backward_cell(magn_z, -1) - (magn_y - backward_cell(magn_y, -2)))
        + source
    )
    elec_y = elec_y + courant * inverse * (
        magn_x - backward_cell(magn_x, -2) - (magn_z - prior_rows(magn_z, prior_z))
    )
    elec_z = elec_z + courant * inverse * (
        magn_y - prior_rows(magn_y, prior_y) - (magn_x - backward_cell(magn_x, -1))
    )
    return (elec_x, elec_y, elec_z, magn_x, magn_y, magn_z)


def intersection_of(fields):
    total = 0.0
    for component in range(3):
        part = fields[component]
        total = total + part[0] * part[1]
    return jnp.sum(total, axis=2)


def on_device(
    inverse_permittivity,
    forward_fields,
    adjoint_fields,
    source_wave,
    source_profile,
    adjoint_wave,
    adjoint_profile,
    source_plane,
    monitor_plane,
    radius_map,
    design_mask,
    design_density,
):
    groups = forward_fields.shape[0]
    rows = forward_fields.shape[2]
    waves = jnp.stack([source_wave, adjoint_wave])
    profiles = jnp.stack([source_profile, adjoint_profile])
    planes = jnp.stack([source_plane, monitor_plane])
    plane_hit = (jnp.arange(NZ, dtype=jnp.int32)[None, None, :] == planes[:, :, None]).astype(
        jnp.float32
    )
    state = jnp.stack([forward_fields, adjoint_fields])
    intersection = jnp.zeros((groups, rows, NY), jnp.float32)
    fields = tuple((state[:, :, component] for component in range(6)))
    for turn in range(STEPS):
        source = (
            waves[:, :, turn][:, :, None, None, None]
            * plane_hit[:, :, None, :, None]
            * profiles[:, :, None, None, :]
        )
        fields = yee_update(fields, inverse_permittivity, source, send_electric, send_magnetic)
        intersection = intersection + intersection_of(fields)
    forward_out = jnp.stack([member[0] for member in fields], axis=1)
    adjoint_out = jnp.stack([member[1] for member in fields], axis=1)
    local = jnp.sum(intersection, axis=0)
    sent = lax.psum_scatter(local, "freq", scatter_dimension=0, tiled=True).T
    tiles = lax.all_to_all(sent, "slab", split_axis=0, concat_axis=1, tiled=True)
    tile_rows = tiles.shape[0]
    width = design_density.shape[1]
    freq_count = lax.axis_size("freq")
    gathered = lax.all_gather(tiles, "freq", axis=1, tiled=True)
    tiles = (
        gathered.reshape(tile_rows, freq_count, lax.axis_size("slab"), rows // freq_count)
        .transpose(0, 2, 1, 3)
        .reshape(tile_rows, width)
    )
    columns = width // radius_map.shape[1]
    radius = jnp.repeat(radius_map, columns, axis=1).astype(jnp.float32)
    chosen = jnp.repeat(design_mask, columns, axis=1).astype(jnp.float32)
    scale = step_size / math.sqrt(3 * STEPS * NZ * FREQS)
    updated = design_density + scale * chosen * tiles
    rim = padded_2(updated, (("slab", 0),), RMAX)
    padded = jnp.pad(rim, ((0, 0), (RMAX, RMAX)))
    global_y = (
        lax.axis_index("slab") * tile_rows
        - RMAX
        + jnp.arange(tile_rows + 2 * RMAX, dtype=jnp.int32)
    )
    inside_y = ((global_y >= 0) & (global_y < NY)).astype(jnp.float32)
    inside_x = jnp.pad(jnp.ones((width,), jnp.float32), RMAX)
    inside = inside_y[:, None] * inside_x[None, :]
    numerator = jnp.zeros((tile_rows, width), jnp.float32)
    weight_total = jnp.zeros((tile_rows, width), jnp.float32)
    for offset_y in range(2 * RMAX + 1):
        for offset_x in range(2 * RMAX + 1):
            distance = jnp.sqrt(
                jnp.asarray((offset_y - RMAX) ** 2 + (offset_x - RMAX) ** 2, jnp.float32)
            )
            weight = jnp.maximum(radius - distance, 0.0)
            piece = padded[offset_y : offset_y + tile_rows, offset_x : offset_x + width]
            present = inside[offset_y : offset_y + tile_rows, offset_x : offset_x + width]
            numerator = numerator + weight * present * piece
            weight_total = weight_total + weight * present
    filtered = numerator / weight_total
    base = math.tanh(sharpness * midpoint)
    projected = (base + jnp.tanh(sharpness * (filtered - midpoint))) / (
        base + math.tanh(sharpness * (1.0 - midpoint))
    )
    return (forward_out, adjoint_out, projected)


def solution(mesh):
    return jax.shard_map(
        on_device,
        mesh=mesh,
        in_specs=(
            P("slab", None, None),
            P("freq", None, "slab", None, None),
            P("freq", None, "slab", None, None),
            P("freq", None),
            P("freq", None),
            P("freq", None),
            P("freq", None),
            P("freq"),
            P("freq"),
            P("slab", None),
            P("slab", None),
            P("slab", None),
        ),
        out_specs=(
            P("freq", None, "slab", None, None),
            P("freq", None, "slab", None, None),
            P("slab", None),
        ),
        check_vma=False,
    )
```

profile of v0, /device:TPU:0, one launch (start us, length us, event | category | flops | bytes accessed | tf_op | source)
XLA Modules:
  0.0 122.8 jit_solution(7881519342884582676)
XLA Ops:
  0.6 1.9 %fusion.9 = (f32[2,1,8,24,512]{4,3,0,2,1:T(8,128)S(1)}, f32[2,1,8,24,512]{4,3,0,2,1:T(8,128)S(1)}, f32[2,1,8,24,512]{4,3,0,2,1:T(8,128)S(1)}) fusion(f32[1,1,6,8,24,512]{5,4,0,3,2,1:T(8,128)} %bitcast.164, f32[1,1,6,8,24,512]{5,4,0,3,2,1:T(8,128)} %bitcast.166), kind=kLoop, calls=%fused_computation.19 | loop fusion | flops 589824 | bytes 7077888 | tf_op jit(solution)/shard_map/squeeze | solution.py:139
  22.8 4.0 %fusion.13 = (f32[2,1,8,24,512]{4,3,0,2,1:T(8,128)S(1)}, f32[2,1,8,24,512]{4,3,0,2,1:T(8,128)S(1)}, f32[2,1,8,24,512]{4,3,0,2,1:T(8,128)S(1)}) fusion(f32[1,1,6,8,24,512]{5,4,0,3,2,1:T(8,128)} %bitcast.167, f32[1,1,6,8,24,512]{5,4,0,3,2,1:T(8,128)} %bitcast.165, f32[2,1,8,24,512]{4,3,0,2,1:T(8,128)S(1)} %get-tuple-element.18, ...), kind=kLoop, calls=%fused_computation.24 | loop fusion | flops 3932160 | bytes 14087168 | tf_op jit(solution)/shard_map/sub | solution.py:81
  26.8 5.5 %collective-permute-start.1 = (f32[2,2,1,24,512]{4,3,1,2,0:T(8,128)S(1)}, f32[2,2,1,24,512]{4,3,1,2,0:T(8,128)S(1)}, u32[]{:S(2)}, u32[]{:S(2)}) collective-permute-start(f32[2,2,1,24,512]{4,3,1,2,0:T(8,128)S(1)} %pad_maximum_fusion.2), channel_id=1, source_target_pairs={{0,1},{1,2},{2,3},{3,4},{4,5},{5,6},{6,7},{8,9},{9,10},{10,11},{11... | collective-permute-start | bytes 589832 | tf_op jit(solution)/shard_map/ppermute | solution.py:24
  32.5 3.9 %collective-permute-done.1 = f32[2,2,1,24,512]{4,3,1,2,0:T(8,128)S(1)} collective-permute-done((f32[2,2,1,24,512]{4,3,1,2,0:T(8,128)S(1)}, f32[2,2,1,24,512]{4,3,1,2,0:T(8,128)S(1)}, u32[]{:S(2)}, u32[]{:S(2)}) %collective-permute-start.1) | collective-permute-done | bytes 196640 | tf_op jit(solution)/shard_map/ppermute | solution.py:24
  36.5 1.5 %fusion.20 = (f32[2,1,8,24,512]{4,3,0,2,1:T(8,128)S(1)}, f32[2,1,8,24,512]{4,3,0,2,1:T(8,128)S(1)}, f32[2,1,8,24,512]{4,3,0,2,1:T(8,128)S(1)}) fusion(f32[2,1,8,24,512]{4,3,0,2,1:T(8,128)S(1)} %get-tuple-element.18, f32[2,1,8,24,512]{4,3,0,2,1:T(8,128)S(1)} %get-tuple-element.16, f32[2,1,7,24,512]{4,3,0,2,1:T(8,128)S(1)} %slice.1076, ...), kind=kLoop, calls=%fused_computation.34 | loop fusion | flops 3538944 | bytes 12219392 | tf_op jit(solution)/shard_map/add | solution.py:98
  38.0 1.3 %collective-permute-start.2 = (f32[2,2,1,24,512]{4,3,1,2,0:T(8,128)S(1)}, f32[2,2,1,24,512]{4,3,1,2,0:T(8,128)S(1)}, u32[]{:S(2)}, u32[]{:S(2)}) collective-permute-start(f32[2,2,1,24,512]{4,3,1,2,0:T(8,128)S(1)} %pad_maximum_fusion.3), channel_id=1, source_target_pairs={{1,0},{2,1},{3,2},{4,3},{5,4},{6,5},{7,6},{9,8},{10,9},{11,10},{12... | collective-permute-start | bytes 589832 | tf_op jit(solution)/shard_map/ppermute | solution.py:24
  40.3 6.1 %collective-permute-done.2 = f32[2,2,1,24,512]{4,3,1,2,0:T(8,128)S(1)} collective-permute-done((f32[2,2,1,24,512]{4,3,1,2,0:T(8,128)S(1)}, f32[2,2,1,24,512]{4,3,1,2,0:T(8,128)S(1)}, u32[]{:S(2)}, u32[]{:S(2)}) %collective-permute-start.2) | collective-permute-done | bytes 196640 | tf_op jit(solution)/shard_map/ppermute | solution.py:24
  47.7 5.1 %collective-permute-start.3 = (f32[2,2,1,24,512]{4,3,1,2,0:T(8,128)S(1)}, f32[2,2,1,24,512]{4,3,1,2,0:T(8,128)S(1)}, u32[]{:S(2)}, u32[]{:S(2)}) collective-permute-start(f32[2,2,1,24,512]{4,3,1,2,0:T(8,128)S(1)} %pad_maximum_fusion.4), channel_id=1, source_target_pairs={{0,1},{1,2},{2,3},{3,4},{4,5},{5,6},{6,7},{8,9},{9,10},{10,11},{11... | collective-permute-start | bytes 589832 | tf_op jit(solution)/shard_map/ppermute | solution.py:24
  53.0 3.0 %collective-permute-done.3 = f32[2,2,1,24,512]{4,3,1,2,0:T(8,128)S(1)} collective-permute-done((f32[2,2,1,24,512]{4,3,1,2,0:T(8,128)S(1)}, f32[2,2,1,24,512]{4,3,1,2,0:T(8,128)S(1)}, u32[]{:S(2)}, u32[]{:S(2)}) %collective-permute-start.3) | collective-permute-done | bytes 196640 | tf_op jit(solution)/shard_map/ppermute | solution.py:24
  57.6 1.3 %collective-permute-start.4 = (f32[2,2,1,24,512]{4,3,1,2,0:T(8,128)S(1)}, f32[2,2,1,24,512]{4,3,1,2,0:T(8,128)S(1)}, u32[]{:S(2)}, u32[]{:S(2)}) collective-permute-start(f32[2,2,1,24,512]{4,3,1,2,0:T(8,128)S(1)} %pad_maximum_fusion.5), channel_id=1, source_target_pairs={{1,0},{2,1},{3,2},{4,3},{5,4},{6,5},{7,6},{9,8},{10,9},{11,10},{12... | collective-permute-start | bytes 589832 | tf_op jit(solution)/shard_map/ppermute | solution.py:24
  59.8 5.9 %collective-permute-done.4 = f32[2,2,1,24,512]{4,3,1,2,0:T(8,128)S(1)} collective-permute-done((f32[2,2,1,24,512]{4,3,1,2,0:T(8,128)S(1)}, f32[2,2,1,24,512]{4,3,1,2,0:T(8,128)S(1)}, u32[]{:S(2)}, u32[]{:S(2)}) %collective-permute-start.4) | collective-permute-done | bytes 196640 | tf_op jit(solution)/shard_map/ppermute | solution.py:24
  66.9 5.0 %collective-permute-start.5 = (f32[2,2,1,24,512]{4,3,1,2,0:T(8,128)S(1)}, f32[2,2,1,24,512]{4,3,1,2,0:T(8,128)S(1)}, u32[]{:S(2)}, u32[]{:S(2)}) collective-permute-start(f32[2,2,1,24,512]{4,3,1,2,0:T(8,128)S(1)} %pad_maximum_fusion.6), channel_id=1, source_target_pairs={{0,1},{1,2},{2,3},{3,4},{4,5},{5,6},{6,7},{8,9},{9,10},{10,11},{11... | collective-permute-start | bytes 589832 | tf_op jit(solution)/shard_map/ppermute | solution.py:24
  72.6 2.3 %collective-permute-done.5 = f32[2,2,1,24,512]{4,3,1,2,0:T(8,128)S(1)} collective-permute-done((f32[2,2,1,24,512]{4,3,1,2,0:T(8,128)S(1)}, f32[2,2,1,24,512]{4,3,1,2,0:T(8,128)S(1)}, u32[]{:S(2)}, u32[]{:S(2)}) %collective-permute-start.5) | collective-permute-done | bytes 196640 | tf_op jit(solution)/shard_map/ppermute | solution.py:24
  74.9 2.7 %fusion.43 = (f32[2,1,8,24,512]{4,3,2,1,0:T(8,128)}, f32[2,1,8,24,512]{4,3,2,1,0:T(8,128)}, f32[2,1,8,24,512]{4,3,2,1,0:T(8,128)S(1)}) fusion(f32[2,1,8,24,512]{4,3,2,1,0:T(8,128)S(1)} %get-tuple-element.25, f32[2,1,8,24,512]{4,3,2,1,0:T(8,128)S(1)} %get-tuple-element.43, f32[2,1,7,24,512]{4,3,2,1,0:T(8,128)S(1)} %slice.1122, ...), kind=kLoop, calls=%fused_computation.66 | loop fusion | flops 3735552 | bytes 12317696 | tf_op jit(solution)/shard_map/add | solution.py:101
  77.6 2.5 %add_reduce_fusion = (f32[8,512]{1,0:T(8,128)S(1)}, f32[1,6,8,24,512]{4,3,2,1,0:T(8,128)}, f32[1,6,8,24,512]{4,3,2,1,0:T(8,128)}) fusion(f32[2,1,8,24,512]{4,3,2,1,0:T(8,128)} %get-tuple-element.21, f32[2,1,8,24,512]{4,3,2,1,0:T(8,128)} %get-tuple-element.22, f32[2,1,8,24,512]{4,3,2,1,0:T(8,128)S(1)} %get-tuple-element.23), kind=kLoop, calls=%fused_computation.96 | loop fusion | flops 585726 | bytes 3162112 | tf_op jit(solution)/shard_map/reduce_sum | solution.py:112
  80.1 10.1 %all-reduce.26 = f32[8,512]{1,0:T(8,128)S(1)} all-reduce(f32[8,512]{1,0:T(8,128)S(1)} %add_add_fusion.2), channel_id=2, replica_groups=mesh['freq'=4,'slab'=8] {'freq'}, use_global_device_ids=true, to_apply=%region_3.0.clone | all-reduce | flops 4096 | bytes 32768
  91.0 7.2 %all-to-all-start = ((f32[8,1,128]{2,1,0:T(1,128)}), f32[8,1,128]{2,1,0:T(1,128)S(1)}, u32[]{:S(2)}, u32[]{:S(2)}) async-start(f32[8,1,128]{2,1,0:T(1,128)} %reshape.778), calls=%async_computation | async-start | bytes 8192 | tf_op jit(solution)/shard_map/all_to_all | solution.py:152
  98.2 2.0 %slice_dynamic-update-slice_fusion.7 = (f32[1,6,8,24,512]{4,3,2,1,0:T(8,128)}, f32[1,6,8,24,512]{4,3,2,1,0:T(8,128)}) fusion(f32[1,6,8,24,512]{4,3,2,1,0:T(8,128)} %get-tuple-element.30, f32[2,1,8,24,512]{4,3,2,1,0:T(8,128)} %get-tuple-element.22, f32[1,6,8,24,512]{4,3,2,1,0:T(8,128)} %get-tuple-element.31), kind=kLoop, calls=%fused_computation.98 | loop fusion | bytes 1572864
  100.2 2.0 %slice_dynamic-update-slice_fusion.6 = (f32[1,6,8,24,512]{4,3,2,1,0:T(8,128)}, f32[1,6,8,24,512]{4,3,2,1,0:T(8,128)}) fusion(f32[1,6,8,24,512]{4,3,2,1,0:T(8,128)} %get-tuple-element.40, f32[2,1,8,24,512]{4,3,2,1,0:T(8,128)} %get-tuple-element.21, f32[1,6,8,24,512]{4,3,2,1,0:T(8,128)} %get-tuple-element.41), kind=kLoop, calls=%fused_computation.97 | loop fusion | bytes 1572864
  105.8 5.2 %all_gather.3 = f32[64,64]{0,1:T(8,128)S(1)} all-gather(f32[64,16]{0,1:T(8,128)S(1)} %bitcast.170), channel_id=1, replica_groups=mesh['freq'=4,'slab'=8] {'freq'}, dimensions={1}, use_global_device_ids=true | all-gather | bytes 20480 | tf_op jit(solution)/shard_map/all_gather | solution.py:156
  111.2 3.5 %collective-permute-start.6 = (f32[4,64]{0,1:T(8,128)S(1)}, f32[4,64]{0,1:T(8,128)S(1)}, u32[]{:S(2)}, u32[]{:S(2)}) collective-permute-start(f32[4,64]{0,1:T(8,128)S(1)} %get-tuple-element.62), channel_id=1, source_target_pairs={{0,1},{1,2},{2,3},{3,4},{4,5},{5,6},{6,7},{8,9},{9,10},{10,11},{11... | collective-permute-start | bytes 3080 | tf_op jit(solution)/shard_map/ppermute | solution.py:35
  114.7 1.3 %collective-permute-start.7 = (f32[4,64]{0,1:T(8,128)S(1)}, f32[4,64]{0,1:T(8,128)S(1)}, u32[]{:S(2)}, u32[]{:S(2)}) collective-permute-start(f32[4,64]{0,1:T(8,128)S(1)} %get-tuple-element.63), channel_id=1, source_target_pairs={{1,0},{2,1},{3,2},{4,3},{5,4},{6,5},{7,6},{9,8},{10,9},{11,10},{12... | collective-permute-start | bytes 3080 | tf_op jit(solution)/shard_map/ppermute | solution.py:37
  116.9 3.6 %collective-permute-done.7 = f32[4,64]{0,1:T(8,128)S(1)} collective-permute-done((f32[4,64]{0,1:T(8,128)S(1)}, f32[4,64]{0,1:T(8,128)S(1)}, u32[]{:S(2)}, u32[]{:S(2)}) %collective-permute-start.7) | collective-permute-done | bytes 1056 | tf_op jit(solution)/shard_map/ppermute | solution.py:37
  120.6 1.5 %fusion.143 = f32[64,64]{0,1:T(8,128)S(1)} fusion(f32[72,72]{0,1:T(8,128)S(1)} %select_maximum_fusion, f32[72,72]{0,1:T(8,128)S(1)} %broadcast_multiply_fusion.4, f32[4,64]{0,1:T(8,128)S(1)} %collective-permute-done.7, f32[64,64]{0,1:T(8,128)S(1)} %multiply_add_fusion.1, f32[4,64]{0,1:T(8,128)S(1)} %collective-permute-done.6, f32[64]{0:T(128)S(1)} %copy-done.5, ...), kind=kLoop, calls=%fused_computation.397 | loop fusion | flops 1372160 | bytes 2545408 | tf_op jit(solution)/shard_map/div | solution.py:191
  (140 shorter events, 31.4 us)
Async XLA Ops:
  3.2 18.6 %collective-permute-start = (f32[2,2,1,24,512]{4,3,1,2,0:T(8,128)}, f32[2,2,1,24,512]{4,3,1,2,0:T(8,128)}, u32[]{:S(2)}, u32[]{:S(2)}) collective-permute-start(f32[2,2,1,24,512]{4,3,1,2,0:T(8,128)} %pad_maximum_fusion.1), channel_id=1, source_target_pairs={{1,0},{2,1},{3,2},{4,3},{5,4},{6,5},{7,6},{9,8},{10,9},{11,10},{12... | collective-permute-start | bytes 589832 | tf_op jit(solution)/shard_map/ppermute | solution.py:24
  6.5 5.2 %copy-start.8 = (s32[1,8]{1,0:T(1,128)S(1)}, s32[1,8]{1,0:T(1,128)}, u32[]{:S(2)}) copy-start(s32[1,8]{1,0:T(1,128)} %param.22) | copy-start | bytes 100
  6.6 5.4 %copy-start.7 = (s32[1,8]{1,0:T(1,128)S(1)}, s32[1,8]{1,0:T(1,128)}, u32[]{:S(2)}) copy-start(s32[1,8]{1,0:T(1,128)} %param.21) | copy-start | bytes 100
  6.6 10.4 %copy-start = (f32[64,64]{1,0:T(8,128)S(1)}, f32[64,64]{1,0:T(8,128)}, u32[]{:S(2)}) copy-start(f32[64,64]{1,0:T(8,128)} %param.23) | copy-start | bytes 49156
  26.8 9.6 %collective-permute-start.1 = (f32[2,2,1,24,512]{4,3,1,2,0:T(8,128)S(1)}, f32[2,2,1,24,512]{4,3,1,2,0:T(8,128)S(1)}, u32[]{:S(2)}, u32[]{:S(2)}) collective-permute-start(f32[2,2,1,24,512]{4,3,1,2,0:T(8,128)S(1)} %pad_maximum_fusion.2), channel_id=1, source_target_pairs={{0,1},{1,2},{2,3},{3,4},{4,5},{5,6},{6,7},{8,9},{9,10},{10,11},{11... | collective-permute-start | bytes 589832 | tf_op jit(solution)/shard_map/ppermute | solution.py:24
  36.4 2.8 %copy-start.6 = (f32[72]{0:T(128)S(1)}, f32[72]{0:T(128)}, u32[]{:S(2)}) copy-start(f32[72]{0:T(128)} %and_convert_fusion) | copy-start | bytes 868
  38.0 8.4 %collective-permute-start.2 = (f32[2,2,1,24,512]{4,3,1,2,0:T(8,128)S(1)}, f32[2,2,1,24,512]{4,3,1,2,0:T(8,128)S(1)}, u32[]{:S(2)}, u32[]{:S(2)}) collective-permute-start(f32[2,2,1,24,512]{4,3,1,2,0:T(8,128)S(1)} %pad_maximum_fusion.3), channel_id=1, source_target_pairs={{1,0},{2,1},{3,2},{4,3},{5,4},{6,5},{7,6},{9,8},{10,9},{11,10},{12... | collective-permute-start | bytes 589832 | tf_op jit(solution)/shard_map/ppermute | solution.py:24
  47.7 8.3 %collective-permute-start.3 = (f32[2,2,1,24,512]{4,3,1,2,0:T(8,128)S(1)}, f32[2,2,1,24,512]{4,3,1,2,0:T(8,128)S(1)}, u32[]{:S(2)}, u32[]{:S(2)}) collective-permute-start(f32[2,2,1,24,512]{4,3,1,2,0:T(8,128)S(1)} %pad_maximum_fusion.4), channel_id=1, source_target_pairs={{0,1},{1,2},{2,3},{3,4},{4,5},{5,6},{6,7},{8,9},{9,10},{10,11},{11... | collective-permute-start | bytes 589832 | tf_op jit(solution)/shard_map/ppermute | solution.py:24
  57.6 8.0 %collective-permute-start.4 = (f32[2,2,1,24,512]{4,3,1,2,0:T(8,128)S(1)}, f32[2,2,1,24,512]{4,3,1,2,0:T(8,128)S(1)}, u32[]{:S(2)}, u32[]{:S(2)}) collective-permute-start(f32[2,2,1,24,512]{4,3,1,2,0:T(8,128)S(1)} %pad_maximum_fusion.5), channel_id=1, source_target_pairs={{1,0},{2,1},{3,2},{4,3},{5,4},{6,5},{7,6},{9,8},{10,9},{11,10},{12... | collective-permute-start | bytes 589832 | tf_op jit(solution)/shard_map/ppermute | solution.py:24
  66.9 8.0 %collective-permute-start.5 = (f32[2,2,1,24,512]{4,3,1,2,0:T(8,128)S(1)}, f32[2,2,1,24,512]{4,3,1,2,0:T(8,128)S(1)}, u32[]{:S(2)}, u32[]{:S(2)}) collective-permute-start(f32[2,2,1,24,512]{4,3,1,2,0:T(8,128)S(1)} %pad_maximum_fusion.6), channel_id=1, source_target_pairs={{0,1},{1,2},{2,3},{3,4},{4,5},{5,6},{6,7},{8,9},{9,10},{10,11},{11... | collective-permute-start | bytes 589832 | tf_op jit(solution)/shard_map/ppermute | solution.py:24
  91.0 13.6 %all-to-all-start = ((f32[8,1,128]{2,1,0:T(1,128)}), f32[8,1,128]{2,1,0:T(1,128)S(1)}, u32[]{:S(2)}, u32[]{:S(2)}) async-start(f32[8,1,128]{2,1,0:T(1,128)} %reshape.778), calls=%async_computation | async-start | bytes 8192 | tf_op jit(solution)/shard_map/all_to_all | solution.py:152
  102.3 18.3 %copy-start.1 = (f32[64]{0:T(128)S(1)}, f32[64]{0:T(128)}, u32[]{:S(2)}) copy-start(f32[64]{0:T(128)} %max.323) | copy-start | bytes 772
  102.3 18.3 %copy-start.2 = (f32[64]{0:T(128)S(1)}, f32[64]{0:T(128)}, u32[]{:S(2)}) copy-start(f32[64]{0:T(128)} %max.326) | copy-start | bytes 772
  102.3 18.3 %copy-start.3 = (f32[64]{0:T(128)S(1)}, f32[64]{0:T(128)}, u32[]{:S(2)}) copy-start(f32[64]{0:T(128)} %max.329) | copy-start | bytes 772
  102.3 18.4 %copy-start.4 = (f32[64]{0:T(128)S(1)}, f32[64]{0:T(128)}, u32[]{:S(2)}) copy-start(f32[64]{0:T(128)} %max.332) | copy-start | bytes 772
  102.3 18.4 %copy-start.5 = (f32[64]{0:T(128)S(1)}, f32[64]{0:T(128)}, u32[]{:S(2)}) copy-start(f32[64]{0:T(128)} %max.335) | copy-start | bytes 772
  111.2 5.8 %collective-permute-start.6 = (f32[4,64]{0,1:T(8,128)S(1)}, f32[4,64]{0,1:T(8,128)S(1)}, u32[]{:S(2)}, u32[]{:S(2)}) collective-permute-start(f32[4,64]{0,1:T(8,128)S(1)} %get-tuple-element.62), channel_id=1, source_target_pairs={{0,1},{1,2},{2,3},{3,4},{4,5},{5,6},{6,7},{8,9},{9,10},{10,11},{11... | collective-permute-start | bytes 3080 | tf_op jit(solution)/shard_map/ppermute | solution.py:35
  114.7 5.8 %collective-permute-start.7 = (f32[4,64]{0,1:T(8,128)S(1)}, f32[4,64]{0,1:T(8,128)S(1)}, u32[]{:S(2)}, u32[]{:S(2)}) collective-permute-start(f32[4,64]{0,1:T(8,128)S(1)} %get-tuple-element.63), channel_id=1, source_target_pairs={{1,0},{2,1},{3,2},{4,3},{5,4},{6,5},{7,6},{9,8},{10,9},{11,10},{12... | collective-permute-start | bytes 3080 | tf_op jit(solution)/shard_map/ppermute | solution.py:37
where the time goes:
time: 123 us
  starting transfers between devices  31.5 us (26%)
  waiting for transfers between devices  25.2 us (20%)
  local copies, waits for them, and re-layouts  24.1 us (20%)
  other arithmetic  23.6 us (19%)
  blocking collectives  15.3 us (12%)
  between operations  3.15 us (3%)
    ppermute x6, waiting for transfers between devices, shifted(): return lax.ppermute(shard, axis, pairs)  21.2 us
    ppermute x6, starting transfers between devices, shifted(): return lax.ppermute(shard, axis, pairs)  19.5 us
    unnamed x1, blocking collectives  10.1 us
    unnamed x27, local copies, waits for them, and re-layouts  8.77 us
    all_to_all x1, starting transfers between devices, on_device(): lax.all_to_all(sent, 'slab', split_axis=0, concat_axis=1, tiled=True)  7.17 us
    slice x12, local copies, waits for them, and re-layouts, forward_cell(): inner = lax.slice_in_dim(field, 1, size, axis=axis)  5.89 us
    sub x3, other arithmetic, yee_update(): magn_x - courant * (forward_cell(elec_z, -1) - elec_z - (forward_cell(ele...  5.3 us
    all_gather x1, blocking collectives, on_device(): gathered = lax.all_gather(tiles, 'freq', axis=1, tiled=True)  5.18 us
  transfers between devices with their start and end apart: 9, of which 7 were waited for; matrix products, arithmetic and copies ran while one was open for 20% of the time, Pallas kernels for 0%

commit v1 on v0

v1 whole, which is shorter than its diff:
```python
import math

import jax
import jax.numpy as jnp
from jax import lax
from jax.experimental import pallas as pl
from jax.experimental.pallas import tpu as pltpu
from jax.sharding import PartitionSpec as P

NY = 512
NZ = 24
FREQS = 4
STEPS = 3
RMAX = 4


courant = 0.5
sharpness = 4.0
midpoint = 0.5
step_size = 0.3

PLANE = (NZ, NY)
VMEM = pl.BlockSpec(memory_space=pltpu.VMEM)
SMEM = pl.BlockSpec(memory_space=pltpu.SMEM)
ANY = pl.BlockSpec(memory_space=pl.ANY)
GRANT = 24 * 1024 * 1024


def ahead(plane, axis):
    size = plane.shape[axis]
    at = lax.broadcasted_iota(jnp.int32, plane.shape, axis)
    return jnp.where(at == size - 1, 0.0, pltpu.roll(plane, size - 1, axis))


def behind(plane, axis):
    at = lax.broadcasted_iota(jnp.int32, plane.shape, axis)
    return jnp.where(at == 0, 0.0, pltpu.roll(plane, 1, axis))


def dy_f(plane):
    return ahead(plane, 1) - plane


def dz_f(plane):
    return ahead(plane, 0) - plane


def dy_b(plane):
    return plane - behind(plane, 1)


def dz_b(plane):
    return plane - behind(plane, 0)


def magnetic_x(magn_x, elec):
    return magn_x - courant * (dy_f(elec[2]) - dz_f(elec[1]))


def magnetic_yz(magn, elec, following):
    next_y, next_z = (0.0, 0.0) if following is None else following
    return (
        magn[0] - courant * (dz_f(elec[0]) - (next_z - elec[2])),
        magn[1] - courant * ((next_y - elec[1]) - dy_f(elec[0])),
    )


def magnetic(magn, elec, following):
    return (magnetic_x(magn[0], elec),) + magnetic_yz(magn[1:], elec, following)


def electric_x(elec_x, magn, scaled):
    return elec_x + scaled * (dy_b(magn[2]) - dz_b(magn[1]))


def electric_yz(elec, magn, prior, scaled):
    prior_y, prior_z = (0.0, 0.0) if prior is None else prior
    return (
        elec[0] + scaled * (dz_b(magn[0]) - (magn[2] - prior_z)),
        elec[1] + scaled * ((magn[1] - prior_y) - dy_b(magn[0])),
    )


def electric(elec, magn, prior, scaled, source):
    return (electric_x(elec[0], magn, scaled) + source,) + electric_yz(
        elec[1:], magn, prior, scaled
    )


def source_of(run, turn, wave, profile, plane):
    at = lax.broadcasted_iota(jnp.int32, PLANE, 0)
    return jnp.where(at == plane[run], wave[run, turn] * profile[pl.ds(run, 1), :], 0.0)


def kernel_call(body, out_shape, in_specs, out_specs, scratch, name, flops=1, **more):
    sizes = sum(math.prod(s.shape) * 4 for s in jax.tree.leaves(out_shape))
    return pl.pallas_call(
        body,
        out_shape=out_shape,
        in_specs=in_specs,
        out_specs=out_specs,
        scratch_shapes=scratch,
        compiler_params=pltpu.CompilerParams(vmem_limit_bytes=GRANT),
        cost_estimate=pl.CostEstimate(flops=flops, bytes_accessed=2 * sizes, transcendentals=0),
        name=name,
        **more,
    )


def shaped(*shape):
    return jax.ShapeDtypeStruct(shape, jnp.float32)


def first_planes(fwd, adj, inverse, to_prior, to_next, rows_in, sems):
    rows = inverse.shape[0]
    copies = [
        pltpu.make_async_copy(fwd.at[0, :, rows - 1], rows_in.at[0], sems.at[0]),
        pltpu.make_async_copy(adj.at[0, :, rows - 1], rows_in.at[1], sems.at[1]),
        pltpu.make_async_copy(fwd.at[0, pl.ds(1, 2), 0], to_prior.at[pl.ds(0, 2)], sems.at[2]),
        pltpu.make_async_copy(adj.at[0, pl.ds(1, 2), 0], to_prior.at[pl.ds(2, 2)], sems.at[3]),
        pltpu.make_async_copy(inverse.at[0], to_prior.at[4], sems.at[4]),
        pltpu.make_async_copy(inverse.at[rows - 1], to_next.at[4], sems.at[5]),
    ]
    for copy in copies:
        copy.start()
    for run in range(2):
        copies[run].wait()
        state = [rows_in[run, k] for k in range(6)]
        magn = magnetic_yz(state[4:], state[:3], None)
        to_next[2 * run] = magn[0]
        to_next[2 * run + 1] = magn[1]
    for copy in copies[2:]:
        copy.wait()


def later_planes(fwd, adj, inverse, wave, profile, plane, to_prior, to_next, head, tail, inv, sems):
    rows = inverse.shape[0]
    copies = []
    for run, fields in enumerate((fwd, adj)):
        copies.append(
            pltpu.make_async_copy(fields.at[0, :, pl.ds(0, 3)], head.at[run], sems.at[2 * run])
        )
        copies.append(
            pltpu.make_async_copy(
                fields.at[0, :, pl.ds(rows - 3, 3)], tail.at[run], sems.at[2 * run + 1]
            )
        )
    copies.append(pltpu.make_async_copy(inverse, inv, sems.at[4]))
    for copy in copies:
        copy.start()
    for copy in copies:
        copy.wait()

    def one_run(run, carry):
        def row(ref, x):
            return (
                tuple(ref[run, k, x] for k in range(3)),
                tuple(ref[run, k, x] for k in range(3, 6)),
            )

        source = source_of(run, 0, wave, profile, plane)
        (elec_0, magn_0), (elec_1, magn_1) = row(head, 0), row(head, 1)
        scaled_0, scaled_1 = courant * inv[0], courant * inv[1]
        magn_0 = magnetic(magn_0, elec_0, elec_1[1:])
        magn_1 = magnetic(magn_1, elec_1, (head[run, 1, 2], head[run, 2, 2]))
        elec_0 = electric(elec_0, magn_0, None, scaled_0, source)
        to_prior[2 * run] = elec_0[1]
        to_prior[2 * run + 1] = elec_0[2]
        after = electric_yz(elec_1[1:], magn_1, magn_0[1:], scaled_1)
        magn_0 = magnetic(magn_0, elec_0, after)
        sent = electric_yz(elec_0[1:], magn_0, None, scaled_0)
        to_prior[4 + 2 * run] = sent[0]
        to_prior[4 + 2 * run + 1] = sent[1]
        (elec_5, magn_5), (elec_6, magn_6), (elec_7, magn_7) = (row(tail, x) for x in range(3))
        scaled_6, scaled_7 = courant * inv[rows - 2], courant * inv[rows - 1]
        yz_5 = magnetic_yz(magn_5[1:], elec_5, elec_6[1:])
        magn_6 = magnetic(magn_6, elec_6, elec_7[1:])
        magn_7 = magnetic(magn_7, elec_7, None)
        elec_6 = electric(elec_6, magn_6, yz_5, scaled_6, source)
        elec_7 = electric(elec_7, magn_7, magn_6[1:], scaled_7, source)
        yz_6 = magnetic_yz(magn_6[1:], elec_6, elec_7[1:])
        magn_7 = magnetic(magn_7, elec_7, None)
        to_next[2 * run] = magn_7[1]
        to_next[2 * run + 1] = magn_7[2]
        source = source_of(run, 1, wave, profile, plane)
        elec_7 = electric(elec_7, magn_7, yz_6, scaled_7, source)
        sent = magnetic_yz(magn_7[1:], elec_7, None)
        to_next[4 + 2 * run] = sent[0]
        to_next[4 + 2 * run + 1] = sent[1]
        return carry

    lax.fori_loop(0, 2, one_run, 0)


def load_row(state, run, first, x):
    return tuple(state[run, first + k, x] for k in range(3))


def store_row(state, run, first, x, planes):
    for k, value in enumerate(planes):
        state[run, first + k, x] = value


def advance_magnetic(state, run, x, following):
    magn = magnetic(load_row(state, run, 3, x), load_row(state, run, 0, x), following)
    store_row(state, run, 3, x, magn)
    return magn


def advance_electric(state, run, x, prior, scaled, source):
    elec = electric(
        load_row(state, run, 0, x), load_row(state, run, 3, x), prior, scaled, source
    )
    store_row(state, run, 0, x, elec)
    return elec


def electric_at(state, run, x):
    return (state[run, 1, x], state[run, 2, x])


def magnetic_at(state, run, x):
    return (state[run, 4, x], state[run, 5, x])


def products(state, x):
    total = state[0, 0, x] * state[1, 0, x]
    for k in (1, 2):
        total = total + state[0, k, x] * state[1, k, x]
    return jnp.sum(total.reshape(NZ // 8, 8, NY), axis=0)


def interior(fwd, adj, inverse, wave, profile, plane, fwd_out, adj_out, share, state, inv, sems):
    rows = inverse.shape[0]
    into = [
        pltpu.make_async_copy(fwd.at[0], state.at[0], sems.at[0]),
        pltpu.make_async_copy(adj.at[0], state.at[1], sems.at[1]),
        pltpu.make_async_copy(inverse, inv, sems.at[2]),
    ]
    for copy in into:
        copy.start()
    for copy in into:
        copy.wait()
    share[...] = jnp.zeros_like(share)
    for turn in range(STEPS):

        def one_run(run, carry, turn=turn):
            source = source_of(run, turn, wave, profile, plane)

            def one_row(x, carry):
                advance_magnetic(state, run, x, electric_at(state, run, x + 1))

                @pl.when(x > turn)
                def _():
                    advance_electric(
                        state, run, x, magnetic_at(state, run, x - 1), courant * inv[x], source
                    )

                return carry

            return lax.fori_loop(turn, rows - 1 - turn, one_row, carry)

        lax.fori_loop(0, 2, one_run, 0)

        def gather(x, carry):
            share[x] = share[x] + products(state, x)
            return carry

        lax.fori_loop(turn + 1, rows - 1 - turn, gather, 0)
    out = [
        pltpu.make_async_copy(state.at[0], fwd_out.at[0], sems.at[0]),
        pltpu.make_async_copy(state.at[1], adj_out.at[0], sems.at[1]),
    ]
    for copy in out:
        copy.start()
    for copy in out:
        copy.wait()


def borders(
    fwd, adj, inverse, wave, profile, plane, has_prior, share, prior_a, prior_b, next_a, next_b,
    fwd_out, adj_out, blocks, state, inv, resp, total, sems,
):
    rows = inverse.shape[0]
    head, tail = pl.ds(0, 3), pl.ds(rows - 4, 4)
    into = [pltpu.make_async_copy(inverse, inv, sems.at[4])]
    for run, fields in enumerate((fwd, adj)):
        for part, where in enumerate((head, tail)):
            into.append(
                pltpu.make_async_copy(
                    fields.at[0, :, where], state.at[run, :, where], sems.at[2 * run + part]
                )
            )
    for copy in into:
        copy.start()
    for copy in into:
        copy.wait()
    last = rows - 1
    flagged = courant * has_prior[0]
    for turn in range(STEPS):

        def one_run(run, carry, turn=turn):
            source = source_of(run, turn, wave, profile, plane)
            scaled_prior = courant * prior_a[4]
            scaled_next = courant * next_a[4]
            own_y, own_z = electric_at(state, run, 0)
            if turn == 0:
                magn_r = (None, flagged * own_z, -flagged * own_y)
                received = (prior_a[2 * run], prior_a[2 * run + 1])
            else:
                elec_r = tuple(resp[run, k] for k in range(3))
                old = tuple(resp[run, k] for k in range(3, 6))
                magn_r = (
                    old[0] - courant * (dy_f(elec_r[2]) - dz_f(elec_r[1])),
                    old[1] - courant * (dz_f(elec_r[0]) + elec_r[2]) + flagged * own_z,
                    old[2] + courant * (elec_r[1] + dy_f(elec_r[0])) - flagged * own_y,
                )
                at = 4 * (turn - 1) + 2 * run
                received = (prior_b[at], prior_b[at + 1])
            prior = (received[0] + magn_r[1], received[1] + magn_r[2])
            if turn == 0:
                resp[run, 0] = scaled_prior * (dy_b(magn_r[2]) - dz_b(magn_r[1]))
                resp[run, 1] = -scaled_prior * magn_r[2]
                resp[run, 2] = scaled_prior * magn_r[1]
                resp[run, 3] = jnp.zeros(PLANE, jnp.float32)
            elif turn == 1:
                resp[run, 0] = elec_r[0] + scaled_prior * (dy_b(magn_r[2]) - dz_b(magn_r[1]))
                resp[run, 1] = elec_r[1] + scaled_prior * (
                    dz_b(magn_r[0]) - (magn_r[2] + courant * elec_r[1])
                )
                resp[run, 2] = elec_r[2] + scaled_prior * (
                    (magn_r[1] - courant * elec_r[2]) - dy_b(magn_r[0])
                )
                resp[run, 3] = magn_r[0]
            if turn < STEPS - 1:
                resp[run, 4] = magn_r[1]
                resp[run, 5] = magn_r[2]
            for x in range(turn):
                advance_magnetic(state, run, x, electric_at(state, run, x + 1))
            for x in range(turn + 1):
                before = prior if x == 0 else magnetic_at(state, run, x - 1)
                advance_electric(state, run, x, before, courant * inv[x], source)
            if turn == 0:
                following = (next_a[2 * run], next_a[2 * run + 1])
            else:
                at = 4 * (turn - 1) + 2 * run
                following = (next_b[at] + resp[run, 6], next_b[at + 1] + resp[run, 7])
            for x in range(last - turn, last):
                advance_magnetic(state, run, x, electric_at(state, run, x + 1))
            magn = advance_magnetic(state, run, last, following)
            for x in range(last - turn, last + 1):
                before = magnetic_at(state, run, x - 1)
                advance_electric(state, run, x, before, courant * inv[x], source)
            if turn == 0:
                resp[run, 6] = scaled_next * magn[2]
                resp[run, 7] = -scaled_next * magn[1]
            elif turn == 1:
                elec_y, elec_z = resp[run, 6], resp[run, 7]
                magn_x = -courant * (dy_f(elec_z) - dz_f(elec_y))
                resp[run, 6] = elec_y + scaled_next * (
                    dz_b(magn_x) - (courant * elec_y - magn[2])
                )
                resp[run, 7] = elec_z + scaled_next * (
                    (-courant * elec_z - magn[1]) - dy_b(magn_x)
                )
            return carry

        lax.fori_loop(0, 2, one_run, 0)
        if turn == STEPS - 1:
            out = []
            for run, fields in enumerate((fwd_out, adj_out)):
                for part, where in enumerate((pl.ds(0, 3), pl.ds(rows - 3, 3))):
                    out.append(
                        pltpu.make_async_copy(
                            state.at[run, :, where], fields.at[0, :, where], sems.at[2 * run + part]
                        )
                    )
            for copy in out:
                copy.start()
        for x in list(range(turn + 1)) + list(range(last - turn, last + 1)):
            before = share[x] if turn == min(x, last - x) else total[x]
            total[x] = before + products(state, x)
    for x in range(STEPS, rows - STEPS):
        total[x] = share[x]
    summed = jnp.sum(total[...], axis=1)
    slabs, width = blocks.shape[1], blocks.shape[3]
    for k in range(slabs):
        turned = pltpu.roll(summed, (RMAX - k * (NY // slabs)) % NY, 1)
        for f in range(blocks.shape[0]):
            blocks[f, k] = turned[:, :width]
    for copy in out:
        copy.wait()


def moved(rows, by):
    if by == 0:
        return rows
    count = rows.shape[0]
    at = lax.broadcasted_iota(jnp.int32, rows.shape, 0)
    keep = at < count - by if by > 0 else at >= -by
    return jnp.where(keep, pltpu.roll(rows, (-by) % count, 0), 0.0)


def weighted(cells, radius):
    tile = cells.shape[1] - 2 * RMAX
    columns = [cells[:, RMAX : RMAX + tile]]
    for a in range(1, RMAX + 1):
        columns.append(
            cells[:, RMAX - a : RMAX - a + tile] + cells[:, RMAX + a : RMAX + a + tile]
        )
    rings = {}
    for a in range(RMAX + 1):
        for b in range(RMAX + 1):
            part = columns[a]
            if b > 0:
                part = moved(part, b) + moved(part, -b)
            square = a * a + b * b
            rings[square] = rings[square] + part if square in rings else part
    total = None
    for square, part in rings.items():
        term = jnp.maximum(radius - math.sqrt(square), 0.0) * part
        total = term if total is None else total + term
    return total


def by_tile(values, count):
    columns = count // values.shape[1]
    at = lax.broadcasted_iota(jnp.int32, (count, 1), 0) // columns
    spread = jnp.zeros((count, 1), jnp.float32)
    for k in range(values.shape[1]):
        spread = jnp.where(at == k, values[0, k].astype(jnp.float32), spread)
    return spread


def weight_sums(radius_map, inside, weights):
    weights[...] = weighted(inside[...], by_tile(radius_map, inside.shape[0]))


def project(blocks, density, chosen, weights, radius_map, projected):
    freqs, slabs, rows, width = blocks.shape
    gradient = jnp.sum(blocks[...], axis=0).reshape(slabs * rows, width)
    updated = density[...] + chosen[...] * gradient
    numerator = weighted(updated, by_tile(radius_map, slabs * rows))
    filtered = numerator / weights[...]
    base = math.tanh(sharpness * midpoint)
    value = (base + jnp.tanh(sharpness * (filtered - midpoint))) / (
        base + math.tanh(sharpness * (1.0 - midpoint))
    )
    projected[...] = value.T


def shifted(shard, axis, by):
    length = lax.axis_size(axis)
    pairs = [(i, i + by) for i in range(length) if 0 <= i + by < length]
    return lax.ppermute(shard, axis, pairs)


def on_device(
    inverse_permittivity,
    forward_fields,
    adjoint_fields,
    source_wave,
    source_profile,
    adjoint_wave,
    adjoint_profile,
    source_plane,
    monitor_plane,
    radius_map,
    design_mask,
    design_density,
):
    rows = forward_fields.shape[2]
    freqs, slabs = lax.axis_size("freq"), lax.axis_size("slab")
    slab = lax.axis_index("slab")
    tile_rows, width = design_density.shape
    reach = tile_rows + 2 * RMAX
    wave = jnp.concatenate([source_wave, adjoint_wave])
    profile = jnp.concatenate([source_profile, adjoint_profile])
    plane = jnp.concatenate([source_plane, monitor_plane])
    fields = (forward_fields, adjoint_fields, inverse_permittivity)
    sources = (wave, profile, plane)
    source_specs = [SMEM, VMEM, SMEM]
    dma = pltpu.SemaphoreType.DMA
    work = 45 * 12 * 1024

    to_prior_a, to_next_a = kernel_call(
        first_planes,
        (shaped(5, *PLANE), shaped(5, *PLANE)),
        [ANY] * 3,
        (VMEM, VMEM),
        [pltpu.VMEM((2, 6) + PLANE, jnp.float32), dma((6,))],
        "first_planes",
    )(*fields)
    next_a = shifted(to_prior_a, "slab", -1)
    prior_a = shifted(to_next_a, "slab", 1)
    to_prior_b, to_next_b = kernel_call(
        later_planes,
        (shaped(8, *PLANE), shaped(8, *PLANE)),
        [ANY] * 3 + source_specs,
        (VMEM, VMEM),
        [
            pltpu.VMEM((2, 6, 3) + PLANE, jnp.float32),
            pltpu.VMEM((2, 6, 3) + PLANE, jnp.float32),
            pltpu.VMEM((rows,) + PLANE, jnp.float32),
            dma((5,)),
        ],
        "later_planes",
        flops=14 * work,
    )(*fields, *sources)
    next_b = shifted(to_prior_b, "slab", -1)
    prior_b = shifted(to_next_b, "slab", 1)

    chosen_row = jnp.repeat(design_mask, width // design_mask.shape[1], axis=1).astype(jnp.float32)
    top = shifted(jnp.concatenate([design_density[-RMAX:], chosen_row]), "slab", 1)
    bottom = shifted(jnp.concatenate([design_density[:RMAX], chosen_row]), "slab", -1)
    density = jnp.concatenate([top[:RMAX], design_density, bottom[:RMAX]]).T
    scale = step_size / math.sqrt(3 * STEPS * NZ * FREQS)
    chosen = scale * jnp.concatenate(
        [
            jnp.broadcast_to(top[RMAX:], (RMAX, width)),
            jnp.broadcast_to(chosen_row, (tile_rows, width)),
            jnp.broadcast_to(bottom[RMAX:], (RMAX, width)),
        ]
    ).T
    global_y = slab * tile_rows - RMAX + jnp.arange(reach, dtype=jnp.int32)
    inside_y = ((global_y >= 0) & (global_y < NY)).astype(jnp.float32)
    inside = jnp.broadcast_to(inside_y[None, :], (width, reach))
    weights = kernel_call(
        weight_sums, shaped(width, tile_rows), [SMEM, VMEM], VMEM, [], "weight_sums"
    )(radius_map, inside)

    state_shape = (2, 6, rows) + PLANE
    forward_part, adjoint_part, share = kernel_call(
        interior,
        (
            shaped(*forward_fields.shape),
            shaped(*adjoint_fields.shape),
            shaped(rows, 8, NY),
        ),
        [ANY] * 3 + source_specs,
        (ANY, ANY, VMEM),
        [
            pltpu.VMEM(state_shape, jnp.float32),
            pltpu.VMEM((rows,) + PLANE, jnp.float32),
            dma((3,)),
        ],
        "interior",
        flops=24 * work,
    )(*fields, *sources)
    has_prior = (slab > 0).astype(jnp.float32).reshape(1)
    forward_out, adjoint_out, blocks = kernel_call(
        borders,
        (
            shaped(*forward_fields.shape),
            shaped(*adjoint_fields.shape),
            shaped(freqs, slabs, rows, reach),
        ),
        [ANY] * 3 + source_specs + [SMEM] + [VMEM] * 5,
        (ANY, ANY, VMEM),
        [
            pltpu.VMEM(state_shape, jnp.float32),
            pltpu.VMEM((rows,) + PLANE, jnp.float32),
            pltpu.VMEM((2, 8) + PLANE, jnp.float32),
            pltpu.VMEM((rows, 8, NY), jnp.float32),
            dma((5,)),
        ],
        "borders",
        flops=24 * work,
        input_output_aliases={0: 0, 1: 1},
    )(
        forward_part, adjoint_part, inverse_permittivity, *sources, has_prior, share,
        prior_a, prior_b, next_a, next_b,
    )

    blocks = blocks.reshape(freqs * slabs, rows, reach)
    blocks = lax.all_to_all(blocks, ("freq", "slab"), 0, 0, tiled=True)
    blocks = blocks.reshape(freqs, slabs, rows, reach)
    projected = kernel_call(
        project,
        shaped(tile_rows, width),
        [VMEM] * 4 + [SMEM],
        VMEM,
        [],
        "project",
    )(blocks, density, chosen, weights, radius_map)
    return (forward_out, adjoint_out, projected)


def solution(mesh):
    return jax.shard_map(
        on_device,
        mesh=mesh,
        in_specs=(
            P("slab", None, None),
            P("freq", None, "slab", None, None),
            P("freq", None, "slab", None, None),
            P("freq", None),
            P("freq", None),
            P("freq", None),
            P("freq", None),
            P("freq"),
            P("freq"),
            P("slab", None),
            P("slab", None),
            P("slab", None),
        ),
        out_specs=(
            P("freq", None, "slab", None, None),
            P("freq", None, "slab", None, None),
            P("slab", None),
        ),
        check_vma=False,
    )
```

time: 123 us -> 81.1 us (0.66)
  Pallas kernels: 0 us -> 24.3 us
  other arithmetic: 23.6 us -> 3.62 us
  waiting for transfers between devices: 25.2 us -> 6.46 us
  blocking collectives: 15.3 us -> 0 us
  local copies, waits for them, and re-layouts: 24.1 us -> 16.8 us
  starting transfers between devices: 31.5 us -> 26.9 us
    pallas_call x0 -> x6, Pallas kernels: none -> 24.3 us  [the longest x1 9.11 us: on_device(): kernel_call(interior, (shaped(*forward_fields.shape), shaped(*adjoint_fie...]
    ppermute x6, waiting for transfers between devices: 21.2 us -> 0.02 us  [shifted(): return lax.ppermute(shard, axis, pairs)]
    unnamed x1 -> x0, blocking collectives: 10.1 us -> none
    all_to_all x1, waiting for transfers between devices: 0.41 us -> 6.45 us  [on_device(): blocks = lax.all_to_all(blocks, ('freq', 'slab'), 0, 0, tiled=True)]
    sub x5 -> x0, other arithmetic: 6.01 us -> none  [the longest x3 5.3 us: yee_update(): magn_x - courant * (forward_cell(elec_z, -1) - elec_z - (forward_cell(ele...]
    all_gather x1 -> x0, blocking collectives: 5.18 us -> none  [on_device(): gathered = lax.all_gather(tiles, 'freq', axis=1, tiled=True)]
    add x6 -> x0, other arithmetic: 5.12 us -> none  [the longest x1 2.66 us: yee_update(): elec_z + courant * inverse * (magn_y - prior_rows(magn_y, prior_y) - (mag...]
    slice x25 -> x3, local copies, waits for them, and re-layouts: 7.4 us -> 2.41 us  [the longest x1 1.31 us: on_device(): design_density[-RMAX:]]
  transfers between devices with their start and end apart: 9 -> 7, of which waited for: 7 -> 1; matrix products, arithmetic and copies ran while one was open for 20% -> 15% of each run, Pallas kernels for 0% -> 25%
where the time goes in v1:
time: 81.1 us; the launch traced here: 80.2 us
  starting transfers between devices  26.9 us (33%)
  Pallas kernels  24.3 us (30%)
  local copies, waits for them, and re-layouts  16.8 us (21%)
  waiting for transfers between devices  6.46 us (8%)
  other arithmetic  3.62 us (4%)
  between operations  2.13 us (3%)
    ppermute x6, starting transfers between devices, shifted(): return lax.ppermute(shard, axis, pairs)  19.4 us
    pallas_call x1, Pallas kernels, on_device(): kernel_call(interior, (shaped(*forward_fields.shape), shaped(*adjoint_fie...  9.11 us
    pallas_call x1, Pallas kernels, on_device(): kernel_call(borders, (shaped(*forward_fields.shape), shaped(*adjoint_fiel...  8.32 us
    unnamed x25, local copies, waits for them, and re-layouts  8.08 us
    all_to_all x1, starting transfers between devices, on_device(): blocks = lax.all_to_all(blocks, ('freq', 'slab'), 0, 0, tiled=True)  7.52 us
    all_to_all x1, waiting for transfers between devices, on_device(): blocks = lax.all_to_all(blocks, ('freq', 'slab'), 0, 0, tiled=True)  6.45 us
    pallas_call x1, Pallas kernels, on_device(): kernel_call(later_planes, (shaped(8, *PLANE), shaped(8, *PLANE)), [ANY] *...  2.96 us
    convert_element_type x2, local copies, waits for them, and re-layouts, on_device(): jnp.repeat(design_mask, width // design_mask.shape[1], axis=1)  2.66 us
  transfers between devices with their start and end apart: 7, of which 1 were waited for; matrix products, arithmetic and copies ran while one was open for 15% of the time, Pallas kernels for 25%

profile of v1, /device:TPU:0, one launch (start us, length us, event | category | flops | bytes accessed | tf_op | source)
XLA Modules:
  0.0 80.2 jit_solution(5811156017585899481)
XLA Ops:
  3.4 1.7 %copy-done = f32[1,6,8,24,512]{4,3,2,1,0:T(8,128)S(1)} copy-done((f32[1,6,8,24,512]{4,3,2,1,0:T(8,128)S(1)}, f32[1,6,8,24,512]{4,3,2,1,0:T(8,128)}, u32[]{:S(2)}) %copy-start) | copy-done | bytes 2359320
  5.1 1.7 %copy-done.2 = f32[1,6,8,24,512]{4,3,2,1,0:T(8,128)S(1)} copy-done((f32[1,6,8,24,512]{4,3,2,1,0:T(8,128)S(1)}, f32[1,6,8,24,512]{4,3,2,1,0:T(8,128)}, u32[]{:S(2)}) %copy-start.2) | copy-done | bytes 2359320
  6.7 1.0 %copy-done.4 = f32[8,24,512]{2,1,0:T(8,128)S(1)} copy-done((f32[8,24,512]{2,1,0:T(8,128)S(1)}, f32[8,24,512]{2,1,0:T(8,128)}, u32[]{:S(2)}) %copy-start.4) | copy-done | bytes 393240
  7.7 3.0 %later_planes.1 = (f32[8,24,512]{2,1,0:T(8,128)}, f32[8,24,512]{2,1,0:T(8,128)}) custom-call(f32[1,6,8,24,512]{4,3,2,1,0:T(8,128)S(1)} %copy-done, f32[1,6,8,24,512]{4,3,2,1,0:T(8,128)S(1)} %copy-done.2, f32[8,24,512]{2,1,0:T(8,128)S(1)} %copy-done.4, f32[2,3]{1,0:T(2,128)S(1)} %pad_maximum_fusion.3.wave, f32[2,512]{1,0:T(2,128)S(1)} %pad_maximum_fusion.2.profile, ...), custom_call_target="tpu_custom_call" | custom-call | flops 7741440 | bytes 1572864 | tf_op jit(solution)/shard_map/later_planes/pallas_call | solution.py:496
  10.7 4.9 %collective-permute-start.1 = (f32[8,24,512]{2,1,0:T(8,128)}, f32[8,24,512]{2,1,0:T(8,128)S(1)}, u32[]{:S(2)}, u32[]{:S(2)}) collective-permute-start(f32[8,24,512]{2,1,0:T(8,128)} %get-tuple-element.17), channel_id=1, source_target_pairs={{0,1},{1,2},{2,3},{3,4},{4,5},{5,6},{6,7},{8,9},{9,10},{10,11},{11... | collective-permute-start | bytes 1179656 | tf_op jit(solution)/shard_map/ppermute | solution.py:455
  15.6 1.6 %collective-permute-start.3 = (f32[8,24,512]{2,1,0:T(8,128)}, f32[8,24,512]{2,1,0:T(8,128)S(1)}, u32[]{:S(2)}, u32[]{:S(2)}) collective-permute-start(f32[8,24,512]{2,1,0:T(8,128)} %get-tuple-element.19), channel_id=1, source_target_pairs={{1,0},{2,1},{3,2},{4,3},{5,4},{6,5},{7,6},{9,8},{10,9},{11,10},{12... | collective-permute-start | bytes 1179656 | tf_op jit(solution)/shard_map/ppermute | solution.py:455
  17.2 1.3 %first_planes.1 = (f32[5,24,512]{2,1,0:T(8,128)}, f32[5,24,512]{2,1,0:T(8,128)}) custom-call(f32[1,6,8,24,512]{4,3,2,1,0:T(8,128)S(1)} %copy-done, f32[1,6,8,24,512]{4,3,2,1,0:T(8,128)S(1)} %copy-done.2, f32[8,24,512]{2,1,0:T(8,128)S(1)} %copy-done.4), custom_call_target="tpu_custom_call" | custom-call | flops 1 | bytes 983040 | tf_op jit(solution)/shard_map/first_planes/pallas_call | solution.py:486
  18.5 5.2 %collective-permute-start = (f32[5,24,512]{2,1,0:T(8,128)}, f32[5,24,512]{2,1,0:T(8,128)}, u32[]{:S(2)}, u32[]{:S(2)}) collective-permute-start(f32[5,24,512]{2,1,0:T(8,128)} %get-tuple-element.16), channel_id=1, source_target_pairs={{0,1},{1,2},{2,3},{3,4},{4,5},{5,6},{6,7},{8,9},{9,10},{10,11},{11... | collective-permute-start | bytes 737288 | tf_op jit(solution)/shard_map/ppermute | solution.py:455
  23.7 1.3 %collective-permute-start.2 = (f32[5,24,512]{2,1,0:T(8,128)}, f32[5,24,512]{2,1,0:T(8,128)}, u32[]{:S(2)}, u32[]{:S(2)}) collective-permute-start(f32[5,24,512]{2,1,0:T(8,128)} %get-tuple-element.18), channel_id=1, source_target_pairs={{1,0},{2,1},{3,2},{4,3},{5,4},{6,5},{7,6},{9,8},{10,9},{11,10},{12... | collective-permute-start | bytes 737288 | tf_op jit(solution)/shard_map/ppermute | solution.py:455
  25.0 1.3 %fusion.1 = (f32[4,64]{1,0:T(4,128)}, f32[4,64]{1,0:T(4,128)}) fusion(f32[64,64]{1,0:T(8,128)} %param.23), kind=kLoop, calls=%fused_computation.12 | loop fusion | bytes 4096 | tf_op jit(solution)/shard_map/slice | solution.py:514
  27.0 1.3 %convert_element_type.34 = f32[1,64]{1,0:T(1,128)} reshape(f32[8,8]{1,0:T(8,128)} %broadcast_in_dim.28) | data formatting | bytes 512 | tf_op jit(solution)/shard_map/convert_element_type | solution.py:513
  28.3 1.3 %pad_maximum_fusion.1 = (f32[5,64]{1,0:T(8,128)}, f32[5,64]{1,0:T(8,128)}) fusion(f32[1,64]{1,0:T(1,128)} %convert_element_type.34, f32[4,64]{1,0:T(4,128)} %get-tuple-element.23, f32[4,64]{1,0:T(4,128)} %get-tuple-element.24), kind=kLoop, calls=%fused_computation.6 | loop fusion | flops 640 | bytes 4864 | tf_op jit(solution)/shard_map/concatenate | solution.py:514
  29.6 1.4 %copy.27 = f32[5,64]{0,1:T(8,128)} copy(f32[5,64]{1,0:T(8,128)} %get-tuple-element.25) | data formatting | bytes 2560 | tf_op jit(solution)/shard_map/concatenate | solution.py:514
  31.0 5.1 %collective-permute-start.4 = (f32[5,64]{0,1:T(8,128)}, f32[5,64]{0,1:T(8,128)}, u32[]{:S(2)}, u32[]{:S(2)}) collective-permute-start(f32[5,64]{0,1:T(8,128)} %copy.27), channel_id=1, source_target_pairs={{0,1},{1,2},{2,3},{3,4},{4,5},{5,6},{6,7},{8,9},{9,10},{10,11},{11... | collective-permute-start | bytes 3848 | tf_op jit(solution)/shard_map/ppermute | solution.py:455
  37.7 1.3 %convert_element_type.35 = f32[64]{0:T(128)} reshape(f32[8,8]{1,0:T(8,128)} %broadcast_in_dim.28) | data formatting | bytes 512 | tf_op jit(solution)/shard_map/convert_element_type | solution.py:513
  39.0 1.4 %copy.29 = f32[64,64]{0,1:T(8,128)} copy(f32[64,64]{1,0:T(8,128)} %param.23) | data formatting | bytes 32768 | tf_op args[11]
  40.5 1.4 %copy.28 = f32[5,64]{0,1:T(8,128)} copy(f32[5,64]{1,0:T(8,128)} %get-tuple-element.26) | data formatting | bytes 2560 | tf_op jit(solution)/shard_map/concatenate | solution.py:515
  41.9 1.7 %copy-done.3 = f32[1,6,8,24,512]{4,3,2,1,0:T(8,128)S(1)} copy-done((f32[1,6,8,24,512]{4,3,2,1,0:T(8,128)S(1)}, f32[1,6,8,24,512]{4,3,2,1,0:T(8,128)}, u32[]{:S(2)}) %copy-start.3) | copy-done | bytes 2359320
  43.5 9.1 %interior.1 = (f32[1,6,8,24,512]{4,3,2,1,0:T(8,128)}, f32[1,6,8,24,512]{4,3,2,1,0:T(8,128)}, f32[8,8,512]{2,1,0:T(8,128)S(1)}) custom-call(f32[1,6,8,24,512]{4,3,2,1,0:T(8,128)S(1)} %copy-done.1, f32[1,6,8,24,512]{4,3,2,1,0:T(8,128)S(1)} %copy-done.3, f32[8,24,512]{2,1,0:T(8,128)S(1)} %copy-done.5, f32[2,3]{1,0:T(2,128)S(1)} %pad_maximum_fusion.3.wave, ...), custom_call_target="tpu_custom_call" | custom-call | flops 13271040 | bytes 9699328 | tf_op jit(solution)/shard_map/interior/pallas_call | solution.py:533
  52.6 1.3 %collective-permute-start.5 = (f32[5,64]{0,1:T(8,128)}, f32[5,64]{0,1:T(8,128)S(1)}, u32[]{:S(2)}, u32[]{:S(2)}) collective-permute-start(f32[5,64]{0,1:T(8,128)} %copy.28), channel_id=1, source_target_pairs={{1,0},{2,1},{3,2},{4,3},{5,4},{6,5},{7,6},{9,8},{10,9},{11,10},{12... | collective-permute-start | bytes 3848 | tf_op jit(solution)/shard_map/ppermute | solution.py:455
  55.0 8.3 %borders.1 = (f32[1,6,8,24,512]{4,3,2,1,0:T(8,128)}, f32[1,6,8,24,512]{4,3,2,1,0:T(8,128)}, f32[4,8,8,72]{3,2,1,0:T(8,128)}) custom-call(f32[1,6,8,24,512]{4,3,2,1,0:T(8,128)} %get-tuple-element.13.fwd, f32[1,6,8,24,512]{4,3,2,1,0:T(8,128)} %get-tuple-element.14.adj, f32[8,24,512]{2,1,0:T(8,128)S(1)} %copy-done.5, ...), custom_call_target="tpu_custom_call", output_to_operand_aliasing={{0}: (0, {}), {1}: (1, {})} | custom-call | flops 13271040 | bytes 9584640 | tf_op jit(solution)/shard_map/borders/pallas_call | solution.py:551
  63.3 7.5 %all-to-all-start = ((f32[32,8,72]{2,1,0:T(8,128)}), f32[32,8,72]{2,1,0:T(8,128)S(1)}, u32[]{:S(2)}, u32[]{:S(2)}) async-start(f32[32,8,72]{2,1,0:T(8,128)} %bitcast.1), calls=%async_computation | async-start | bytes 262144 | tf_op jit(solution)/shard_map/all_to_all | solution.py:576
  72.1 6.4 %all-to-all-done = f32[32,8,72]{2,1,0:T(8,128)S(1)} async-done(((f32[32,8,72]{2,1,0:T(8,128)}), f32[32,8,72]{2,1,0:T(8,128)S(1)}, u32[]{:S(2)}, u32[]{:S(2)}) %all-to-all-start) | async-done | bytes 73760 | tf_op jit(solution)/shard_map/all_to_all | solution.py:576
  78.6 1.7 %project.1 = f32[64,64]{1,0:T(8,128)} custom-call(f32[4,8,8,72]{3,2,1,0:T(8,128)S(1)} %bitcast.11, f32[64,72]{1,0:T(8,128)S(1)} %get-tuple-element.27.density, f32[64,72]{1,0:T(8,128)S(1)} %get-tuple-element.28.chosen, f32[64,64]{1,0:T(8,128)S(1)} %copy-done.7, s32[1,8]{1,0:T(1,128)S(1)} %copy-done.8), custom_call_target="tpu_custom_call" | custom-call | flops 1 | bytes 32768 | tf_op jit(solution)/shard_map/project/pallas_call | solution.py:578
  (40 shorter events, 5.9 us)
Async XLA Ops:
  3.4 1.7 %copy-start = (f32[1,6,8,24,512]{4,3,2,1,0:T(8,128)S(1)}, f32[1,6,8,24,512]{4,3,2,1,0:T(8,128)}, u32[]{:S(2)}) copy-start(f32[1,6,8,24,512]{4,3,2,1,0:T(8,128)} %fwd.5) | copy-start | bytes 7077892
  5.1 1.7 %copy-start.2 = (f32[1,6,8,24,512]{4,3,2,1,0:T(8,128)S(1)}, f32[1,6,8,24,512]{4,3,2,1,0:T(8,128)}, u32[]{:S(2)}) copy-start(f32[1,6,8,24,512]{4,3,2,1,0:T(8,128)} %adj.5) | copy-start | bytes 7077892
  6.7 1.0 %copy-start.4 = (f32[8,24,512]{2,1,0:T(8,128)S(1)}, f32[8,24,512]{2,1,0:T(8,128)}, u32[]{:S(2)}) copy-start(f32[8,24,512]{2,1,0:T(8,128)} %inverse.7) | copy-start | bytes 1179652
  10.7 44.2 %collective-permute-start.1 = (f32[8,24,512]{2,1,0:T(8,128)}, f32[8,24,512]{2,1,0:T(8,128)S(1)}, u32[]{:S(2)}, u32[]{:S(2)}) collective-permute-start(f32[8,24,512]{2,1,0:T(8,128)} %get-tuple-element.17), channel_id=1, source_target_pairs={{0,1},{1,2},{2,3},{3,4},{4,5},{5,6},{6,7},{8,9},{9,10},{10,11},{11... | collective-permute-start | bytes 1179656 | tf_op jit(solution)/shard_map/ppermute | solution.py:455
  15.6 10.8 %copy-start.11 = (s32[1,8]{1,0:T(1,128)S(1)}, s32[1,8]{1,0:T(1,128)}, u32[]{:S(2)}) copy-start(s32[1,8]{1,0:T(1,128)} %param.22) | copy-start | bytes 100
  15.6 20.6 %copy-start.8 = (s32[1,8]{1,0:T(1,128)S(1)}, s32[1,8]{1,0:T(1,128)}, u32[]{:S(2)}) copy-start(s32[1,8]{1,0:T(1,128)} %radius_map.3) | copy-start | bytes 100
  15.6 26.3 %copy-start.1 = (f32[1,6,8,24,512]{4,3,2,1,0:T(8,128)S(1)}, f32[1,6,8,24,512]{4,3,2,1,0:T(8,128)}, u32[]{:S(2)}) copy-start(f32[1,6,8,24,512]{4,3,2,1,0:T(8,128)} %fwd.5) | copy-start | bytes 7077892
  15.6 26.3 %copy-start.5 = (f32[8,24,512]{2,1,0:T(8,128)S(1)}, f32[8,24,512]{2,1,0:T(8,128)}, u32[]{:S(2)}) copy-start(f32[8,24,512]{2,1,0:T(8,128)} %inverse.7) | copy-start | bytes 1179652
  15.6 39.3 %collective-permute-start.3 = (f32[8,24,512]{2,1,0:T(8,128)}, f32[8,24,512]{2,1,0:T(8,128)S(1)}, u32[]{:S(2)}, u32[]{:S(2)}) collective-permute-start(f32[8,24,512]{2,1,0:T(8,128)} %get-tuple-element.19), channel_id=1, source_target_pairs={{1,0},{2,1},{3,2},{4,3},{5,4},{6,5},{7,6},{9,8},{10,9},{11,10},{12... | collective-permute-start | bytes 1179656 | tf_op jit(solution)/shard_map/ppermute | solution.py:455
  18.5 36.4 %collective-permute-start = (f32[5,24,512]{2,1,0:T(8,128)}, f32[5,24,512]{2,1,0:T(8,128)}, u32[]{:S(2)}, u32[]{:S(2)}) collective-permute-start(f32[5,24,512]{2,1,0:T(8,128)} %get-tuple-element.16), channel_id=1, source_target_pairs={{0,1},{1,2},{2,3},{3,4},{4,5},{5,6},{6,7},{8,9},{9,10},{10,11},{11... | collective-permute-start | bytes 737288 | tf_op jit(solution)/shard_map/ppermute | solution.py:455
  23.7 31.2 %collective-permute-start.2 = (f32[5,24,512]{2,1,0:T(8,128)}, f32[5,24,512]{2,1,0:T(8,128)}, u32[]{:S(2)}, u32[]{:S(2)}) collective-permute-start(f32[5,24,512]{2,1,0:T(8,128)} %get-tuple-element.18), channel_id=1, source_target_pairs={{1,0},{2,1},{3,2},{4,3},{5,4},{6,5},{7,6},{9,8},{10,9},{11,10},{12... | collective-permute-start | bytes 737288 | tf_op jit(solution)/shard_map/ppermute | solution.py:455
  31.0 21.6 %collective-permute-start.4 = (f32[5,64]{0,1:T(8,128)}, f32[5,64]{0,1:T(8,128)}, u32[]{:S(2)}, u32[]{:S(2)}) collective-permute-start(f32[5,64]{0,1:T(8,128)} %copy.27), channel_id=1, source_target_pairs={{0,1},{1,2},{2,3},{3,4},{4,5},{5,6},{6,7},{8,9},{9,10},{10,11},{11... | collective-permute-start | bytes 3848 | tf_op jit(solution)/shard_map/ppermute | solution.py:455
  37.1 0.6 copy-start.6
  41.9 1.7 %copy-start.3 = (f32[1,6,8,24,512]{4,3,2,1,0:T(8,128)S(1)}, f32[1,6,8,24,512]{4,3,2,1,0:T(8,128)}, u32[]{:S(2)}) copy-start(f32[1,6,8,24,512]{4,3,2,1,0:T(8,128)} %adj.5) | copy-start | bytes 7077892
  52.6 18.2 %collective-permute-start.5 = (f32[5,64]{0,1:T(8,128)}, f32[5,64]{0,1:T(8,128)S(1)}, u32[]{:S(2)}, u32[]{:S(2)}) collective-permute-start(f32[5,64]{0,1:T(8,128)} %copy.28), channel_id=1, source_target_pairs={{1,0},{2,1},{3,2},{4,3},{5,4},{6,5},{7,6},{9,8},{10,9},{11,10},{12... | collective-permute-start | bytes 3848 | tf_op jit(solution)/shard_map/ppermute | solution.py:455
  54.9 16.2 %copy-start.10 = (f32[64]{0:T(128)S(1)}, f32[64]{0:T(128)}, u32[]{:S(2)}) copy-start(f32[64]{0:T(128)} %convert_element_type.35) | copy-start | bytes 772
  54.9 16.3 %copy-start.9 = (f32[64,64]{0,1:T(8,128)S(1)}, f32[64,64]{0,1:T(8,128)}, u32[]{:S(2)}) copy-start(f32[64,64]{0,1:T(8,128)} %copy.29) | copy-start | bytes 49156
  54.9 23.6 %copy-start.7 = (f32[64,64]{1,0:T(8,128)S(1)}, f32[64,64]{1,0:T(8,128)}, u32[]{:S(2)}) copy-start(f32[64,64]{1,0:T(8,128)} %copy-done.6) | copy-start | bytes 49156
  63.3 15.3 %all-to-all-start = ((f32[32,8,72]{2,1,0:T(8,128)}), f32[32,8,72]{2,1,0:T(8,128)S(1)}, u32[]{:S(2)}, u32[]{:S(2)}) async-start(f32[32,8,72]{2,1,0:T(8,128)} %bitcast.1), calls=%async_computation | async-start | bytes 262144 | tf_op jit(solution)/shard_map/all_to_all | solution.py:576

commit v2 on v0

v2 whole, which is shorter than its diff:
```python
import math

import jax
import jax.numpy as jnp
from jax import lax
from jax.experimental import pallas as pl
from jax.experimental.pallas import tpu as pltpu
from jax.sharding import PartitionSpec as P

NY = 512
NZ = 24
FREQS = 4
STEPS = 3
RMAX = 4


courant = 0.5
sharpness = 4.0
midpoint = 0.5
step_size = 0.3

PLANE = (NZ, NY)
VMEM = pl.BlockSpec(memory_space=pltpu.VMEM)
SMEM = pl.BlockSpec(memory_space=pltpu.SMEM)
HBM = pl.BlockSpec(memory_space=pltpu.HBM)
ANY = pl.BlockSpec(memory_space=pl.ANY)
GRANT = 16 * 1024 * 1024
EXTRA = 8
SENT = 5 * NZ + EXTRA


def ahead(plane, axis):
    size = plane.shape[axis]
    at = lax.broadcasted_iota(jnp.int32, plane.shape, axis)
    return jnp.where(at == size - 1, 0.0, pltpu.roll(plane, size - 1, axis))


def behind(plane, axis):
    at = lax.broadcasted_iota(jnp.int32, plane.shape, axis)
    return jnp.where(at == 0, 0.0, pltpu.roll(plane, 1, axis))


def dy_f(plane):
    return ahead(plane, 1) - plane


def dz_f(plane):
    return ahead(plane, 0) - plane


def dy_b(plane):
    return plane - behind(plane, 1)


def dz_b(plane):
    return plane - behind(plane, 0)


def magnetic_x(magn_x, elec):
    return magn_x - courant * (dy_f(elec[2]) - dz_f(elec[1]))


def magnetic_yz(magn, elec, following):
    next_y, next_z = (0.0, 0.0) if following is None else following
    return (
        magn[0] - courant * (dz_f(elec[0]) - (next_z - elec[2])),
        magn[1] - courant * ((next_y - elec[1]) - dy_f(elec[0])),
    )


def magnetic(magn, elec, following):
    return (magnetic_x(magn[0], elec),) + magnetic_yz(magn[1:], elec, following)


def electric_x(elec_x, magn, scaled):
    return elec_x + scaled * (dy_b(magn[2]) - dz_b(magn[1]))


def electric_yz(elec, magn, prior, scaled):
    prior_y, prior_z = (0.0, 0.0) if prior is None else prior
    return (
        elec[0] + scaled * (dz_b(magn[0]) - (magn[2] - prior_z)),
        elec[1] + scaled * ((magn[1] - prior_y) - dy_b(magn[0])),
    )


def electric(elec, magn, prior, scaled, source):
    return (electric_x(elec[0], magn, scaled) + source,) + electric_yz(
        elec[1:], magn, prior, scaled
    )


SOURCE_SCRATCH = [
    pltpu.VMEM((2, 1, STEPS), jnp.float32),
    pltpu.VMEM((2, 1, NY), jnp.float32),
    pltpu.SemaphoreType.DMA((4,)),
]
SOURCE_SPECS = [HBM] * 4 + [SMEM] * 2
SOURCE_VALUES = [VMEM] * 4 + [SMEM] * 2


def source_copies(given, scratch):
    wave, profile, sems = scratch
    return [
        pltpu.make_async_copy(given[2 * k + run], ref.at[run], sems.at[2 * k + run])
        for k, ref in enumerate((wave, profile))
        for run in range(2)
    ]


def source_of(run, turn, given, scratch):
    if scratch:
        wave, profile = scratch[0][run], scratch[1][run]
    else:
        wave, profile = (jnp.where(run == 0, given[k][...], given[k + 1][...]) for k in (0, 2))
    row = wave[:, turn : turn + 1] * profile
    plane = jnp.where(run == 0, given[4][0], given[5][0])
    at = lax.broadcasted_iota(jnp.int32, PLANE, 0)
    return jnp.where(at == plane, row, 0.0)


def kernel_call(body, out_shape, in_specs, out_specs, scratch, name, micros=1, **more):
    sizes = sum(math.prod(s.shape) * 4 for s in jax.tree.leaves(out_shape))
    return pl.pallas_call(
        body,
        out_shape=out_shape,
        in_specs=in_specs,
        out_specs=out_specs,
        scratch_shapes=scratch,
        compiler_params=pltpu.CompilerParams(vmem_limit_bytes=GRANT),
        cost_estimate=pl.CostEstimate(
            flops=micros * 10**9, bytes_accessed=2 * sizes, transcendentals=0
        ),
        name=name,
        **more,
    )


def shaped(*shape):
    return jax.ShapeDtypeStruct(shape, jnp.float32)


def start_all(copies):
    for copy in copies:
        copy.start()


def wait_all(copies):
    for copy in copies:
        copy.wait()


def plane_at(index):
    return pl.ds(pl.multiple_of(index * NZ, 8), NZ)


def first_planes(
    fwd, adj, inverse, density, mask, to_prior, to_next, rows_in, cells, chosen, sems
):
    rows = inverse.shape[0]
    width = density.shape[1]
    copies = [
        pltpu.make_async_copy(fwd.at[0, :, rows - 1], rows_in.at[0], sems.at[0]),
        pltpu.make_async_copy(adj.at[0, :, rows - 1], rows_in.at[1], sems.at[1]),
        pltpu.make_async_copy(density, cells, sems.at[2]),
        pltpu.make_async_copy(mask, chosen, sems.at[3]),
        pltpu.make_async_copy(inverse.at[0], to_prior.at[plane_at(4)], sems.at[4]),
        pltpu.make_async_copy(inverse.at[rows - 1], to_next.at[plane_at(4)], sems.at[5]),
    ]
    for run, fields in enumerate((fwd, adj)):
        for k in range(2):
            at = 2 * run + k
            copies.append(
                pltpu.make_async_copy(
                    fields.at[0, 1 + k, 0], to_prior.at[plane_at(at)], sems.at[6 + at]
                )
            )
    start_all(copies)
    wait_all(copies[2:4])
    at = lax.broadcasted_iota(jnp.int32, (1, width), 1) // (width // mask.shape[1])
    spread = jnp.zeros((1, width), jnp.float32)
    for k in range(mask.shape[1]):
        spread = jnp.where(at == k, chosen[:, k : k + 1].astype(jnp.float32), spread)
    for sent, first in ((to_prior, 0), (to_next, density.shape[0] - RMAX)):
        sent[pl.ds(5 * NZ, EXTRA), :] = jnp.zeros((EXTRA, NY), jnp.float32)
        sent[pl.ds(5 * NZ, RMAX), pl.ds(0, width)] = cells[pl.ds(first, RMAX), :]
        sent[pl.ds(5 * NZ + RMAX, 1), pl.ds(0, width)] = spread
    for run in range(2):
        copies[run].wait()
        planes = [rows_in[run, k] for k in range(6)]
        magn = magnetic_yz(planes[4:], planes[:3], None)
        for k in range(2):
            to_next[plane_at(2 * run + k), :] = magn[k]
    wait_all(copies[4:])


class State:
    def __init__(self, given, home, written):
        self.given, self.home = given, home
        self.written = None if given is None else set(written)

    def load(self, run, first, x, count=3):
        parts = []
        for k in range(first, first + count):
            at_home = self.written is None or (k, x) in self.written
            ref, at = (self.home if at_home else self.given)(k, x)
            parts.append(ref[run, k, at])
        return tuple(parts)

    def store(self, run, first, x, planes):
        for k, value in enumerate(planes):
            ref, at = self.home(first + k, x)
            ref[run, first + k, at] = value
            if self.written is not None:
                self.written.add((first + k, x))

    def magnetic(self, run, x, following):
        magn = magnetic(self.load(run, 3, x), self.load(run, 0, x), following)
        self.store(run, 3, x, magn)
        return magn

    def electric(self, run, x, prior, scaled, source):
        elec = electric(self.load(run, 0, x), self.load(run, 3, x), prior, scaled, source)
        self.store(run, 0, x, elec)

    def electric_yz(self, run, x):
        return self.load(run, 1, x, 2)

    def magnetic_yz(self, run, x):
        return self.load(run, 4, x, 2)


def in_place(ref):
    return State(None, lambda k, x: (ref, x), ())


def products(ref, x):
    total = ref[0, 0, x] * ref[1, 0, x]
    for k in (1, 2):
        total = total + ref[0, k, x] * ref[1, k, x]
    return jnp.sum(total.reshape(NZ // 8, 8, NY), axis=0)


def interior(fwd, adj, inverse, *rest):
    given, (to_prior, to_next, own, fwd_out, adj_out, state, share), (inv, sems, *scratch) = (
        rest[:6], rest[6:13], rest[13:]
    )
    rows = inverse.shape[0]
    last = rows - 1
    into = source_copies(given, scratch) + [pltpu.make_async_copy(inverse, inv, sems.at[4])]

    def load(fields, run):
        return pltpu.make_async_copy(fields.at[0], state.at[run], sems.at[run])

    start_all([load(fwd, 0)] + into + [load(adj, 1)])
    wait_all(into)
    rows_of = in_place(state)

    def edges(run, source):
        elec = electric(
            rows_of.load(run, 0, 0), rows_of.load(run, 3, 0), None, courant * inv[0], source
        )
        for k in range(2):
            to_prior[plane_at(2 * run + k), :] = elec[1 + k]
        for k in range(3):
            own[run, k] = elec[k]
        elec, magn = rows_of.load(run, 0, last), rows_of.load(run, 3, last)
        magn = magnetic(magn, elec, None)
        elec = electric(
            elec, magn, rows_of.magnetic_yz(run, last - 1), courant * inv[last], source
        )
        magn = magnetic(magn, elec, None)
        for k in range(2):
            to_next[plane_at(2 * run + k), :] = magn[1 + k]
        for k in range(3):
            own[run, 3 + k] = elec[k]
            own[run, 6 + k] = magn[k]

    for turn in range(STEPS):

        def one_run(run, carry, turn=turn):
            if turn == 0:
                load(fwd, run).wait()
            source = source_of(run, turn, given, scratch)
            for x in range(turn, last - turn):
                rows_of.magnetic(run, x, rows_of.electric_yz(run, x + 1))
                if x > turn:
                    rows_of.electric(
                        run, x, rows_of.magnetic_yz(run, x - 1), courant * inv[x], source
                    )
            if turn == 0:
                edges(run, source)
            return carry

        lax.fori_loop(0, 2, one_run, 0)
        for x in range(turn + 1, last - turn):
            share[x] = products(state, x) + (share[x] if turn > 0 else 0.0)
    for x in (0, last):
        share[x] = jnp.zeros(share.shape[1:], jnp.float32)
    out = []
    for run, fields in enumerate((fwd_out, adj_out)):
        for kind, first in enumerate((STEPS, STEPS - 1)):
            done = (pl.ds(3 * kind, 3), pl.ds(first, rows - STEPS - first))
            out.append(
                pltpu.make_async_copy(
                    state.at[run, *done], fields.at[0, *done], sems.at[2 * run + kind]
                )
            )
    start_all(out)
    wait_all(out)


def flags():
    slab = lax.axis_index("slab")
    has_prior = (slab > 0).astype(jnp.float32)
    has_next = (slab < lax.axis_size("slab") - 1).astype(jnp.float32)
    return has_prior, has_next


def border_rows(run, turn, state, source, inv, resp_in, resp_out, prior_a, next_a, here):
    has_prior, has_next = flags()
    flagged = courant * has_prior
    last = inv.shape[0] - 1
    whole = here is not None
    scaled_prior = flagged * prior_a[plane_at(4), :]
    scaled_next = (courant * has_next) * next_a[plane_at(4), :]

    def received(ref):
        return tuple(ref[plane_at(2 * run + k), :] for k in range(2))

    own_y, own_z = state.electric_yz(run, 0)
    if turn == 0:
        magn_r = (None, flagged * own_z, -flagged * own_y)
    else:
        elec_r = tuple(resp_in[run, k] for k in range(3))
        old = tuple(resp_in[run, k] for k in range(3, 6))
        magn_r = (
            old[0] - courant * (dy_f(elec_r[2]) - dz_f(elec_r[1])),
            old[1] - courant * (dz_f(elec_r[0]) + elec_r[2]) + flagged * own_z,
            old[2] + courant * (elec_r[1] + dy_f(elec_r[0])) - flagged * own_y,
        )
    if turn == 0:
        resp_out[run, 0] = scaled_prior * (dy_b(magn_r[2]) - dz_b(magn_r[1]))
        resp_out[run, 1] = -scaled_prior * magn_r[2]
        resp_out[run, 2] = scaled_prior * magn_r[1]
        resp_out[run, 3] = jnp.zeros(PLANE, jnp.float32)
    elif whole:
        resp_out[run, 0] = elec_r[0] + scaled_prior * (dy_b(magn_r[2]) - dz_b(magn_r[1]))
        resp_out[run, 1] = elec_r[1] + scaled_prior * (
            dz_b(magn_r[0]) - (magn_r[2] + courant * elec_r[1])
        )
        resp_out[run, 2] = elec_r[2] + scaled_prior * (
            (magn_r[1] - courant * elec_r[2]) - dy_b(magn_r[0])
        )
        resp_out[run, 3] = magn_r[0]
    resp_out[run, 4] = magn_r[1]
    resp_out[run, 5] = magn_r[2]
    for x in range(turn):
        state.magnetic(run, x, state.electric_yz(run, x + 1))
    if whole:
        arrived = received(here[0])
        prior = tuple(has_prior * arrived[k] + magn_r[1 + k] for k in range(2))
        state.electric(run, 0, prior, courant * inv[0], source)
    else:
        elec_x = electric_x(state.load(run, 0, 0, 1)[0], state.load(run, 3, 0), courant * inv[0])
        state.store(run, 0, 0, (elec_x + source,))
    for x in range(1, turn + 1):
        state.electric(run, x, state.magnetic_yz(run, x - 1), courant * inv[x], source)
    for x in range(last - turn, last):
        state.magnetic(run, x, state.electric_yz(run, x + 1))
    if whole:
        arrived = received(here[1])
        following = tuple(has_next * plane for plane in arrived)
        if turn > 0:
            following = tuple(following[k] + resp_in[run, 6 + k] for k in range(2))
        magn = state.magnetic(run, last, following)
    else:
        magn_x = magnetic_x(state.load(run, 3, last, 1)[0], state.load(run, 0, last))
        state.store(run, 3, last, (magn_x,))
    for x in range(last - turn, last + (1 if whole else 0)):
        state.electric(run, x, state.magnetic_yz(run, x - 1), courant * inv[x], source)
    if turn == 0:
        resp_out[run, 6] = scaled_next * magn[2]
        resp_out[run, 7] = -scaled_next * magn[1]
    elif whole:
        elec_y, elec_z = resp_in[run, 6], resp_in[run, 7]
        magn_x = -courant * (dy_f(elec_z) - dz_f(elec_y))
        resp_out[run, 6] = elec_y + scaled_next * (dz_b(magn_x) - (courant * elec_y - magn[2]))
        resp_out[run, 7] = elec_z + scaled_next * (
            (-courant * elec_z - magn[1]) - dy_b(magn_x)
        )
    else:
        resp_out[run, 6] = resp_in[run, 6]
        resp_out[run, 7] = resp_in[run, 7]


def step_one(inv, *rest):
    given, (before, own, prior_a, next_a), (to_prior, to_next, early, resp, share) = (
        rest[:6], rest[6:10], rest[10:]
    )
    last = inv.shape[0] - 1

    def one_run(run, carry):
        state = State(lambda k, x: (before, x), lambda k, x: (early, min(x, 1)), ())
        source = source_of(run, 0, given, ())
        scaled = courant * inv[0]
        elec = tuple(own[run, k] for k in range(3))
        magn = magnetic(state.load(run, 3, 0), elec, state.electric_yz(run, 1))
        sent = electric_yz(elec[1:], magn, None, scaled)
        for k in range(2):
            to_prior[plane_at(2 * run + k), :] = sent[k]
        elec = tuple(own[run, 3 + k] for k in range(3))
        magn = tuple(own[run, 6 + k] for k in range(3))
        yz = magnetic_yz(
            state.magnetic_yz(run, last - 1), state.load(run, 0, last - 1), elec[1:]
        )
        elec = electric(elec, magn, yz, courant * inv[last], source_of(run, 1, given, ()))
        sent = magnetic_yz(magn[1:], elec, None)
        for k in range(2):
            to_next[plane_at(2 * run + k), :] = sent[k]
        border_rows(
            run, 0, state, source, inv, None, resp, prior_a, next_a, (prior_a, next_a)
        )
        return carry

    lax.fori_loop(0, 2, one_run, 0)
    for side in range(2):
        share[side] = products(early, side)


def borders(fwd, adj, inv, *rest):
    given, (before, early, resp_in, share, ends, prior_a, next_a, prior_b, next_b) = (
        rest[:6], rest[6:15]
    )
    fwd_out, adj_out, kept, summed, waiting, inner, resp, total, sems = rest[15:]
    rows = inv.shape[0]
    last = rows - 1
    homes = {0: (kept, 0), last - 1: (kept, 1), last: (kept, 2)}
    homes |= {1: (inner, 0), 2: (inner, 1), last - 2: (inner, 2)}

    def handed_in(k, x):
        if x == last or (x == 0 and k < 3):
            return (early, min(x, 1))
        return (before, x)

    written = set()
    for turn in range(1, STEPS):
        whole = turn < STEPS - 1
        seen = []

        def one_run(run, carry, turn=turn, whole=whole, seen=seen):
            state = State(handed_in, lambda k, x: homes[x], written)
            border_rows(
                run, turn, state, source_of(run, turn, given, ()), inv,
                resp_in if turn == 1 else resp, resp if whole else waiting, prior_a, next_a,
                (prior_b, next_b) if whole else None,
            )
            seen[:] = [state.written]
            return carry

        lax.fori_loop(0, 2, one_run, 0)
        written = seen[0]
        if not whole:
            out = []
            for run, fields in enumerate((fwd_out, adj_out)):
                for part, (ref, at, x, count, first, parts) in enumerate(
                    (
                        (inner, 0, 1, 1, 0, 6),
                        (inner, 1, 2, 1, 0, 3),
                        (inner, 2, last - 2, 1, 0, 6),
                        (kept, 1, last - 1, 1, 0, 6),
                        (kept, 0, 0, 1, 0, 1),
                        (kept, 0, 0, 1, 3, 3),
                        (kept, 2, last, 1, 3, 1),
                    )
                ):
                    out.append(
                        pltpu.make_async_copy(
                            ref.at[run, pl.ds(first, parts), pl.ds(at, count)],
                            fields.at[0, pl.ds(first, parts), pl.ds(x, count)],
                            sems.at[7 * run + part],
                        )
                    )
            start_all(out)
        reached = list(range(turn + 1)) + list(range(last - turn, last + 1))
        for x in reached if whole else reached[1:-1]:
            if turn > 1 and min(x, last - x) < turn:
                so_far = total[x]
            else:
                so_far = ends[min(x, 1)] if x in (0, last) else share[x]
            total[x] = so_far + products(*homes[x])
    for x in range(STEPS, rows - STEPS):
        total[x] = share[x]
    summed[...] = jnp.sum(total[...], axis=1)
    wait_all(out)


def last_planes(fwd, adj, inv, *rest):
    given, (kept, summed, waiting, prior_c, next_c) = rest[:6], rest[6:11]
    fwd_out, adj_out, blocks, front, back, back_h, sems = rest[11:]
    last = inv.shape[0] - 1
    has_prior, has_next = flags()

    def one_run(run, carry):
        def row(first, slot, count):
            return tuple(kept[run, first + k, slot] for k in range(count))

        def arrived(ref, flag, first):
            return tuple(
                flag * ref[plane_at(2 * run + k), :] + waiting[run, first + k] for k in range(2)
            )

        elec = electric_yz(
            row(1, 0, 2), row(3, 0, 3), arrived(prior_c, has_prior, 4), courant * inv[0]
        )
        for k in range(2):
            front[run, k] = elec[k]
        elec = row(0, 2, 3)
        yz = magnetic_yz(row(4, 2, 2), elec, arrived(next_c, has_next, 6))
        source = source_of(run, STEPS - 1, given, ())
        elec = electric(elec, row(3, 2, 1) + yz, row(4, 1, 2), courant * inv[last], source)
        for k in range(3):
            back[run, k] = elec[k]
        for k in range(2):
            back_h[run, k] = yz[k]
        return carry

    lax.fori_loop(0, 2, one_run, 0)
    out = []
    for run, fields in enumerate((fwd_out, adj_out)):
        for part, (source, first, count, x) in enumerate(
            ((front, 1, 2, 0), (back, 0, 3, last), (back_h, 4, 2, last))
        ):
            out.append(
                pltpu.make_async_copy(
                    source.at[run],
                    fields.at[0, pl.ds(first, count), x],
                    sems.at[3 * run + part],
                )
            )
    start_all(out)

    def row_sum(pairs):
        total = pairs[0][0] * pairs[0][1]
        for first, second in pairs[1:]:
            total = total + first * second
        return jnp.sum(total, axis=0, keepdims=True)

    head = row_sum([(kept[0, 0, 0], kept[1, 0, 0])] + [(front[0, k], front[1, k]) for k in range(2)])
    tail = row_sum([(back[0, k], back[1, k]) for k in range(3)])
    at = lax.broadcasted_iota(jnp.int32, summed.shape, 0)
    full = summed[...] + jnp.where(at == 0, head, 0.0) + jnp.where(at == last, tail, 0.0)
    slabs, width = blocks.shape[1], blocks.shape[3]
    for k in range(slabs):
        turned = pltpu.roll(full, (RMAX - k * (NY // slabs)) % NY, 1)
        for f in range(blocks.shape[0]):
            blocks[f, k] = turned[:, :width]
    wait_all(out)


def moved(rows, by):
    if by == 0:
        return rows
    count = rows.shape[0]
    at = lax.broadcasted_iota(jnp.int32, rows.shape, 0)
    keep = at < count - by if by > 0 else at >= -by
    return jnp.where(keep, pltpu.roll(rows, (-by) % count, 0), 0.0)


def weighted(cells, radius):
    tile = cells.shape[1] - 2 * RMAX
    columns = [cells[:, RMAX : RMAX + tile]]
    for a in range(1, RMAX + 1):
        columns.append(
            cells[:, RMAX - a : RMAX - a + tile] + cells[:, RMAX + a : RMAX + a + tile]
        )
    rings = {}
    for a in range(RMAX + 1):
        for b in range(RMAX + 1):
            part = columns[a]
            if b > 0:
                part = moved(part, b) + moved(part, -b)
            square = a * a + b * b
            rings[square] = rings[square] + part if square in rings else part
    total = None
    for square, part in rings.items():
        term = jnp.maximum(radius - math.sqrt(square), 0.0) * part
        total = term if total is None else total + term
    return total


def by_tile(values, count):
    columns = count // values.shape[1]
    at = lax.broadcasted_iota(jnp.int32, (count, 1), 0) // columns
    spread = jnp.zeros((count, 1), jnp.float32)
    for k in range(values.shape[1]):
        spread = jnp.where(at == k, values[:, k : k + 1].astype(jnp.float32), spread)
    return spread


def filter_operands(
    prior_a, next_a, density, mask, radius_map, padded, chosen, weights, rows_of, marks_of
):
    tile_rows, width = density.shape
    reach = padded.shape[1]
    above, below = (ref[pl.ds(5 * NZ, EXTRA), :] for ref in (prior_a, next_a))
    rows_of[pl.ds(0, RMAX), :] = above[:RMAX, :width]
    rows_of[pl.ds(RMAX, tile_rows), :] = density[...]
    rows_of[pl.ds(RMAX + tile_rows, RMAX), :] = below[:RMAX, :width]
    marks_of[...] = jnp.zeros_like(marks_of)
    marks_of[pl.ds(0, 1), :] = above[RMAX : RMAX + 1, :width]
    marks_of[pl.ds(1, 1), :] = below[RMAX : RMAX + 1, :width]
    sides = marks_of[...].T
    first = lax.axis_index("slab") * tile_rows - RMAX
    at = lax.broadcasted_iota(jnp.int32, (width, reach), 1)
    inside = (at + first >= 0) & (at + first < NY)
    padded[...] = jnp.where(inside, rows_of[...].T, 0.0)
    mark = jnp.where(
        at < RMAX,
        sides[:, 0:1],
        jnp.where(at < RMAX + tile_rows, by_tile(mask, width), sides[:, 1:2]),
    )
    scale = step_size / math.sqrt(3 * STEPS * NZ * FREQS)
    chosen[...] = jnp.where(inside, scale * mark, 0.0)
    weights[...] = weighted(inside.astype(jnp.float32), by_tile(radius_map, width))


def project(blocks, padded, chosen, weights, radius_map, projected):
    freqs, slabs, rows, width = blocks.shape
    gradient = jnp.sum(blocks[...], axis=0).reshape(slabs * rows, width)
    updated = padded[...] + chosen[...] * gradient
    numerator = weighted(updated, by_tile(radius_map, slabs * rows))
    filtered = numerator / weights[...]
    base = math.tanh(sharpness * midpoint)
    value = (base + jnp.tanh(sharpness * (filtered - midpoint))) / (
        base + math.tanh(sharpness * (1.0 - midpoint))
    )
    projected[...] = value.T


def around(shard, axis, by):
    count = lax.axis_size(axis)
    return lax.ppermute(shard, axis, [(i, (i + by) % count) for i in range(count)])


def on_device(
    inverse_permittivity,
    forward_fields,
    adjoint_fields,
    source_wave,
    source_profile,
    adjoint_wave,
    adjoint_profile,
    source_plane,
    monitor_plane,
    radius_map,
    design_mask,
    design_density,
):
    rows = forward_fields.shape[2]
    freqs, slabs = lax.axis_size("freq"), lax.axis_size("slab")
    tile_rows, width = design_density.shape
    reach = tile_rows + 2 * RMAX
    waves = (source_wave, adjoint_wave, source_profile, adjoint_profile)
    planes = (source_plane, monitor_plane)

    def pinned(arrays):
        return tuple(pltpu.with_memory_space_constraint(array, pltpu.HBM) for array in arrays)

    fields = pinned((forward_fields, adjoint_fields, inverse_permittivity))
    sources = pinned(waves) + planes
    dma = pltpu.SemaphoreType.DMA
    field_shape = shaped(*forward_fields.shape)
    state_shape = shaped(2, 6, rows, *PLANE)
    four = shaped(4 * NZ, NY)

    def vmem(*shape, kind=jnp.float32):
        return pltpu.VMEM(shape, kind)

    to_prior, to_next = kernel_call(
        first_planes,
        (shaped(SENT, NY), shaped(SENT, NY)),
        [HBM] * 5,
        (VMEM, VMEM),
        [
            vmem(2, 6, *PLANE),
            vmem(tile_rows, width),
            vmem(*design_mask.shape, kind=jnp.int32),
            dma((10,)),
        ],
        "first_planes",
    )(*fields, *pinned((design_density, design_mask)))
    prior_a = around(to_next, "slab", 1)
    next_a = around(to_prior, "slab", -1)
    to_prior, to_next, own, forward_part, adjoint_part, state, share = kernel_call(
        interior,
        (
            four,
            four,
            shaped(2, 9, *PLANE),
            field_shape,
            field_shape,
            state_shape,
            shaped(rows, 8, NY),
        ),
        [HBM] * 3 + SOURCE_SPECS,
        (VMEM, VMEM, VMEM, HBM, HBM, VMEM, VMEM),
        [vmem(rows, *PLANE), dma((5,)), *SOURCE_SCRATCH],
        "interior",
        micros=8,
    )(*fields, *sources)
    prior_b = around(to_next, "slab", 1)
    next_b = around(to_prior, "slab", -1)
    to_prior, to_next, early, resp, ends = kernel_call(
        step_one,
        (four, four, shaped(2, 6, 2, *PLANE), shaped(2, 8, *PLANE), shaped(2, 8, NY)),
        [VMEM] + SOURCE_VALUES + [VMEM] * 4,
        (VMEM,) * 5,
        [],
        "step_one",
        micros=3,
    )(inverse_permittivity, *waves, *planes, state, own, prior_a, next_a)
    prior_c = around(to_next, "slab", 1)
    next_c = around(to_prior, "slab", -1)
    padded, chosen, weights = kernel_call(
        filter_operands,
        (shaped(width, reach), shaped(width, reach), shaped(width, tile_rows)),
        [VMEM] * 5,
        (VMEM,) * 3,
        [vmem(reach, width), vmem(8, width)],
        "filter_operands",
    )(prior_a, next_a, design_density, design_mask, radius_map)
    forward_part, adjoint_part, kept, summed, waiting = kernel_call(
        borders,
        (
            field_shape,
            field_shape,
            shaped(2, 6, 3, *PLANE),
            shaped(rows, NY),
            shaped(2, 8, *PLANE),
        ),
        [HBM] * 2 + [VMEM] + SOURCE_VALUES + [VMEM] * 9,
        (HBM, HBM, VMEM, VMEM, VMEM),
        [
            vmem(2, 6, 3, *PLANE),
            vmem(2, 8, *PLANE),
            vmem(rows, 8, NY),
            dma((14,)),
        ],
        "borders",
        micros=3,
        input_output_aliases={0: 0, 1: 1},
    )(
        forward_part, adjoint_part, inverse_permittivity, *waves, *planes, state, early, resp,
        share, ends, prior_a, next_a, prior_b, next_b,
    )
    forward_out, adjoint_out, blocks = kernel_call(
        last_planes,
        (field_shape, field_shape, shaped(freqs, slabs, rows, reach)),
        [HBM] * 2 + [VMEM] + SOURCE_VALUES + [VMEM] * 5,
        (HBM, HBM, VMEM),
        [
            vmem(2, 2, *PLANE),
            vmem(2, 3, *PLANE),
            vmem(2, 2, *PLANE),
            dma((6,)),
        ],
        "last_planes",
        micros=2,
        input_output_aliases={0: 0, 1: 1},
    )(
        forward_part, adjoint_part, inverse_permittivity, *waves, *planes,
        kept, summed, waiting, prior_c, next_c,
    )

    blocks = blocks.reshape(freqs * slabs, rows, reach)
    blocks = lax.all_to_all(blocks, ("freq", "slab"), 0, 0, tiled=True)
    blocks = blocks.reshape(freqs, slabs, rows, reach)
    projected = kernel_call(
        project,
        shaped(tile_rows, width),
        [VMEM] * 5,
        VMEM,
        [],
        "project",
    )(blocks, padded, chosen, weights, radius_map)
    return (forward_out, adjoint_out, projected)


def solution(mesh):
    return jax.shard_map(
        on_device,
        mesh=mesh,
        in_specs=(
            P("slab", None, None),
            P("freq", None, "slab", None, None),
            P("freq", None, "slab", None, None),
            P("freq", None),
            P("freq", None),
            P("freq", None),
            P("freq", None),
            P("freq"),
            P("freq"),
            P("slab", None),
            P("slab", None),
            P("slab", None),
        ),
        out_specs=(
            P("freq", None, "slab", None, None),
            P("freq", None, "slab", None, None),
            P("slab", None),
        ),
        check_vma=False,
    )
```

time: 123 us -> 51.2 us (0.42)
  local copies, waits for them, and re-layouts: 24.1 us -> 0.05 us
  other arithmetic: 23.6 us -> 0 us
  Pallas kernels: 0 us -> 17.4 us
  blocking collectives: 15.3 us -> 0 us
  starting transfers between devices: 31.5 us -> 18.7 us
  waiting for transfers between devices: 25.2 us -> 12.7 us
    ppermute x8 -> x6, waiting for transfers between devices: 24.8 us -> 5.95 us  [around(): lax.ppermute(shard, axis, [(i, (i + by) % count) for i in range(count)])]
    pallas_call x0 -> x7, Pallas kernels: none -> 17.4 us  [the longest x1 7.33 us: on_device(): kernel_call(interior, (four, four, shaped(2, 9, *PLANE), field_shape, fie...]
    unnamed x1 -> x0, blocking collectives: 10.1 us -> none
    unnamed x27 -> x16, local copies, waits for them, and re-layouts: 8.77 us -> 0.05 us
    ppermute x8 -> x6, starting transfers between devices: 24.3 us -> 15.6 us  [around(): lax.ppermute(shard, axis, [(i, (i + by) % count) for i in range(count)])]
    slice x25 -> x0, local copies, waits for them, and re-layouts: 7.4 us -> none  [the longest x12 5.89 us: forward_cell(): inner = lax.slice_in_dim(field, 1, size, axis=axis)]
    all_to_all x1, waiting for transfers between devices: 0.41 us -> 6.8 us  [on_device(): blocks = lax.all_to_all(blocks, ('freq', 'slab'), 0, 0, tiled=True)]
    sub x5 -> x0, other arithmetic: 6.01 us -> none  [the longest x3 5.3 us: yee_update(): magn_x - courant * (forward_cell(elec_z, -1) - elec_z - (forward_cell(ele...]
  transfers between devices with their start and end apart: 9 -> 7, of which waited for: 7 -> 3; matrix products, arithmetic and copies ran while one was open for 20% -> 0% of each run, Pallas kernels for 0% -> 25%
where the time goes in v2:
time: 51.2 us; the launch traced here: 51 us
  starting transfers between devices  18.7 us (37%)
  Pallas kernels  17.4 us (34%)
  waiting for transfers between devices  12.7 us (25%)
  between operations  2.13 us (4%)
    ppermute x6, starting transfers between devices, around(): lax.ppermute(shard, axis, [(i, (i + by) % count) for i in range(count)])  15.6 us
    pallas_call x1, Pallas kernels, on_device(): kernel_call(interior, (four, four, shaped(2, 9, *PLANE), field_shape, fie...  7.33 us
    all_to_all x1, waiting for transfers between devices, on_device(): blocks = lax.all_to_all(blocks, ('freq', 'slab'), 0, 0, tiled=True)  6.8 us
    ppermute x6, waiting for transfers between devices, around(): lax.ppermute(shard, axis, [(i, (i + by) % count) for i in range(count)])  5.95 us
    pallas_call x1, Pallas kernels, on_device(): kernel_call(borders, (field_shape, field_shape, shaped(2, 6, 3, *PLANE),...  3.56 us
    all_to_all x1, starting transfers between devices, on_device(): blocks = lax.all_to_all(blocks, ('freq', 'slab'), 0, 0, tiled=True)  3.1 us
    pallas_call x1, Pallas kernels, on_device(): kernel_call(last_planes, (field_shape, field_shape, shaped(freqs, slabs,...  1.87 us
    pallas_call x1, Pallas kernels, on_device(): kernel_call(project, shaped(tile_rows, width), [VMEM] * 5, VMEM, [], 'pro...  1.59 us
  transfers between devices with their start and end apart: 7, of which 3 were waited for; matrix products, arithmetic and copies ran while one was open for 0% of the time, Pallas kernels for 25%

profile of v2, /device:TPU:0, one launch (start us, length us, event | category | flops | bytes accessed | tf_op | source)
XLA Modules:
  0.0 51.0 jit_solution(7179569557690402853)
XLA Ops:
  0.6 1.3 %first_planes.1 = (f32[128,512]{1,0:T(8,128)S(1)}, f32[128,512]{1,0:T(8,128)S(1)}) custom-call(f32[1,6,8,24,512]{4,3,2,1,0:T(8,128)} %fwd.3, f32[1,6,8,24,512]{4,3,2,1,0:T(8,128)} %adj.3, f32[8,24,512]{2,1,0:T(8,128)} %inv.5, f32[64,64]{1,0:T(8,128)} %density.3, s32[1,8]{1,0:T(1,128)} %mask.3), custom_call_target="tpu_custom_call" | custom-call | flops 1000000000 | bytes 1048576 | tf_op jit(solution)/shard_map/first_planes/pallas_call | solution.py:680
  1.9 3.0 %collective-permute-start = (f32[128,512]{1,0:T(8,128)S(1)}, f32[128,512]{1,0:T(8,128)S(1)}, u32[]{:S(2)}, u32[]{:S(2)}) collective-permute-start(f32[128,512]{1,0:T(8,128)S(1)} %get-tuple-element.32), channel_id=1, source_target_pairs={{0,1},{1,2},{2,3},{3,4},{4,5},{5,6},{6,7},{7,0},{8,9},{9,10},{10,1... | collective-permute-start | bytes 786440 | tf_op jit(solution)/shard_map/ppermute | solution.py:643
  4.9 3.1 %collective-permute-start.1 = (f32[128,512]{1,0:T(8,128)S(1)}, f32[128,512]{1,0:T(8,128)S(1)}, u32[]{:S(2)}, u32[]{:S(2)}) collective-permute-start(f32[128,512]{1,0:T(8,128)S(1)} %get-tuple-element.33), channel_id=1, source_target_pairs={{0,7},{1,0},{2,1},{3,2},{4,3},{5,4},{6,5},{7,6},{8,15},{9,8},{10,9... | collective-permute-start | bytes 786440 | tf_op jit(solution)/shard_map/ppermute | solution.py:643
  9.3 0.0 copy-start
  9.3 0.0 copy-start.2
  9.3 0.0 copy-start.3
  9.4 0.0 copy-start.4
  9.4 0.0 copy-start.5
  9.4 7.3 %interior.1 = (f32[96,512]{1,0:T(8,128)S(1)}, f32[96,512]{1,0:T(8,128)S(1)}, f32[2,9,24,512]{3,2,1,0:T(8,128)S(1)}, f32[1,6,8,24,512]{4,3,2,1,0:T(8,128)}, f32[1...) custom-call(f32[1,6,8,24,512]{4,3,2,1,0:T(8,128)} %fwd.3, ...), custom_call_target="tpu_custom_call" | custom-call | flops 8000000000 | bytes 21692416 | tf_op jit(solution)/shard_map/interior/pallas_call | solution.py:695
  16.7 0.1 collective-permute-start.2
  16.8 4.7 %collective-permute-start.3 = (f32[96,512]{1,0:T(8,128)S(1)}, f32[96,512]{1,0:T(8,128)S(1)}, u32[]{:S(2)}, u32[]{:S(2)}) collective-permute-start(f32[96,512]{1,0:T(8,128)S(1)} %get-tuple-element.39), channel_id=1, source_target_pairs={{0,7},{1,0},{2,1},{3,2},{4,3},{5,4},{6,5},{7,6},{8,15},{9,8},{10,9... | collective-permute-start | bytes 589832 | tf_op jit(solution)/shard_map/ppermute | solution.py:643
  21.6 0.8 %step_one.1 = (f32[96,512]{1,0:T(8,128)S(1)}, f32[96,512]{1,0:T(8,128)S(1)}, f32[2,6,2,24,512]{4,3,2,1,0:T(8,128)S(1)}, f32[2,8,24,512]{3,2,1,0:T(8,128)S(1)}, f32[2,8,512]{2,1,0:T(8,128)S(1)}) custom-call(f32[8,24,512]{2,1,0:T(8,128)S(1)} %copy-done, f32[1,3]{1,0:T(1,128)S(1)} %copy-done.4, f32[1,3]{1,0:T(1,128)S(1)} %copy-done.5, f32[1,512]{1,0:T(1,128)S(1)} %copy-done.2, ...), custom_call_target="tpu_custom_call" | custom-call | flops 3000000000 | bytes 4784128 | tf_op jit(solution)/shard_map/step_one/pallas_call | solution.py:714
  22.4 0.1 collective-permute-start.4
  22.4 4.7 %collective-permute-start.5 = (f32[96,512]{1,0:T(8,128)S(1)}, f32[96,512]{1,0:T(8,128)S(1)}, u32[]{:S(2)}, u32[]{:S(2)}) collective-permute-start(f32[96,512]{1,0:T(8,128)S(1)} %get-tuple-element.46), channel_id=1, source_target_pairs={{0,7},{1,0},{2,1},{3,2},{4,3},{5,4},{6,5},{7,6},{8,15},{9,8},{10,9... | collective-permute-start | bytes 589832 | tf_op jit(solution)/shard_map/ppermute | solution.py:643
  27.2 1.2 %collective-permute-done.2.rest_13_ = f32[96,512]{1,0:T(8,128)S(1)} collective-permute-done((f32[96,512]{1,0:T(8,128)S(1)}, f32[96,512]{1,0:T(8,128)S(1)}, u32[]{:S(2)}, u32[]{:S(2)}) %collective-permute-start.2) | collective-permute-done | bytes 196640 | tf_op jit(solution)/shard_map/ppermute | solution.py:643
  28.4 4.7 %collective-permute-done.3.rest_14_ = f32[96,512]{1,0:T(8,128)S(1)} collective-permute-done((f32[96,512]{1,0:T(8,128)S(1)}, f32[96,512]{1,0:T(8,128)S(1)}, u32[]{:S(2)}, u32[]{:S(2)}) %collective-permute-start.3) | collective-permute-done | bytes 196640 | tf_op jit(solution)/shard_map/ppermute | solution.py:643
  33.1 3.6 %borders.1 = (f32[1,6,8,24,512]{4,3,2,1,0:T(8,128)}, f32[1,6,8,24,512]{4,3,2,1,0:T(8,128)}, f32[2,6,3,24,512]{4,3,2,1,0:T(8,128)S(1)}, f32[8,512]{1,0:T(8,128)S(1)}, f32[2,8,24,512]{3,2,1,0:T(8,128)S(1)}) custom-call(f32[1,6,8,24,512]{4,3,2,1,0:T(8,128)} %get-tuple-element.28.fwd, ...), custom_call_target="tpu_custom_call", output_to_operand_aliasing={{0}: (0, {}), {1}: (1, {})} | custom-call | flops 3000000000 | bytes 14581760 | tf_op jit(solution)/shard_map/borders/pallas_call | solution.py:733
  36.7 0.0 copy-start.1
  36.7 0.0 copy-start.6
  36.7 1.9 %last_planes.1 = (f32[1,6,8,24,512]{4,3,2,1,0:T(8,128)}, f32[1,6,8,24,512]{4,3,2,1,0:T(8,128)}, f32[4,8,8,72]{3,2,1,0:T(8,128)}) custom-call(f32[1,6,8,24,512]{4,3,2,1,0:T(8,128)} %get-tuple-element.40.fwd, f32[1,6,8,24,512]{4,3,2,1,0:T(8,128)} %get-tuple-element.41.adj, f32[8,24,512]{2,1,0:T(8,128)S(1)} %copy-done, ...), custom_call_target="tpu_custom_call", output_to_operand_aliasing={{0}: (0, {}), {1}: (1, {})} | custom-call | flops 2000000000 | bytes 9584640 | tf_op jit(solution)/shard_map/last_planes/pallas_call | solution.py:757
  38.6 3.1 %all-to-all-start = ((f32[32,8,72]{2,1,0:T(8,128)}), f32[32,8,72]{2,1,0:T(8,128)S(1)}, u32[]{:S(2)}, u32[]{:S(2)}) async-start(f32[32,8,72]{2,1,0:T(8,128)} %bitcast), calls=%async_computation | async-start | bytes 262144 | tf_op jit(solution)/shard_map/all_to_all | solution.py:777
  41.7 0.9 %filter_operands.1 = (f32[64,72]{1,0:T(8,128)S(1)}, f32[64,72]{1,0:T(8,128)S(1)}, f32[64,64]{1,0:T(8,128)S(1)}) custom-call(f32[128,512]{1,0:T(8,128)S(1)} %collective-permute-done.rest_8_.rest_11_.prior_a, f32[128,512]{1,0:T(8,128)S(1)} %collective-permute-done.1.rest_9_.rest_12_.next_a, f32[64,64]{1,0:T(8,128)S(1)} %copy-done.1, s32[1,8]{1,0:T(1,128)S(1)} %copy-done.6, ...), custom_call_target="tpu_custom_call" | custom-call | flops 1000000000 | bytes 106496 | tf_op jit(solution)/shard_map/filter_operands/pallas_call | solution.py:725
  42.6 6.8 %all-to-all-done = f32[32,8,72]{2,1,0:T(8,128)S(1)} async-done(((f32[32,8,72]{2,1,0:T(8,128)}), f32[32,8,72]{2,1,0:T(8,128)S(1)}, u32[]{:S(2)}, u32[]{:S(2)}) %all-to-all-start) | async-done | bytes 73760 | tf_op jit(solution)/shard_map/all_to_all | solution.py:777
  49.4 1.6 %project.1 = f32[64,64]{1,0:T(8,128)} custom-call(f32[4,8,8,72]{3,2,1,0:T(8,128)S(1)} %bitcast.2, f32[64,72]{1,0:T(8,128)S(1)} %get-tuple-element.50.padded, f32[64,72]{1,0:T(8,128)S(1)} %get-tuple-element.51.chosen, f32[64,64]{1,0:T(8,128)S(1)} %get-tuple-element.52.weights, s32[1,8]{1,0:T(1,128)S(1)} %copy-done.7), custom_call_target="tpu_custom_call" | custom-call | flops 1000000000 | bytes 32768 | tf_op jit(solution)/shard_map/project/pallas_call | solution.py:779
  (13 shorter events, 0.0 us)
Async XLA Ops:
  1.9 19.6 %collective-permute-start = (f32[128,512]{1,0:T(8,128)S(1)}, f32[128,512]{1,0:T(8,128)S(1)}, u32[]{:S(2)}, u32[]{:S(2)}) collective-permute-start(f32[128,512]{1,0:T(8,128)S(1)} %get-tuple-element.32), channel_id=1, source_target_pairs={{0,1},{1,2},{2,3},{3,4},{4,5},{5,6},{6,7},{7,0},{8,9},{9,10},{10,1... | collective-permute-start | bytes 786440 | tf_op jit(solution)/shard_map/ppermute | solution.py:643
  4.9 16.6 %collective-permute-start.1 = (f32[128,512]{1,0:T(8,128)S(1)}, f32[128,512]{1,0:T(8,128)S(1)}, u32[]{:S(2)}, u32[]{:S(2)}) collective-permute-start(f32[128,512]{1,0:T(8,128)S(1)} %get-tuple-element.33), channel_id=1, source_target_pairs={{0,7},{1,0},{2,1},{3,2},{4,3},{5,4},{6,5},{7,6},{8,15},{9,8},{10,9... | collective-permute-start | bytes 786440 | tf_op jit(solution)/shard_map/ppermute | solution.py:643
  9.3 12.2 %copy-start = (f32[8,24,512]{2,1,0:T(8,128)S(1)}, f32[8,24,512]{2,1,0:T(8,128)}, u32[]{:S(2)}) copy-start(f32[8,24,512]{2,1,0:T(8,128)} %inv.5) | copy-start | bytes 1179652
  9.3 12.2 %copy-start.2 = (f32[1,512]{1,0:T(1,128)S(1)}, f32[1,512]{1,0:T(1,128)}, u32[]{:S(2)}) copy-start(f32[1,512]{1,0:T(1,128)} %rest_2_.7) | copy-start | bytes 6148
  9.3 12.2 %copy-start.3 = (f32[1,512]{1,0:T(1,128)S(1)}, f32[1,512]{1,0:T(1,128)}, u32[]{:S(2)}) copy-start(f32[1,512]{1,0:T(1,128)} %rest_3_.7) | copy-start | bytes 6148
  9.4 12.2 %copy-start.4 = (f32[1,3]{1,0:T(1,128)S(1)}, f32[1,3]{1,0:T(1,128)}, u32[]{:S(2)}) copy-start(f32[1,3]{1,0:T(1,128)} %rest_0_.7) | copy-start | bytes 40
  9.4 12.2 %copy-start.5 = (f32[1,3]{1,0:T(1,128)S(1)}, f32[1,3]{1,0:T(1,128)}, u32[]{:S(2)}) copy-start(f32[1,3]{1,0:T(1,128)} %rest_1_.7) | copy-start | bytes 40
  16.7 11.6 %collective-permute-start.2 = (f32[96,512]{1,0:T(8,128)S(1)}, f32[96,512]{1,0:T(8,128)S(1)}, u32[]{:S(2)}, u32[]{:S(2)}) collective-permute-start(f32[96,512]{1,0:T(8,128)S(1)} %get-tuple-element.38), channel_id=1, source_target_pairs={{0,1},{1,2},{2,3},{3,4},{4,5},{5,6},{6,7},{7,0},{8,9},{9,10},{10,1... | collective-permute-start | bytes 589832 | tf_op jit(solution)/shard_map/ppermute | solution.py:643
  16.8 16.3 %collective-permute-start.3 = (f32[96,512]{1,0:T(8,128)S(1)}, f32[96,512]{1,0:T(8,128)S(1)}, u32[]{:S(2)}, u32[]{:S(2)}) collective-permute-start(f32[96,512]{1,0:T(8,128)S(1)} %get-tuple-element.39), channel_id=1, source_target_pairs={{0,7},{1,0},{2,1},{3,2},{4,3},{5,4},{6,5},{7,6},{8,15},{9,8},{10,9... | collective-permute-start | bytes 589832 | tf_op jit(solution)/shard_map/ppermute | solution.py:643
  22.4 14.3 %collective-permute-start.4 = (f32[96,512]{1,0:T(8,128)S(1)}, f32[96,512]{1,0:T(8,128)S(1)}, u32[]{:S(2)}, u32[]{:S(2)}) collective-permute-start(f32[96,512]{1,0:T(8,128)S(1)} %get-tuple-element.45), channel_id=1, source_target_pairs={{0,1},{1,2},{2,3},{3,4},{4,5},{5,6},{6,7},{7,0},{8,9},{9,10},{10,1... | collective-permute-start | bytes 589832 | tf_op jit(solution)/shard_map/ppermute | solution.py:643
  22.4 14.2 %collective-permute-start.5 = (f32[96,512]{1,0:T(8,128)S(1)}, f32[96,512]{1,0:T(8,128)S(1)}, u32[]{:S(2)}, u32[]{:S(2)}) collective-permute-start(f32[96,512]{1,0:T(8,128)S(1)} %get-tuple-element.46), channel_id=1, source_target_pairs={{0,7},{1,0},{2,1},{3,2},{4,3},{5,4},{6,5},{7,6},{8,15},{9,8},{10,9... | collective-permute-start | bytes 589832 | tf_op jit(solution)/shard_map/ppermute | solution.py:643
  36.7 5.0 %copy-start.1 = (f32[64,64]{1,0:T(8,128)S(1)}, f32[64,64]{1,0:T(8,128)}, u32[]{:S(2)}) copy-start(f32[64,64]{1,0:T(8,128)} %density.3) | copy-start | bytes 49156
  36.7 5.0 %copy-start.6 = (s32[1,8]{1,0:T(1,128)S(1)}, s32[1,8]{1,0:T(1,128)}, u32[]{:S(2)}) copy-start(s32[1,8]{1,0:T(1,128)} %mask.3) | copy-start | bytes 100
  36.7 5.0 %copy-start.7 = (s32[1,8]{1,0:T(1,128)S(1)}, s32[1,8]{1,0:T(1,128)}, u32[]{:S(2)}) copy-start(s32[1,8]{1,0:T(1,128)} %radius_map.3) | copy-start | bytes 100
  38.6 10.8 %all-to-all-start = ((f32[32,8,72]{2,1,0:T(8,128)}), f32[32,8,72]{2,1,0:T(8,128)S(1)}, u32[]{:S(2)}, u32[]{:S(2)}) async-start(f32[32,8,72]{2,1,0:T(8,128)} %bitcast), calls=%async_computation | async-start | bytes 262144 | tf_op jit(solution)/shard_map/all_to_all | solution.py:777

commit v3 on v2

--- a/solution.py
+++ b/solution.py
@@ -21,23 +21,45 @@
 
 PLANE = (NZ, NY)
 VMEM = pl.BlockSpec(memory_space=pltpu.VMEM)
-SMEM = pl.BlockSpec(memory_space=pltpu.SMEM)
 HBM = pl.BlockSpec(memory_space=pltpu.HBM)
 ANY = pl.BlockSpec(memory_space=pl.ANY)
-GRANT = 16 * 1024 * 1024
-EXTRA = 8
-SENT = 5 * NZ + EXTRA
+GRANT = 8 * 1024 * 1024
+HALF = NZ // 2
+HALO = 4 * NZ + HALF
+
+
+def mark_at(width):
+    return (HALO, width) if 2 * width <= NY else (HALO + RMAX, 0)
+
+
+def sent_rows(width):
+    return -(-(max(HALO + RMAX, mark_at(width)[0] + 1)) // 8) * 8
+
+
+def second_core():
+    return lax.rem(lax.axis_index("freq"), 2) == 1
+
+
+def neighbour(plane, axis, by):
+    size = (8, 128)[axis]
+    count = plane.shape[axis] // size
+    tiles = [lax.slice_in_dim(plane, k * size, (k + 1) * size, axis=axis) for k in range(count)]
+    turned = [pltpu.roll(tile, (-by) % size, axis) for tile in tiles]
+    at = lax.broadcasted_iota(jnp.int32, tiles[0].shape, axis)
+    edge = at == (size - 1 if by > 0 else 0)
+    out = []
+    for k in range(count):
+        other = turned[k + by] if 0 <= k + by < count else 0.0
+        out.append(jnp.where(edge, other, turned[k]))
+    return jnp.concatenate(out, axis=axis)
 
 
 def ahead(plane, axis):
-    size = plane.shape[axis]
-    at = lax.broadcasted_iota(jnp.int32, plane.shape, axis)
-    return jnp.where(at == size - 1, 0.0, pltpu.roll(plane, size - 1, axis))
+    return neighbour(plane, axis, 1)
 
 
 def behind(plane, axis):
-    at = lax.broadcasted_iota(jnp.int32, plane.shape, axis)
-    return jnp.where(at == 0, 0.0, pltpu.roll(plane, 1, axis))
+    return neighbour(plane, axis, -1)
 
 
 def dy_f(plane):
@@ -95,8 +117,8 @@
     pltpu.VMEM((2, 1, NY), jnp.float32),
     pltpu.SemaphoreType.DMA((4,)),
 ]
-SOURCE_SPECS = [HBM] * 4 + [SMEM] * 2
-SOURCE_VALUES = [VMEM] * 4 + [SMEM] * 2
+SOURCE_SPECS = [HBM] * 4 + [VMEM] * 2
+SOURCE_VALUES = [VMEM] * 6
 
 
 def source_copies(given, scratch):
@@ -114,22 +136,21 @@
     else:
         wave, profile = (jnp.where(run == 0, given[k][...], given[k + 1][...]) for k in (0, 2))
     row = wave[:, turn : turn + 1] * profile
-    plane = jnp.where(run == 0, given[4][0], given[5][0])
+    plane = jnp.where(run == 0, *(given[k][...].reshape(1, 1) for k in (4, 5)))
     at = lax.broadcasted_iota(jnp.int32, PLANE, 0)
     return jnp.where(at == plane, row, 0.0)
 
 
-def kernel_call(body, out_shape, in_specs, out_specs, scratch, name, micros=1, **more):
-    sizes = sum(math.prod(s.shape) * 4 for s in jax.tree.leaves(out_shape))
+def kernel_call(body, out_shape, in_specs, out_specs, scratch, name, micros=1, grant=GRANT, **more):
     return pl.pallas_call(
         body,
         out_shape=out_shape,
         in_specs=in_specs,
         out_specs=out_specs,
         scratch_shapes=scratch,
-        compiler_params=pltpu.CompilerParams(vmem_limit_bytes=GRANT),
+        compiler_params=pltpu.CompilerParams(vmem_limit_bytes=grant),
         cost_estimate=pl.CostEstimate(
-            flops=micros * 10**9, bytes_accessed=2 * sizes, transcendentals=0
+            flops=micros * 10**9, bytes_accessed=0, transcendentals=0
         ),
         name=name,
         **more,
@@ -155,7 +176,7 @@
 
 
 def first_planes(
-    fwd, adj, inverse, density, mask, to_prior, to_next, rows_in, cells, chosen, sems
+    fwd, adj, inverse, density, mask, to_prior, to_next, rows_in, inv, cells, chosen, sems
 ):
     rows = inverse.shape[0]
     width = density.shape[1]
@@ -164,8 +185,8 @@
         pltpu.make_async_copy(adj.at[0, :, rows - 1], rows_in.at[1], sems.at[1]),
         pltpu.make_async_copy(density, cells, sems.at[2]),
         pltpu.make_async_copy(mask, chosen, sems.at[3]),
-        pltpu.make_async_copy(inverse.at[0], to_prior.at[plane_at(4)], sems.at[4]),
-        pltpu.make_async_copy(inverse.at[rows - 1], to_next.at[plane_at(4)], sems.at[5]),
+        pltpu.make_async_copy(inverse.at[0], inv.at[0], sems.at[4]),
+        pltpu.make_async_copy(inverse.at[rows - 1], inv.at[1], sems.at[5]),
     ]
     for run, fields in enumerate((fwd, adj)):
         for k in range(2):
@@ -176,22 +197,76 @@
                 )
             )
     start_all(copies)
-    wait_all(copies[2:4])
+    wait_all(copies[2:6])
     at = lax.broadcasted_iota(jnp.int32, (1, width), 1) // (width // mask.shape[1])
     spread = jnp.zeros((1, width), jnp.float32)
     for k in range(mask.shape[1]):
         spread = jnp.where(at == k, chosen[:, k : k + 1].astype(jnp.float32), spread)
-    for sent, first in ((to_prior, 0), (to_next, density.shape[0] - RMAX)):
-        sent[pl.ds(5 * NZ, EXTRA), :] = jnp.zeros((EXTRA, NY), jnp.float32)
-        sent[pl.ds(5 * NZ, RMAX), pl.ds(0, width)] = cells[pl.ds(first, RMAX), :]
-        sent[pl.ds(5 * NZ + RMAX, 1), pl.ds(0, width)] = spread
+    mark_row, mark_lane = mark_at(width)
+    tail = to_next.shape[0] - HALO
+    for side, (sent, first) in enumerate(((to_prior, 0), (to_next, density.shape[0] - RMAX))):
+        half = jnp.where(second_core(), inv[side, HALF:, :], inv[side, :HALF, :])
+        sent[pl.ds(4 * NZ, HALF), :] = half
+        sent[pl.ds(HALO, tail), :] = jnp.zeros((tail, NY), jnp.float32)
+        sent[pl.ds(HALO, RMAX), pl.ds(0, width)] = cells[pl.ds(first, RMAX), :]
+        sent[pl.ds(mark_row, 1), pl.ds(mark_lane, width)] = spread
     for run in range(2):
         copies[run].wait()
         planes = [rows_in[run, k] for k in range(6)]
         magn = magnetic_yz(planes[4:], planes[:3], None)
         for k in range(2):
             to_next[plane_at(2 * run + k), :] = magn[k]
-    wait_all(copies[4:])
+    wait_all(copies[6:])
+
+
+def second_planes(fwd, adj, inverse, *rest):
+    given, (_, to_prior, to_next, own, head, tail, inv, sems, *scratch) = rest[:6], rest[6:]
+    rows = inverse.shape[0]
+    small = source_copies(given, scratch) + [
+        pltpu.make_async_copy(inverse.at[0], inv.at[0], sems.at[4]),
+        pltpu.make_async_copy(inverse.at[rows - 1], inv.at[1], sems.at[5]),
+    ]
+
+    def ends(fields, run):
+        return [
+            pltpu.make_async_copy(fields.at[0, :, pl.ds(0, 2)], head.at[run], sems.at[2 * run]),
+            pltpu.make_async_copy(
+                fields.at[0, :, pl.ds(rows - 2, 2)], tail.at[run], sems.at[2 * run + 1]
+            ),
+        ]
+
+    start_all(ends(fwd, 0) + small + ends(adj, 1))
+    wait_all(small)
+
+    def one_run(run, carry):
+        wait_all(ends(fwd, run))
+
+        def row(ref, x):
+            return tuple(
+                tuple(ref[run, k, x] for k in range(first, first + 3)) for first in (0, 3)
+            )
+
+        source = source_of(run, 0, given, scratch)
+        elec, magn = row(head, 0)
+        magn = magnetic(magn, elec, (head[run, 1, 1], head[run, 2, 1]))
+        elec = electric(elec, magn, None, courant * inv[0], source)
+        for k in range(2):
+            to_prior[plane_at(2 * run + k), :] = elec[1 + k]
+        for k in range(3):
+            own[run, k] = elec[k]
+        (elec_6, magn_6), (elec, magn) = row(tail, 0), row(tail, 1)
+        yz_6 = magnetic_yz(magn_6[1:], elec_6, elec[1:])
+        magn = magnetic(magn, elec, None)
+        elec = electric(elec, magn, yz_6, courant * inv[1], source)
+        magn = magnetic(magn, elec, None)
+        for k in range(2):
+            to_next[plane_at(2 * run + k), :] = magn[1 + k]
+        for k in range(3):
+            own[run, 3 + k] = elec[k]
+            own[run, 6 + k] = magn[k]
+        return carry
+
+    lax.fori_loop(0, 2, one_run, 0)
 
 
 class State:
@@ -242,9 +317,7 @@
 
 
 def interior(fwd, adj, inverse, *rest):
-    given, (to_prior, to_next, own, fwd_out, adj_out, state, share), (inv, sems, *scratch) = (
-        rest[:6], rest[6:13], rest[13:]
-    )
+    given, (_, state, share, inv, sems, *scratch) = rest[:6], rest[6:]
     rows = inverse.shape[0]
     last = rows - 1
     into = source_copies(given, scratch) + [pltpu.make_async_copy(inverse, inv, sems.at[4])]
@@ -255,26 +328,6 @@
     start_all([load(fwd, 0)] + into + [load(adj, 1)])
     wait_all(into)
     rows_of = in_place(state)
-
-    def edges(run, source):
-        elec = electric(
-            rows_of.load(run, 0, 0), rows_of.load(run, 3, 0), None, courant * inv[0], source
-        )
-        for k in range(2):
-            to_prior[plane_at(2 * run + k), :] = elec[1 + k]
-        for k in range(3):
-            own[run, k] = elec[k]
-        elec, magn = rows_of.load(run, 0, last), rows_of.load(run, 3, last)
-        magn = magnetic(magn, elec, None)
-        elec = electric(
-            elec, magn, rows_of.magnetic_yz(run, last - 1), courant * inv[last], source
-        )
-        magn = magnetic(magn, elec, None)
-        for k in range(2):
-            to_next[plane_at(2 * run + k), :] = magn[1 + k]
-        for k in range(3):
-            own[run, 3 + k] = elec[k]
-            own[run, 6 + k] = magn[k]
 
     for turn in range(STEPS):
 
@@ -288,8 +341,6 @@
                     rows_of.electric(
                         run, x, rows_of.magnetic_yz(run, x - 1), courant * inv[x], source
                     )
-            if turn == 0:
-                edges(run, source)
             return carry
 
         lax.fori_loop(0, 2, one_run, 0)
@@ -297,17 +348,6 @@
             share[x] = products(state, x) + (share[x] if turn > 0 else 0.0)
     for x in (0, last):
         share[x] = jnp.zeros(share.shape[1:], jnp.float32)
-    out = []
-    for run, fields in enumerate((fwd_out, adj_out)):
-        for kind, first in enumerate((STEPS, STEPS - 1)):
-            done = (pl.ds(3 * kind, 3), pl.ds(first, rows - STEPS - first))
-            out.append(
-                pltpu.make_async_copy(
-                    state.at[run, *done], fields.at[0, *done], sems.at[2 * run + kind]
-                )
-            )
-    start_all(out)
-    wait_all(out)
 
 
 def flags():
@@ -317,13 +357,46 @@
     return has_prior, has_next
 
 
-def border_rows(run, turn, state, source, inv, resp_in, resp_out, prior_a, next_a, here):
+def write_copies(parts, fields, sems):
+    return [
+        pltpu.make_async_copy(
+            ref.at[run, *(pl.ds(at, n) for at, n in zip(source, count))],
+            fields[run].at[0, *(pl.ds(at, n) for at, n in zip(target, count))],
+            sems.at[len(parts) * run + part],
+        )
+        for run in range(2)
+        for part, (ref, source, count, target) in enumerate(parts)
+    ]
+
+
+def respond(before, early, own, other, resp, scaled):
+    second = second_core()
+    for side, flag in enumerate(flags()):
+        mine, theirs = (ref[pl.ds(side * HALF, HALF), :] for ref in (own, other))
+        scaled[side, pl.ds(0, HALF), :] = courant * flag * jnp.where(second, theirs, mine)
+        scaled[side, pl.ds(HALF, HALF), :] = courant * flag * jnp.where(second, mine, theirs)
+    flagged = courant * flags()[0]
+
+    def one_run(run, carry):
+        magn_y, magn_z = flagged * before[run, 2, 0], -flagged * before[run, 1, 0]
+        resp[run, 0] = scaled[0] * (dy_b(magn_z) - dz_b(magn_y))
+        resp[run, 1] = -scaled[0] * magn_z
+        resp[run, 2] = scaled[0] * magn_y
+        resp[run, 3] = jnp.zeros(PLANE, jnp.float32)
+        resp[run, 4] = magn_y
+        resp[run, 5] = magn_z
+        resp[run, 6] = scaled[1] * early[run, 5, 1]
+        resp[run, 7] = -scaled[1] * early[run, 4, 1]
+        return carry
+
+    lax.fori_loop(0, 2, one_run, 0)
+
+
+def border_rows(run, turn, state, source, inv, here, resp_in=None, resp_out=None, scaled=None):
     has_prior, has_next = flags()
     flagged = courant * has_prior
     last = inv.shape[0] - 1
     whole = here is not None
-    scaled_prior = flagged * prior_a[plane_at(4), :]
-    scaled_next = (courant * has_next) * next_a[plane_at(4), :]
 
     def received(ref):
         return tuple(ref[plane_at(2 * run + k), :] for k in range(2))
@@ -339,22 +412,17 @@
             old[1] - courant * (dz_f(elec_r[0]) + elec_r[2]) + flagged * own_z,
             old[2] + courant * (elec_r[1] + dy_f(elec_r[0])) - flagged * own_y,
         )
-    if turn == 0:
-        resp_out[run, 0] = scaled_prior * (dy_b(magn_r[2]) - dz_b(magn_r[1]))
-        resp_out[run, 1] = -scaled_prior * magn_r[2]
-        resp_out[run, 2] = scaled_prior * magn_r[1]
-        resp_out[run, 3] = jnp.zeros(PLANE, jnp.float32)
-    elif whole:
-        resp_out[run, 0] = elec_r[0] + scaled_prior * (dy_b(magn_r[2]) - dz_b(magn_r[1]))
-        resp_out[run, 1] = elec_r[1] + scaled_prior * (
-            dz_b(magn_r[0]) - (magn_r[2] + courant * elec_r[1])
-        )
-        resp_out[run, 2] = elec_r[2] + scaled_prior * (
-            (magn_r[1] - courant * elec_r[2]) - dy_b(magn_r[0])
-        )
-        resp_out[run, 3] = magn_r[0]
-    resp_out[run, 4] = magn_r[1]
-    resp_out[run, 5] = magn_r[2]
+        if whole:
+            resp_out[run, 0] = elec_r[0] + scaled[0] * (dy_b(magn_r[2]) - dz_b(magn_r[1]))
+            resp_out[run, 1] = elec_r[1] + scaled[0] * (
+                dz_b(magn_r[0]) - (magn_r[2] + courant * elec_r[1])
+            )
+            resp_out[run, 2] = elec_r[2] + scaled[0] * (
+                (magn_r[1] - courant * elec_r[2]) - dy_b(magn_r[0])
+            )
+            resp_out[run, 3] = magn_r[0]
+        resp_out[run, 4] = magn_r[1]
+        resp_out[run, 5] = magn_r[2]
     for x in range(turn):
         state.magnetic(run, x, state.electric_yz(run, x + 1))
     if whole:
@@ -379,34 +447,25 @@
         state.store(run, 3, last, (magn_x,))
     for x in range(last - turn, last + (1 if whole else 0)):
         state.electric(run, x, state.magnetic_yz(run, x - 1), courant * inv[x], source)
-    if turn == 0:
-        resp_out[run, 6] = scaled_next * magn[2]
-        resp_out[run, 7] = -scaled_next * magn[1]
-    elif whole:
+    if turn > 0 and whole:
         elec_y, elec_z = resp_in[run, 6], resp_in[run, 7]
         magn_x = -courant * (dy_f(elec_z) - dz_f(elec_y))
-        resp_out[run, 6] = elec_y + scaled_next * (dz_b(magn_x) - (courant * elec_y - magn[2]))
-        resp_out[run, 7] = elec_z + scaled_next * (
-            (-courant * elec_z - magn[1]) - dy_b(magn_x)
-        )
-    else:
+        resp_out[run, 6] = elec_y + scaled[1] * (dz_b(magn_x) - (courant * elec_y - magn[2]))
+        resp_out[run, 7] = elec_z + scaled[1] * ((-courant * elec_z - magn[1]) - dy_b(magn_x))
+    elif turn > 0:
         resp_out[run, 6] = resp_in[run, 6]
         resp_out[run, 7] = resp_in[run, 7]
 
 
-def step_one(inv, *rest):
-    given, (before, own, prior_a, next_a), (to_prior, to_next, early, resp, share) = (
-        rest[:6], rest[6:10], rest[10:]
-    )
+def third_planes(inv, *rest):
+    given, (before, own, to_prior, to_next) = rest[:6], rest[6:]
     last = inv.shape[0] - 1
 
     def one_run(run, carry):
-        state = State(lambda k, x: (before, x), lambda k, x: (early, min(x, 1)), ())
-        source = source_of(run, 0, given, ())
-        scaled = courant * inv[0]
+        state = State(lambda k, x: (before, x), None, ())
         elec = tuple(own[run, k] for k in range(3))
         magn = magnetic(state.load(run, 3, 0), elec, state.electric_yz(run, 1))
-        sent = electric_yz(elec[1:], magn, None, scaled)
+        sent = electric_yz(elec[1:], magn, None, courant * inv[0])
         for k in range(2):
             to_prior[plane_at(2 * run + k), :] = sent[k]
         elec = tuple(own[run, 3 + k] for k in range(3))
@@ -418,9 +477,19 @@
         sent = magnetic_yz(magn[1:], elec, None)
         for k in range(2):
             to_next[plane_at(2 * run + k), :] = sent[k]
-        border_rows(
-            run, 0, state, source, inv, None, resp, prior_a, next_a, (prior_a, next_a)
-        )
+        return carry
+
+    lax.fori_loop(0, 2, one_run, 0)
+
+
+def step_one(inv, *rest):
+    given, (before, prior_a, next_a, early, halves, share) = rest[:6], rest[6:]
+    for side, ref in enumerate((prior_a, next_a)):
+        halves[pl.ds(side * HALF, HALF), :] = ref[pl.ds(4 * NZ, HALF), :]
+
+    def one_run(run, carry):
+        state = State(lambda k, x: (before, x), lambda k, x: (early, min(x, 1)), ())
+        border_rows(run, 0, state, source_of(run, 0, given, ()), inv, (prior_a, next_a))
         return carry
 
     lax.fori_loop(0, 2, one_run, 0)
@@ -428,13 +497,21 @@
         share[side] = products(early, side)
 
 
-def borders(fwd, adj, inv, *rest):
-    given, (before, early, resp_in, share, ends, prior_a, next_a, prior_b, next_b) = (
-        rest[:6], rest[6:15]
-    )
-    fwd_out, adj_out, kept, summed, waiting, inner, resp, total, sems = rest[15:]
+def borders(inv, *rest):
+    given, (before, early, resp_in, scaled, share, ends, prior_b, next_b) = rest[:6], rest[6:14]
+    kept, inner, summed, waiting, fwd_out, adj_out, resp, total, sems = rest[14:]
     rows = inv.shape[0]
     last = rows - 1
+    inside = rows - 2 * STEPS
+    out = write_copies(
+        (
+            (before, (0, STEPS), (3, inside), (0, STEPS)),
+            (before, (3, STEPS - 1), (3, inside + 1), (3, STEPS - 1)),
+        ),
+        (fwd_out, adj_out),
+        sems,
+    )
+    start_all(out)
     homes = {0: (kept, 0), last - 1: (kept, 1), last: (kept, 2)}
     homes |= {1: (inner, 0), 2: (inner, 1), last - 2: (inner, 2)}
 
@@ -452,36 +529,14 @@
             state = State(handed_in, lambda k, x: homes[x], written)
             border_rows(
                 run, turn, state, source_of(run, turn, given, ()), inv,
-                resp_in if turn == 1 else resp, resp if whole else waiting, prior_a, next_a,
                 (prior_b, next_b) if whole else None,
+                resp_in if turn == 1 else resp, resp if whole else waiting, scaled,
             )
             seen[:] = [state.written]
             return carry
 
         lax.fori_loop(0, 2, one_run, 0)
         written = seen[0]
-        if not whole:
-            out = []
-            for run, fields in enumerate((fwd_out, adj_out)):
-                for part, (ref, at, x, count, first, parts) in enumerate(
-                    (
-                        (inner, 0, 1, 1, 0, 6),
-                        (inner, 1, 2, 1, 0, 3),
-                        (inner, 2, last - 2, 1, 0, 6),
-                        (kept, 1, last - 1, 1, 0, 6),
-                        (kept, 0, 0, 1, 0, 1),
-                        (kept, 0, 0, 1, 3, 3),
-                        (kept, 2, last, 1, 3, 1),
-                    )
-                ):
-                    out.append(
-                        pltpu.make_async_copy(
-                            ref.at[run, pl.ds(first, parts), pl.ds(at, count)],
-                            fields.at[0, pl.ds(first, parts), pl.ds(x, count)],
-                            sems.at[7 * run + part],
-                        )
-                    )
-            start_all(out)
         reached = list(range(turn + 1)) + list(range(last - turn, last + 1))
         for x in reached if whole else reached[1:-1]:
             if turn > 1 and min(x, last - x) < turn:
@@ -495,9 +550,8 @@
     wait_all(out)
 
 
-def last_planes(fwd, adj, inv, *rest):
-    given, (kept, summed, waiting, prior_c, next_c) = rest[:6], rest[6:11]
-    fwd_out, adj_out, blocks, front, back, back_h, sems = rest[11:]
+def last_planes(inv, *rest):
+    given, (kept, summed, waiting, prior_c, next_c, _, blocks, ends) = rest[:6], rest[6:]
     last = inv.shape[0] - 1
     has_prior, has_next = flags()
 
@@ -514,31 +568,18 @@
             row(1, 0, 2), row(3, 0, 3), arrived(prior_c, has_prior, 4), courant * inv[0]
         )
         for k in range(2):
-            front[run, k] = elec[k]
+            ends[run, k, 0] = elec[k]
         elec = row(0, 2, 3)
         yz = magnetic_yz(row(4, 2, 2), elec, arrived(next_c, has_next, 6))
         source = source_of(run, STEPS - 1, given, ())
         elec = electric(elec, row(3, 2, 1) + yz, row(4, 1, 2), courant * inv[last], source)
         for k in range(3):
-            back[run, k] = elec[k]
+            ends[run, 2 + k, 0] = elec[k]
         for k in range(2):
-            back_h[run, k] = yz[k]
+            ends[run, 5 + k, 0] = yz[k]
         return carry
 
     lax.fori_loop(0, 2, one_run, 0)
-    out = []
-    for run, fields in enumerate((fwd_out, adj_out)):
-        for part, (source, first, count, x) in enumerate(
-            ((front, 1, 2, 0), (back, 0, 3, last), (back_h, 4, 2, last))
-        ):
-            out.append(
-                pltpu.make_async_copy(
-                    source.at[run],
-                    fields.at[0, pl.ds(first, count), x],
-                    sems.at[3 * run + part],
-                )
-            )
-    start_all(out)
 
     def row_sum(pairs):
         total = pairs[0][0] * pairs[0][1]
@@ -546,8 +587,10 @@
             total = total + first * second
         return jnp.sum(total, axis=0, keepdims=True)
 
-    head = row_sum([(kept[0, 0, 0], kept[1, 0, 0])] + [(front[0, k], front[1, k]) for k in range(2)])
-    tail = row_sum([(back[0, k], back[1, k]) for k in range(3)])
+    head = row_sum(
+        [(kept[0, 0, 0], kept[1, 0, 0])] + [(ends[0, k, 0], ends[1, k, 0]) for k in range(2)]
+    )
+    tail = row_sum([(ends[0, 2 + k, 0], ends[1, 2 + k, 0]) for k in range(3)])
     at = lax.broadcasted_iota(jnp.int32, summed.shape, 0)
     full = summed[...] + jnp.where(at == 0, head, 0.0) + jnp.where(at == last, tail, 0.0)
     slabs, width = blocks.shape[1], blocks.shape[3]
@@ -555,6 +598,40 @@
         turned = pltpu.roll(full, (RMAX - k * (NY // slabs)) % NY, 1)
         for f in range(blocks.shape[0]):
             blocks[f, k] = turned[:, :width]
+
+
+def write_borders(fwd, adj, kept, inner, fwd_out, adj_out, done, sems):
+    last = fwd.shape[2] - 1
+    done[...] = jnp.zeros_like(done)
+    out = write_copies(
+        (
+            (inner, (0, 0), (6, 1), (0, 1)),
+            (inner, (0, 1), (3, 1), (0, 2)),
+            (inner, (0, 2), (6, 1), (0, last - 2)),
+            (kept, (0, 1), (6, 1), (0, last - 1)),
+            (kept, (0, 0), (1, 1), (0, 0)),
+            (kept, (3, 0), (3, 1), (3, 0)),
+            (kept, (3, 2), (1, 1), (3, last)),
+        ),
+        (fwd_out, adj_out),
+        sems,
+    )
+    start_all(out)
+    wait_all(out)
+
+
+def write_ends(fwd, adj, ends, fwd_out, adj_out, sems):
+    last = fwd.shape[2] - 1
+    out = write_copies(
+        (
+            (ends, (0, 0), (2, 1), (1, 0)),
+            (ends, (2, 0), (3, 1), (0, last)),
+            (ends, (5, 0), (2, 1), (4, last)),
+        ),
+        (fwd_out, adj_out),
+        sems,
+    )
+    start_all(out)
     wait_all(out)
 
 
@@ -603,13 +680,14 @@
 ):
     tile_rows, width = density.shape
     reach = padded.shape[1]
-    above, below = (ref[pl.ds(5 * NZ, EXTRA), :] for ref in (prior_a, next_a))
-    rows_of[pl.ds(0, RMAX), :] = above[:RMAX, :width]
+    above, below = (ref[pl.ds(HALO, RMAX), :] for ref in (prior_a, next_a))
+    mark_row, mark_lane = mark_at(width)
+    rows_of[pl.ds(0, RMAX), :] = above[:, :width]
     rows_of[pl.ds(RMAX, tile_rows), :] = density[...]
-    rows_of[pl.ds(RMAX + tile_rows, RMAX), :] = below[:RMAX, :width]
+    rows_of[pl.ds(RMAX + tile_rows, RMAX), :] = below[:, :width]
     marks_of[...] = jnp.zeros_like(marks_of)
-    marks_of[pl.ds(0, 1), :] = above[RMAX : RMAX + 1, :width]
-    marks_of[pl.ds(1, 1), :] = below[RMAX : RMAX + 1, :width]
+    for side, ref in enumerate((prior_a, next_a)):
+        marks_of[pl.ds(side, 1), :] = ref[pl.ds(mark_row, 1), pl.ds(mark_lane, width)]
     sides = marks_of[...].T
     first = lax.axis_index("slab") * tile_rows - RMAX
     at = lax.broadcasted_iota(jnp.int32, (width, reach), 1)
@@ -679,11 +757,12 @@
 
     to_prior, to_next = kernel_call(
         first_planes,
-        (shaped(SENT, NY), shaped(SENT, NY)),
+        (shaped(sent_rows(width), NY),) * 2,
         [HBM] * 5,
         (VMEM, VMEM),
         [
             vmem(2, 6, *PLANE),
+            vmem(2, *PLANE),
             vmem(tile_rows, width),
             vmem(*design_mask.shape, kind=jnp.int32),
             dma((10,)),
@@ -692,36 +771,61 @@
     )(*fields, *pinned((design_density, design_mask)))
     prior_a = around(to_next, "slab", 1)
     next_a = around(to_prior, "slab", -1)
-    to_prior, to_next, own, forward_part, adjoint_part, state, share = kernel_call(
+    to_prior, to_next, own = kernel_call(
+        second_planes,
+        (four, four, shaped(2, 9, *PLANE)),
+        [HBM] * 3 + SOURCE_SPECS + [ANY],
+        (VMEM,) * 3,
+        [
+            vmem(2, 6, 2, *PLANE),
+            vmem(2, 6, 2, *PLANE),
+            vmem(2, *PLANE),
+            dma((6,)),
+            *SOURCE_SCRATCH,
+        ],
+        "second_planes",
+        micros=2,
+    )(*fields, *sources, to_prior)
+    prior_b = around(to_next, "slab", 1)
+    next_b = around(to_prior, "slab", -1)
+    state, share = kernel_call(
         interior,
-        (
-            four,
-            four,
-            shaped(2, 9, *PLANE),
-            field_shape,
-            field_shape,
-            state_shape,
-            shaped(rows, 8, NY),
-        ),
-        [HBM] * 3 + SOURCE_SPECS,
-        (VMEM, VMEM, VMEM, HBM, HBM, VMEM, VMEM),
+        (state_shape, shaped(rows, 8, NY)),
+        [HBM] * 3 + SOURCE_SPECS + [ANY],
+        (VMEM, VMEM),
         [vmem(rows, *PLANE), dma((5,)), *SOURCE_SCRATCH],
         "interior",
         micros=8,
-    )(*fields, *sources)
-    prior_b = around(to_next, "slab", 1)
-    next_b = around(to_prior, "slab", -1)
-    to_prior, to_next, early, resp, ends = kernel_call(
+    )(*fields, *sources, own)
+    to_prior, to_next = kernel_call(
+        third_planes,
+        (four, four),
+        [VMEM] + SOURCE_VALUES + [VMEM] * 2,
+        (VMEM,) * 2,
+        [],
+        "third_planes",
+    )(inverse_permittivity, *waves, *planes, state, own)
+    prior_c = around(to_next, "slab", 1)
+    next_c = around(to_prior, "slab", -1)
+    early, halves, ends = kernel_call(
         step_one,
-        (four, four, shaped(2, 6, 2, *PLANE), shaped(2, 8, *PLANE), shaped(2, 8, NY)),
-        [VMEM] + SOURCE_VALUES + [VMEM] * 4,
-        (VMEM,) * 5,
+        (shaped(2, 6, 2, *PLANE), shaped(*PLANE), shaped(2, 8, NY)),
+        [VMEM] + SOURCE_VALUES + [VMEM] * 3,
+        (VMEM,) * 3,
         [],
         "step_one",
-        micros=3,
-    )(inverse_permittivity, *waves, *planes, state, own, prior_a, next_a)
-    prior_c = around(to_next, "slab", 1)
-    next_c = around(to_prior, "slab", -1)
+        micros=0,
+    )(inverse_permittivity, *waves, *planes, state, prior_a, next_a)
+    other = lax.ppermute(halves, "freq", [(i, i ^ 1) for i in range(freqs)])
+    resp, scaled = kernel_call(
+        respond,
+        (shaped(2, 8, *PLANE), shaped(2, *PLANE)),
+        [VMEM] * 4,
+        (VMEM,) * 2,
+        [],
+        "respond",
+        micros=0,
+    )(state, early, halves, other)
     padded, chosen, weights = kernel_call(
         filter_operands,
         (shaped(width, reach), shaped(width, reach), shaped(width, tile_rows)),
@@ -729,49 +833,48 @@
         (VMEM,) * 3,
         [vmem(reach, width), vmem(8, width)],
         "filter_operands",
+        micros=0,
     )(prior_a, next_a, design_density, design_mask, radius_map)
-    forward_part, adjoint_part, kept, summed, waiting = kernel_call(
+    three = shaped(2, 6, 3, *PLANE)
+    kept, inner, summed, waiting, forward_part, adjoint_part = kernel_call(
         borders,
-        (
-            field_shape,
-            field_shape,
-            shaped(2, 6, 3, *PLANE),
-            shaped(rows, NY),
-            shaped(2, 8, *PLANE),
-        ),
-        [HBM] * 2 + [VMEM] + SOURCE_VALUES + [VMEM] * 9,
-        (HBM, HBM, VMEM, VMEM, VMEM),
-        [
-            vmem(2, 6, 3, *PLANE),
-            vmem(2, 8, *PLANE),
-            vmem(rows, 8, NY),
-            dma((14,)),
-        ],
+        (three, three, shaped(rows, NY), shaped(2, 8, *PLANE), field_shape, field_shape),
+        [VMEM] + SOURCE_VALUES + [VMEM] * 8,
+        (VMEM,) * 4 + (HBM,) * 2,
+        [vmem(2, 8, *PLANE), vmem(rows, 8, NY), dma((4,))],
         "borders",
-        micros=3,
+        micros=0,
+        grant=2 * GRANT,
+    )(
+        inverse_permittivity, *waves, *planes, state, early, resp, scaled, share, ends,
+        prior_b, next_b,
+    )
+    forward_part, adjoint_part, done = kernel_call(
+        write_borders,
+        (field_shape, field_shape, shaped(8, 128)),
+        [HBM] * 2 + [VMEM] * 2,
+        (HBM, HBM, VMEM),
+        [dma((14,))],
+        "write_borders",
         input_output_aliases={0: 0, 1: 1},
-    )(
-        forward_part, adjoint_part, inverse_permittivity, *waves, *planes, state, early, resp,
-        share, ends, prior_a, next_a, prior_b, next_b,
-    )
-    forward_out, adjoint_out, blocks = kernel_call(
+    )(forward_part, adjoint_part, kept, inner)
+    blocks, ends = kernel_call(
         last_planes,
-        (field_shape, field_shape, shaped(freqs, slabs, rows, reach)),
-        [HBM] * 2 + [VMEM] + SOURCE_VALUES + [VMEM] * 5,
-        (HBM, HBM, VMEM),
-        [
-            vmem(2, 2, *PLANE),
-            vmem(2, 3, *PLANE),
-            vmem(2, 2, *PLANE),
-            dma((6,)),
-        ],
+        (shaped(freqs, slabs, rows, reach), shaped(2, 7, 1, *PLANE)),
+        [VMEM] + SOURCE_VALUES + [VMEM] * 6,
+        (VMEM, VMEM),
+        [],
         "last_planes",
-        micros=2,
+    )(inverse_permittivity, *waves, *planes, kept, summed, waiting, prior_c, next_c, done)
+    forward_out, adjoint_out = kernel_call(
+        write_ends,
+        (field_shape, field_shape),
+        [HBM] * 2 + [VMEM],
+        (HBM, HBM),
+        [dma((6,))],
+        "write_ends",
         input_output_aliases={0: 0, 1: 1},
-    )(
-        forward_part, adjoint_part, inverse_permittivity, *waves, *planes,
-        kept, summed, waiting, prior_c, next_c,
-    )
+    )(forward_part, adjoint_part, ends)
 
     blocks = blocks.reshape(freqs * slabs, rows, reach)
     blocks = lax.all_to_all(blocks, ("freq", "slab"), 0, 0, tiled=True)

time: 51.2 us -> 49.3 us (0.963)
  waiting for transfers between devices: 12.7 us -> 8.09 us
  starting transfers between devices: 18.7 us -> 20.3 us
  Pallas kernels: 17.4 us -> 18.4 us
    ppermute x6, waiting for transfers between devices: 5.95 us -> 0.91 us  [around(): lax.ppermute(shard, axis, [(i, (i + by) % count) for i in range(count)])]
    all_to_all x1, starting transfers between devices: 3.1 us -> 4.64 us  [on_device(): blocks = lax.all_to_all(blocks, ('freq', 'slab'), 0, 0, tiled=True)]
    ppermute x0 -> x1, waiting for transfers between devices: none -> 1.22 us  [on_device(): other = lax.ppermute(halves, 'freq', [(i, i ^ 1) for i in range(freqs)])]
    pallas_call x5 -> x10, Pallas kernels: 14.9 us -> 16 us  [the longest x1 5.6 us: on_device(): kernel_call(interior, (state_shape, shaped(rows, 8, NY)), [HBM] * 3 + SOU...]
    all_to_all x1, waiting for transfers between devices: 6.8 us -> 5.96 us  [on_device(): blocks = lax.all_to_all(blocks, ('freq', 'slab'), 0, 0, tiled=True)]
  transfers between devices with their start and end apart: 7 -> 8, of which waited for: 3 -> 3; matrix products, arithmetic and copies ran while one was open for 0% -> 0% of each run, Pallas kernels for 25% -> 29%
where the time goes in v3:
time: 49.3 us; the launch traced here: 49 us
  starting transfers between devices  20.3 us (41%)
  Pallas kernels  18.4 us (37%)
  waiting for transfers between devices  8.09 us (16%)
  between operations  2.16 us (4%)
    ppermute x6, starting transfers between devices, around(): lax.ppermute(shard, axis, [(i, (i + by) % count) for i in range(count)])  15.6 us
    all_to_all x1, waiting for transfers between devices, on_device(): blocks = lax.all_to_all(blocks, ('freq', 'slab'), 0, 0, tiled=True)  5.96 us
    pallas_call x1, Pallas kernels, on_device(): kernel_call(interior, (state_shape, shaped(rows, 8, NY)), [HBM] * 3 + SOU...  5.6 us
    all_to_all x1, starting transfers between devices, on_device(): blocks = lax.all_to_all(blocks, ('freq', 'slab'), 0, 0, tiled=True)  4.64 us
    pallas_call x1, Pallas kernels, on_device(): kernel_call(borders, (three, three, shaped(rows, NY), shaped(2, 8, *PLANE...  2.16 us
    pallas_call x1, Pallas kernels, on_device(): kernel_call(second_planes, (four, four, shaped(2, 9, *PLANE)), [HBM] * 3...  2.1 us
    pallas_call x1, Pallas kernels, on_device(): kernel_call(project, shaped(tile_rows, width), [VMEM] * 5, VMEM, [], 'pro...  1.59 us
    pallas_call x1, Pallas kernels, on_device(): kernel_call(write_borders, (field_shape, field_shape, shaped(8, 128)), [H...  1.57 us
  transfers between devices with their start and end apart: 8, of which 3 were waited for; matrix products, arithmetic and copies ran while one was open for 0% of the time, Pallas kernels for 29%

profile of v3, /device:TPU:0, one launch (start us, length us, event | category | flops | bytes accessed | tf_op | source)
XLA Modules:
  0.0 49.0 jit_solution(6633174354627282394)
XLA Ops:
  0.6 1.4 %first_planes.1 = (f32[112,512]{1,0:T(8,128)S(1)}, f32[112,512]{1,0:T(8,128)S(1)}) custom-call(f32[1,6,8,24,512]{4,3,2,1,0:T(8,128)} %fwd.5, f32[1,6,8,24,512]{4,3,2,1,0:T(8,128)} %adj.5, f32[8,24,512]{2,1,0:T(8,128)} %inv.7, f32[64,64]{1,0:T(8,128)} %density.3, s32[1,8]{1,0:T(1,128)} %mask.3), custom_call_target="tpu_custom_call" | custom-call | flops 1000000000 | tf_op jit(solution)/shard_map/first_planes/pallas_call | solution.py:758
  2.1 3.0 %collective-permute-start = (f32[112,512]{1,0:T(8,128)S(1)}, f32[112,512]{1,0:T(8,128)S(1)}, u32[]{:S(2)}, u32[]{:S(2)}) collective-permute-start(f32[112,512]{1,0:T(8,128)S(1)} %get-tuple-element.36), channel_id=1, source_target_pairs={{0,1},{1,2},{2,3},{3,4},{4,5},{5,6},{6,7},{7,0},{8,9},{9,10},{10,1... | collective-permute-start | bytes 688136 | tf_op jit(solution)/shard_map/ppermute | solution.py:721
  5.1 3.1 %collective-permute-start.1 = (f32[112,512]{1,0:T(8,128)S(1)}, f32[112,512]{1,0:T(8,128)S(1)}, u32[]{:S(2)}, u32[]{:S(2)}) collective-permute-start(f32[112,512]{1,0:T(8,128)S(1)} %get-tuple-element.33.rest_6_), channel_id=1, source_target_pairs={{0,7},{1,0},{2,1},{3,2},{4,3},{5,4},{6,5},{7,6},{8,15},{9,8},{10,9... | collective-permute-start | bytes 688136 | tf_op jit(solution)/shard_map/ppermute | solution.py:721
  9.5 2.1 %second_planes.1 = (f32[96,512]{1,0:T(8,128)S(1)}, f32[96,512]{1,0:T(8,128)S(1)}, f32[2,9,24,512]{3,2,1,0:T(8,128)S(1)}) custom-call(f32[1,6,8,24,512]{4,3,2,1,0:T(8,128)} %fwd.5, f32[1,6,8,24,512]{4,3,2,1,0:T(8,128)} %adj.5, f32[8,24,512]{2,1,0:T(8,128)} %inv.7, f32[1,3]{1,0:T(1,128)} %rest_0_.11, f32[1,3]{1,0:T(1,128)} %rest_1_.11, f32[1,512]{1,0:T(1,128)} %rest_2_.11, ...), custom_call_target="tpu_custom_call" | custom-call | flops 2000000000 | tf_op jit(solution)/shard_map/second_planes/pallas_call | solution.py:774
  11.6 0.1 collective-permute-start.3
  11.7 4.7 %collective-permute-start.4 = (f32[96,512]{1,0:T(8,128)S(1)}, f32[96,512]{1,0:T(8,128)S(1)}, u32[]{:S(2)}, u32[]{:S(2)}) collective-permute-start(f32[96,512]{1,0:T(8,128)S(1)} %get-tuple-element.44), channel_id=1, source_target_pairs={{0,7},{1,0},{2,1},{3,2},{4,3},{5,4},{6,5},{7,6},{8,15},{9,8},{10,9... | collective-permute-start | bytes 589832 | tf_op jit(solution)/shard_map/ppermute | solution.py:721
  16.4 0.0 copy-start.5
  16.4 5.6 %interior.1 = (f32[2,6,8,24,512]{4,3,2,1,0:T(8,128)S(1)}, f32[8,8,512]{2,1,0:T(8,128)S(1)}) custom-call(f32[1,6,8,24,512]{4,3,2,1,0:T(8,128)} %fwd.5, f32[1,6,8,24,512]{4,3,2,1,0:T(8,128)} %adj.5, f32[8,24,512]{2,1,0:T(8,128)} %inv.7, f32[1,3]{1,0:T(1,128)} %rest_0_.11, f32[1,3]{1,0:T(1,128)} %rest_1_.11, f32[1,512]{1,0:T(1,128)} %rest_2_.11, ...), custom_call_target="tpu_custom_call" | custom-call | flops 8000000000 | tf_op jit(solution)/shard_map/interior/pallas_call | solution.py:791
  22.0 0.4 third_planes.1
  22.5 0.1 collective-permute-start.5
  22.6 4.7 %collective-permute-start.6 = (f32[96,512]{1,0:T(8,128)S(1)}, f32[96,512]{1,0:T(8,128)S(1)}, u32[]{:S(2)}, u32[]{:S(2)}) collective-permute-start(f32[96,512]{1,0:T(8,128)S(1)} %get-tuple-element.54), channel_id=1, source_target_pairs={{0,7},{1,0},{2,1},{3,2},{4,3},{5,4},{6,5},{7,6},{8,15},{9,8},{10,9... | collective-permute-start | bytes 589832 | tf_op jit(solution)/shard_map/ppermute | solution.py:721
  27.3 0.4 step_one.1
  27.7 0.1 collective-permute-start.2
  27.8 1.2 %collective-permute-done.2.other = f32[24,512]{1,0:T(8,128)S(1)} collective-permute-done((f32[24,512]{1,0:T(8,128)S(1)}, f32[24,512]{1,0:T(8,128)S(1)}, u32[]{:S(2)}, u32[]{:S(2)}) %collective-permute-start.2) | collective-permute-done | bytes 49184 | tf_op jit(solution)/shard_map/ppermute | solution.py:819
  29.0 0.2 respond.1
  29.2 2.2 %borders.1 = (f32[2,6,3,24,512]{4,3,2,1,0:T(8,128)S(1)}, f32[2,6,3,24,512]{4,3,2,1,0:T(8,128)S(1)}, f32[8,512]{1,0:T(8,128)S(1)}, f32[2,8,24,512]{3,2,1,0:T(8,12...) custom-call(f32[8,24,512]{2,1,0:T(8,128)S(1)} %copy-done, f32[1,3]{1,0:T(1,128)S(1)} %copy-done.4, ...), custom_call_target="tpu_custom_call" | custom-call | tf_op jit(solution)/shard_map/borders/pallas_call | solution.py:839
  31.4 1.6 %write_borders.1 = (f32[1,6,8,24,512]{4,3,2,1,0:T(8,128)}, f32[1,6,8,24,512]{4,3,2,1,0:T(8,128)}, f32[8,128]{1,0:T(8,128)S(1)}) custom-call(f32[1,6,8,24,512]{4,3,2,1,0:T(8,128)} %get-tuple-element.45.fwd, f32[1,6,8,24,512]{4,3,2,1,0:T(8,128)} %get-tuple-element.46.adj, ...), custom_call_target="tpu_custom_call", output_to_operand_aliasing={{0}: (0, {}), {1}: (1, {})} | custom-call | flops 1000000000 | tf_op jit(solution)/shard_map/write_borders/pallas_call | solution.py:852
  33.0 0.9 %collective-permute-done.6.rest_10_ = f32[96,512]{1,0:T(8,128)S(1)} collective-permute-done((f32[96,512]{1,0:T(8,128)S(1)}, f32[96,512]{1,0:T(8,128)S(1)}, u32[]{:S(2)}, u32[]{:S(2)}) %collective-permute-start.6) | collective-permute-done | bytes 196640 | tf_op jit(solution)/shard_map/ppermute | solution.py:721
  33.9 1.1 %last_planes.1 = (f32[4,8,8,72]{3,2,1,0:T(8,128)}, f32[2,7,1,24,512]{4,3,2,1,0:T(8,128)S(1)}) custom-call(f32[8,24,512]{2,1,0:T(8,128)S(1)} %copy-done, f32[1,3]{1,0:T(1,128)S(1)} %copy-done.4, f32[1,3]{1,0:T(1,128)S(1)} %copy-done.5, f32[1,512]{1,0:T(1,128)S(1)} %copy-done.2, f32[1,512]{1,0:T(1,128)S(1)} %copy-done.3, s32[1]{0:T(128)S(6)} %copy.23.rest_4_, ...), custom_call_target="tpu_custom_call" | custom-call | flops 1000000000 | tf_op jit(solution)/shard_map/last_planes/pallas_call | solution.py:861
  35.0 4.6 %all-to-all-start = ((f32[32,8,72]{2,1,0:T(8,128)}), f32[32,8,72]{2,1,0:T(8,128)S(1)}, u32[]{:S(2)}, u32[]{:S(2)}) async-start(f32[32,8,72]{2,1,0:T(8,128)} %bitcast), calls=%async_computation | async-start | bytes 262144 | tf_op jit(solution)/shard_map/all_to_all | solution.py:880
  39.7 0.8 %filter_operands.1 = (f32[64,72]{1,0:T(8,128)S(1)}, f32[64,72]{1,0:T(8,128)S(1)}, f32[64,64]{1,0:T(8,128)S(1)}) custom-call(f32[112,512]{1,0:T(8,128)S(1)} %collective-permute-done.rest_7_.prior_a, f32[112,512]{1,0:T(8,128)S(1)} %collective-permute-done.1.rest_8_.next_a, f32[64,64]{1,0:T(8,128)S(1)} %copy-done.1, s32[1,8]{1,0:T(1,128)S(1)} %copy-done.6, ...), custom_call_target="tpu_custom_call" | custom-call | tf_op jit(solution)/shard_map/filter_operands/pallas_call | solution.py:829
  40.6 0.9 %write_ends.1 = (f32[1,6,8,24,512]{4,3,2,1,0:T(8,128)}, f32[1,6,8,24,512]{4,3,2,1,0:T(8,128)}) custom-call(f32[1,6,8,24,512]{4,3,2,1,0:T(8,128)} %get-tuple-element.49.fwd, f32[1,6,8,24,512]{4,3,2,1,0:T(8,128)} %get-tuple-element.50.adj, f32[2,7,1,24,512]{4,3,2,1,0:T(8,128)S(1)} %get-tuple-element.56.ends), custom_call_target="tpu_custom_call", output_to_operand_aliasing={{0}: (0, {}), {1}: (1, {})} | custom-call | flops 1000000000 | tf_op jit(solution)/shard_map/write_ends/pallas_call | solution.py:869
  41.5 6.0 %all-to-all-done = f32[32,8,72]{2,1,0:T(8,128)S(1)} async-done(((f32[32,8,72]{2,1,0:T(8,128)}), f32[32,8,72]{2,1,0:T(8,128)S(1)}, u32[]{:S(2)}, u32[]{:S(2)}) %all-to-all-start) | async-done | bytes 73760 | tf_op jit(solution)/shard_map/all_to_all | solution.py:880
  47.4 1.6 %project.1 = f32[64,64]{1,0:T(8,128)} custom-call(f32[4,8,8,72]{3,2,1,0:T(8,128)S(1)} %bitcast.2, f32[64,72]{1,0:T(8,128)S(1)} %get-tuple-element.60.padded, f32[64,72]{1,0:T(8,128)S(1)} %get-tuple-element.61.chosen, f32[64,64]{1,0:T(8,128)S(1)} %get-tuple-element.62.weights, s32[1,8]{1,0:T(1,128)S(1)} %copy-done.7), custom_call_target="tpu_custom_call" | custom-call | flops 1000000000 | tf_op jit(solution)/shard_map/project/pallas_call | solution.py:882
  (20 shorter events, 0.0 us)
Async XLA Ops:
  2.1 20.5 %collective-permute-start = (f32[112,512]{1,0:T(8,128)S(1)}, f32[112,512]{1,0:T(8,128)S(1)}, u32[]{:S(2)}, u32[]{:S(2)}) collective-permute-start(f32[112,512]{1,0:T(8,128)S(1)} %get-tuple-element.36), channel_id=1, source_target_pairs={{0,1},{1,2},{2,3},{3,4},{4,5},{5,6},{6,7},{7,0},{8,9},{9,10},{10,1... | collective-permute-start | bytes 688136 | tf_op jit(solution)/shard_map/ppermute | solution.py:721
  5.1 22.2 %collective-permute-start.1 = (f32[112,512]{1,0:T(8,128)S(1)}, f32[112,512]{1,0:T(8,128)S(1)}, u32[]{:S(2)}, u32[]{:S(2)}) collective-permute-start(f32[112,512]{1,0:T(8,128)S(1)} %get-tuple-element.33.rest_6_), channel_id=1, source_target_pairs={{0,7},{1,0},{2,1},{3,2},{4,3},{5,4},{6,5},{7,6},{8,15},{9,8},{10,9... | collective-permute-start | bytes 688136 | tf_op jit(solution)/shard_map/ppermute | solution.py:721
  11.6 17.6 %collective-permute-start.3 = (f32[96,512]{1,0:T(8,128)S(1)}, f32[96,512]{1,0:T(8,128)S(1)}, u32[]{:S(2)}, u32[]{:S(2)}) collective-permute-start(f32[96,512]{1,0:T(8,128)S(1)} %get-tuple-element.43), channel_id=1, source_target_pairs={{0,1},{1,2},{2,3},{3,4},{4,5},{5,6},{6,7},{7,0},{8,9},{9,10},{10,1... | collective-permute-start | bytes 589832 | tf_op jit(solution)/shard_map/ppermute | solution.py:721
  11.7 17.5 %collective-permute-start.4 = (f32[96,512]{1,0:T(8,128)S(1)}, f32[96,512]{1,0:T(8,128)S(1)}, u32[]{:S(2)}, u32[]{:S(2)}) collective-permute-start(f32[96,512]{1,0:T(8,128)S(1)} %get-tuple-element.44), channel_id=1, source_target_pairs={{0,7},{1,0},{2,1},{3,2},{4,3},{5,4},{6,5},{7,6},{8,15},{9,8},{10,9... | collective-permute-start | bytes 589832 | tf_op jit(solution)/shard_map/ppermute | solution.py:721
  16.4 5.6 %copy-start = (f32[8,24,512]{2,1,0:T(8,128)S(1)}, f32[8,24,512]{2,1,0:T(8,128)}, u32[]{:S(2)}) copy-start(f32[8,24,512]{2,1,0:T(8,128)} %inv.7) | copy-start | bytes 1179652
  16.4 5.6 %copy-start.2 = (f32[1,512]{1,0:T(1,128)S(1)}, f32[1,512]{1,0:T(1,128)}, u32[]{:S(2)}) copy-start(f32[1,512]{1,0:T(1,128)} %rest_2_.11) | copy-start | bytes 6148
  16.4 5.7 %copy-start.3 = (f32[1,512]{1,0:T(1,128)S(1)}, f32[1,512]{1,0:T(1,128)}, u32[]{:S(2)}) copy-start(f32[1,512]{1,0:T(1,128)} %rest_3_.11) | copy-start | bytes 6148
  16.4 5.7 %copy-start.4 = (f32[1,3]{1,0:T(1,128)S(1)}, f32[1,3]{1,0:T(1,128)}, u32[]{:S(2)}) copy-start(f32[1,3]{1,0:T(1,128)} %rest_0_.11) | copy-start | bytes 40
  16.4 5.7 %copy-start.5 = (f32[1,3]{1,0:T(1,128)S(1)}, f32[1,3]{1,0:T(1,128)}, u32[]{:S(2)}) copy-start(f32[1,3]{1,0:T(1,128)} %rest_1_.11) | copy-start | bytes 40
  22.5 10.5 %collective-permute-start.5 = (f32[96,512]{1,0:T(8,128)S(1)}, f32[96,512]{1,0:T(8,128)S(1)}, u32[]{:S(2)}, u32[]{:S(2)}) collective-permute-start(f32[96,512]{1,0:T(8,128)S(1)} %get-tuple-element.53), channel_id=1, source_target_pairs={{0,1},{1,2},{2,3},{3,4},{4,5},{5,6},{6,7},{7,0},{8,9},{9,10},{10,1... | collective-permute-start | bytes 589832 | tf_op jit(solution)/shard_map/ppermute | solution.py:721
  22.6 11.3 %collective-permute-start.6 = (f32[96,512]{1,0:T(8,128)S(1)}, f32[96,512]{1,0:T(8,128)S(1)}, u32[]{:S(2)}, u32[]{:S(2)}) collective-permute-start(f32[96,512]{1,0:T(8,128)S(1)} %get-tuple-element.54), channel_id=1, source_target_pairs={{0,7},{1,0},{2,1},{3,2},{4,3},{5,4},{6,5},{7,6},{8,15},{9,8},{10,9... | collective-permute-start | bytes 589832 | tf_op jit(solution)/shard_map/ppermute | solution.py:721
  27.7 1.3 %collective-permute-start.2 = (f32[24,512]{1,0:T(8,128)S(1)}, f32[24,512]{1,0:T(8,128)S(1)}, u32[]{:S(2)}, u32[]{:S(2)}) collective-permute-start(f32[24,512]{1,0:T(8,128)S(1)} %get-tuple-element.38.own), channel_id=1, source_target_pairs={{0,8},{8,0},{16,24},{24,16},{1,9},{9,1},{17,25},{25,17},{2,10},{10... | collective-permute-start | bytes 147464 | tf_op jit(solution)/shard_map/ppermute | solution.py:819
  33.0 6.7 %copy-start.1 = (f32[64,64]{1,0:T(8,128)S(1)}, f32[64,64]{1,0:T(8,128)}, u32[]{:S(2)}) copy-start(f32[64,64]{1,0:T(8,128)} %density.3) | copy-start | bytes 49156
  33.0 6.7 %copy-start.6 = (s32[1,8]{1,0:T(1,128)S(1)}, s32[1,8]{1,0:T(1,128)}, u32[]{:S(2)}) copy-start(s32[1,8]{1,0:T(1,128)} %mask.3) | copy-start | bytes 100
  33.0 6.7 %copy-start.7 = (s32[1,8]{1,0:T(1,128)S(1)}, s32[1,8]{1,0:T(1,128)}, u32[]{:S(2)}) copy-start(s32[1,8]{1,0:T(1,128)} %radius_map.3) | copy-start | bytes 100
  35.0 12.4 %all-to-all-start = ((f32[32,8,72]{2,1,0:T(8,128)}), f32[32,8,72]{2,1,0:T(8,128)S(1)}, u32[]{:S(2)}, u32[]{:S(2)}) async-start(f32[32,8,72]{2,1,0:T(8,128)} %bitcast), calls=%async_computation | async-start | bytes 262144 | tf_op jit(solution)/shard_map/all_to_all | solution.py:880

commit v4 on v3

--- a/solution.py
+++ b/solution.py
@@ -644,26 +644,25 @@
     return jnp.where(keep, pltpu.roll(rows, (-by) % count, 0), 0.0)
 
 
-def weighted(cells, radius):
+def rings(cells):
     tile = cells.shape[1] - 2 * RMAX
     columns = [cells[:, RMAX : RMAX + tile]]
     for a in range(1, RMAX + 1):
         columns.append(
             cells[:, RMAX - a : RMAX - a + tile] + cells[:, RMAX + a : RMAX + a + tile]
         )
-    rings = {}
+    sums = {}
     for a in range(RMAX + 1):
         for b in range(RMAX + 1):
             part = columns[a]
             if b > 0:
                 part = moved(part, b) + moved(part, -b)
             square = a * a + b * b
-            rings[square] = rings[square] + part if square in rings else part
-    total = None
-    for square, part in rings.items():
-        term = jnp.maximum(radius - math.sqrt(square), 0.0) * part
-        total = term if total is None else total + term
-    return total
+            sums[square] = sums[square] + part if square in sums else part
+    return sums.items()
+
+
+RINGS = len({a * a + b * b for a in range(RMAX + 1) for b in range(RMAX + 1)})
 
 
 def by_tile(values, count):
@@ -700,15 +699,24 @@
     )
     scale = step_size / math.sqrt(3 * STEPS * NZ * FREQS)
     chosen[...] = jnp.where(inside, scale * mark, 0.0)
-    weights[...] = weighted(inside.astype(jnp.float32), by_tile(radius_map, width))
-
-
-def project(blocks, padded, chosen, weights, radius_map, projected):
+    radius = by_tile(radius_map, width)
+    total = jnp.zeros((width, tile_rows), jnp.float32)
+    for k, (square, part) in enumerate(rings(inside.astype(jnp.float32))):
+        weight = jnp.maximum(radius - math.sqrt(square), 0.0)
+        weights[k] = jnp.broadcast_to(weight, total.shape)
+        total = total + weight * part
+    total = 1.0 / total
+    for k in range(RINGS):
+        weights[k] = weights[k] * total
+
+
+def project(blocks, padded, chosen, weights, projected):
     freqs, slabs, rows, width = blocks.shape
     gradient = jnp.sum(blocks[...], axis=0).reshape(slabs * rows, width)
     updated = padded[...] + chosen[...] * gradient
-    numerator = weighted(updated, by_tile(radius_map, slabs * rows))
-    filtered = numerator / weights[...]
+    filtered = jnp.zeros(weights.shape[1:], jnp.float32)
+    for k, (_, part) in enumerate(rings(updated)):
+        filtered = filtered + weights[k] * part
     base = math.tanh(sharpness * midpoint)
     value = (base + jnp.tanh(sharpness * (filtered - midpoint))) / (
         base + math.tanh(sharpness * (1.0 - midpoint))
@@ -828,7 +836,7 @@
     )(state, early, halves, other)
     padded, chosen, weights = kernel_call(
         filter_operands,
-        (shaped(width, reach), shaped(width, reach), shaped(width, tile_rows)),
+        (shaped(width, reach), shaped(width, reach), shaped(RINGS, width, tile_rows)),
         [VMEM] * 5,
         (VMEM,) * 3,
         [vmem(reach, width), vmem(8, width)],
@@ -882,11 +890,11 @@
     projected = kernel_call(
         project,
         shaped(tile_rows, width),
-        [VMEM] * 5,
+        [VMEM] * 4,
         VMEM,
         [],
         "project",
-    )(blocks, padded, chosen, weights, radius_map)
+    )(blocks, padded, chosen, weights)
     return (forward_out, adjoint_out, projected)
 
 

time: 49.3 us -> 48.6 us (0.986)
  Pallas kernels: 18.4 us -> 17.8 us
    pallas_call x1, Pallas kernels: 1.59 us -> 0.98 us  [on_device(): kernel_call(project, shaped(tile_rows, width), [VMEM] * 4, VMEM, [], 'pro...]
where the time goes in v4:
time: 48.6 us; the launch traced here: 48.4 us
  starting transfers between devices  20.3 us (42%)
  Pallas kernels  17.8 us (37%)
  waiting for transfers between devices  8.08 us (17%)
  between operations  2.17 us (4%)
    ppermute x6, starting transfers between devices, around(): lax.ppermute(shard, axis, [(i, (i + by) % count) for i in range(count)])  15.6 us
    all_to_all x1, waiting for transfers between devices, on_device(): blocks = lax.all_to_all(blocks, ('freq', 'slab'), 0, 0, tiled=True)  5.95 us
    pallas_call x1, Pallas kernels, on_device(): kernel_call(interior, (state_shape, shaped(rows, 8, NY)), [HBM] * 3 + SOU...  5.6 us
    all_to_all x1, starting transfers between devices, on_device(): blocks = lax.all_to_all(blocks, ('freq', 'slab'), 0, 0, tiled=True)  4.64 us
    pallas_call x1, Pallas kernels, on_device(): kernel_call(borders, (three, three, shaped(rows, NY), shaped(2, 8, *PLANE...  2.16 us
    pallas_call x1, Pallas kernels, on_device(): kernel_call(second_planes, (four, four, shaped(2, 9, *PLANE)), [HBM] * 3...  2.1 us
    pallas_call x1, Pallas kernels, on_device(): kernel_call(write_borders, (field_shape, field_shape, shaped(8, 128)), [H...  1.57 us
    pallas_call x1, Pallas kernels, on_device(): kernel_call(first_planes, (shaped(sent_rows(width), NY),) * 2, [HBM] * 5,...  1.45 us
  transfers between devices with their start and end apart: 8, of which 3 were waited for; matrix products, arithmetic and copies ran while one was open for 0% of the time, Pallas kernels for 29%

profile of v4, /device:TPU:0, one launch (start us, length us, event | category | flops | bytes accessed | tf_op | source)
XLA Modules:
  0.0 48.4 jit_solution(16572928209047985773)
XLA Ops:
  0.6 1.4 %first_planes.1 = (f32[112,512]{1,0:T(8,128)S(1)}, f32[112,512]{1,0:T(8,128)S(1)}) custom-call(f32[1,6,8,24,512]{4,3,2,1,0:T(8,128)} %fwd.5, f32[1,6,8,24,512]{4,3,2,1,0:T(8,128)} %adj.5, f32[8,24,512]{2,1,0:T(8,128)} %inv.7, f32[64,64]{1,0:T(8,128)} %density.3, s32[1,8]{1,0:T(1,128)} %mask.3), custom_call_target="tpu_custom_call" | custom-call | flops 1000000000 | tf_op jit(solution)/shard_map/first_planes/pallas_call | solution.py:766
  2.1 3.0 %collective-permute-start = (f32[112,512]{1,0:T(8,128)S(1)}, f32[112,512]{1,0:T(8,128)S(1)}, u32[]{:S(2)}, u32[]{:S(2)}) collective-permute-start(f32[112,512]{1,0:T(8,128)S(1)} %get-tuple-element.36), channel_id=1, source_target_pairs={{0,1},{1,2},{2,3},{3,4},{4,5},{5,6},{6,7},{7,0},{8,9},{9,10},{10,1... | collective-permute-start | bytes 688136 | tf_op jit(solution)/shard_map/ppermute | solution.py:729
  5.1 3.1 %collective-permute-start.1 = (f32[112,512]{1,0:T(8,128)S(1)}, f32[112,512]{1,0:T(8,128)S(1)}, u32[]{:S(2)}, u32[]{:S(2)}) collective-permute-start(f32[112,512]{1,0:T(8,128)S(1)} %get-tuple-element.33.rest_6_), channel_id=1, source_target_pairs={{0,7},{1,0},{2,1},{3,2},{4,3},{5,4},{6,5},{7,6},{8,15},{9,8},{10,9... | collective-permute-start | bytes 688136 | tf_op jit(solution)/shard_map/ppermute | solution.py:729
  9.5 2.1 %second_planes.1 = (f32[96,512]{1,0:T(8,128)S(1)}, f32[96,512]{1,0:T(8,128)S(1)}, f32[2,9,24,512]{3,2,1,0:T(8,128)S(1)}) custom-call(f32[1,6,8,24,512]{4,3,2,1,0:T(8,128)} %fwd.5, f32[1,6,8,24,512]{4,3,2,1,0:T(8,128)} %adj.5, f32[8,24,512]{2,1,0:T(8,128)} %inv.7, f32[1,3]{1,0:T(1,128)} %rest_0_.11, f32[1,3]{1,0:T(1,128)} %rest_1_.11, f32[1,512]{1,0:T(1,128)} %rest_2_.11, ...), custom_call_target="tpu_custom_call" | custom-call | flops 2000000000 | tf_op jit(solution)/shard_map/second_planes/pallas_call | solution.py:782
  11.6 0.1 collective-permute-start.3
  11.7 4.7 %collective-permute-start.4 = (f32[96,512]{1,0:T(8,128)S(1)}, f32[96,512]{1,0:T(8,128)S(1)}, u32[]{:S(2)}, u32[]{:S(2)}) collective-permute-start(f32[96,512]{1,0:T(8,128)S(1)} %get-tuple-element.44), channel_id=1, source_target_pairs={{0,7},{1,0},{2,1},{3,2},{4,3},{5,4},{6,5},{7,6},{8,15},{9,8},{10,9... | collective-permute-start | bytes 589832 | tf_op jit(solution)/shard_map/ppermute | solution.py:729
  16.4 0.0 copy-start.5
  16.4 5.6 %interior.1 = (f32[2,6,8,24,512]{4,3,2,1,0:T(8,128)S(1)}, f32[8,8,512]{2,1,0:T(8,128)S(1)}) custom-call(f32[1,6,8,24,512]{4,3,2,1,0:T(8,128)} %fwd.5, f32[1,6,8,24,512]{4,3,2,1,0:T(8,128)} %adj.5, f32[8,24,512]{2,1,0:T(8,128)} %inv.7, f32[1,3]{1,0:T(1,128)} %rest_0_.11, f32[1,3]{1,0:T(1,128)} %rest_1_.11, f32[1,512]{1,0:T(1,128)} %rest_2_.11, ...), custom_call_target="tpu_custom_call" | custom-call | flops 8000000000 | tf_op jit(solution)/shard_map/interior/pallas_call | solution.py:799
  22.0 0.4 third_planes.1
  22.5 0.1 collective-permute-start.5
  22.6 4.7 %collective-permute-start.6 = (f32[96,512]{1,0:T(8,128)S(1)}, f32[96,512]{1,0:T(8,128)S(1)}, u32[]{:S(2)}, u32[]{:S(2)}) collective-permute-start(f32[96,512]{1,0:T(8,128)S(1)} %get-tuple-element.54), channel_id=1, source_target_pairs={{0,7},{1,0},{2,1},{3,2},{4,3},{5,4},{6,5},{7,6},{8,15},{9,8},{10,9... | collective-permute-start | bytes 589832 | tf_op jit(solution)/shard_map/ppermute | solution.py:729
  27.3 0.4 step_one.1
  27.7 0.1 collective-permute-start.2
  27.8 1.2 %collective-permute-done.2.other = f32[24,512]{1,0:T(8,128)S(1)} collective-permute-done((f32[24,512]{1,0:T(8,128)S(1)}, f32[24,512]{1,0:T(8,128)S(1)}, u32[]{:S(2)}, u32[]{:S(2)}) %collective-permute-start.2) | collective-permute-done | bytes 49184 | tf_op jit(solution)/shard_map/ppermute | solution.py:827
  29.0 0.2 respond.1
  29.2 2.2 %borders.1 = (f32[2,6,3,24,512]{4,3,2,1,0:T(8,128)S(1)}, f32[2,6,3,24,512]{4,3,2,1,0:T(8,128)S(1)}, f32[8,512]{1,0:T(8,128)S(1)}, f32[2,8,24,512]{3,2,1,0:T(8,12...) custom-call(f32[8,24,512]{2,1,0:T(8,128)S(1)} %copy-done, f32[1,3]{1,0:T(1,128)S(1)} %copy-done.4, ...), custom_call_target="tpu_custom_call" | custom-call | tf_op jit(solution)/shard_map/borders/pallas_call | solution.py:847
  31.4 1.6 %write_borders.1 = (f32[1,6,8,24,512]{4,3,2,1,0:T(8,128)}, f32[1,6,8,24,512]{4,3,2,1,0:T(8,128)}, f32[8,128]{1,0:T(8,128)S(1)}) custom-call(f32[1,6,8,24,512]{4,3,2,1,0:T(8,128)} %get-tuple-element.45.fwd, f32[1,6,8,24,512]{4,3,2,1,0:T(8,128)} %get-tuple-element.46.adj, ...), custom_call_target="tpu_custom_call", output_to_operand_aliasing={{0}: (0, {}), {1}: (1, {})} | custom-call | flops 1000000000 | tf_op jit(solution)/shard_map/write_borders/pallas_call | solution.py:860
  33.0 0.9 %collective-permute-done.6.rest_10_ = f32[96,512]{1,0:T(8,128)S(1)} collective-permute-done((f32[96,512]{1,0:T(8,128)S(1)}, f32[96,512]{1,0:T(8,128)S(1)}, u32[]{:S(2)}, u32[]{:S(2)}) %collective-permute-start.6) | collective-permute-done | bytes 196640 | tf_op jit(solution)/shard_map/ppermute | solution.py:729
  33.9 1.1 %last_planes.1 = (f32[4,8,8,72]{3,2,1,0:T(8,128)}, f32[2,7,1,24,512]{4,3,2,1,0:T(8,128)S(1)}) custom-call(f32[8,24,512]{2,1,0:T(8,128)S(1)} %copy-done, f32[1,3]{1,0:T(1,128)S(1)} %copy-done.4, f32[1,3]{1,0:T(1,128)S(1)} %copy-done.5, f32[1,512]{1,0:T(1,128)S(1)} %copy-done.2, f32[1,512]{1,0:T(1,128)S(1)} %copy-done.3, s32[1]{0:T(128)S(6)} %copy.23.rest_4_, ...), custom_call_target="tpu_custom_call" | custom-call | flops 1000000000 | tf_op jit(solution)/shard_map/last_planes/pallas_call | solution.py:869
  35.0 4.6 %all-to-all-start = ((f32[32,8,72]{2,1,0:T(8,128)}), f32[32,8,72]{2,1,0:T(8,128)S(1)}, u32[]{:S(2)}, u32[]{:S(2)}) async-start(f32[32,8,72]{2,1,0:T(8,128)} %bitcast), calls=%async_computation | async-start | bytes 262144 | tf_op jit(solution)/shard_map/all_to_all | solution.py:888
  39.7 0.8 %filter_operands.1 = (f32[64,72]{1,0:T(8,128)S(1)}, f32[64,72]{1,0:T(8,128)S(1)}, f32[15,64,64]{2,1,0:T(8,128)S(1)}) custom-call(f32[112,512]{1,0:T(8,128)S(1)} %collective-permute-done.rest_7_.prior_a, f32[112,512]{1,0:T(8,128)S(1)} %collective-permute-done.1.rest_8_.next_a, f32[64,64]{1,0:T(8,128)S(1)} %copy-done.1, s32[1,8]{1,0:T(1,128)S(1)} %copy-done.6, ...), custom_call_target="tpu_custom_call" | custom-call | tf_op jit(solution)/shard_map/filter_operands/pallas_call | solution.py:837
  40.6 0.9 %write_ends.1 = (f32[1,6,8,24,512]{4,3,2,1,0:T(8,128)}, f32[1,6,8,24,512]{4,3,2,1,0:T(8,128)}) custom-call(f32[1,6,8,24,512]{4,3,2,1,0:T(8,128)} %get-tuple-element.49.fwd, f32[1,6,8,24,512]{4,3,2,1,0:T(8,128)} %get-tuple-element.50.adj, f32[2,7,1,24,512]{4,3,2,1,0:T(8,128)S(1)} %get-tuple-element.56.ends), custom_call_target="tpu_custom_call", output_to_operand_aliasing={{0}: (0, {}), {1}: (1, {})} | custom-call | flops 1000000000 | tf_op jit(solution)/shard_map/write_ends/pallas_call | solution.py:877
  41.5 6.0 %all-to-all-done = f32[32,8,72]{2,1,0:T(8,128)S(1)} async-done(((f32[32,8,72]{2,1,0:T(8,128)}), f32[32,8,72]{2,1,0:T(8,128)S(1)}, u32[]{:S(2)}, u32[]{:S(2)}) %all-to-all-start) | async-done | bytes 73760 | tf_op jit(solution)/shard_map/all_to_all | solution.py:888
  47.4 1.0 %project.1 = f32[64,64]{1,0:T(8,128)} custom-call(f32[4,8,8,72]{3,2,1,0:T(8,128)S(1)} %bitcast.2, f32[64,72]{1,0:T(8,128)S(1)} %get-tuple-element.60.padded, f32[64,72]{1,0:T(8,128)S(1)} %get-tuple-element.61.chosen, f32[15,64,64]{2,1,0:T(8,128)S(1)} %get-tuple-element.62.weights), custom_call_target="tpu_custom_call" | custom-call | flops 1000000000 | tf_op jit(solution)/shard_map/project/pallas_call | solution.py:890
  (20 shorter events, 0.0 us)
Async XLA Ops:
  2.1 20.5 %collective-permute-start = (f32[112,512]{1,0:T(8,128)S(1)}, f32[112,512]{1,0:T(8,128)S(1)}, u32[]{:S(2)}, u32[]{:S(2)}) collective-permute-start(f32[112,512]{1,0:T(8,128)S(1)} %get-tuple-element.36), channel_id=1, source_target_pairs={{0,1},{1,2},{2,3},{3,4},{4,5},{5,6},{6,7},{7,0},{8,9},{9,10},{10,1... | collective-permute-start | bytes 688136 | tf_op jit(solution)/shard_map/ppermute | solution.py:729
  5.1 22.2 %collective-permute-start.1 = (f32[112,512]{1,0:T(8,128)S(1)}, f32[112,512]{1,0:T(8,128)S(1)}, u32[]{:S(2)}, u32[]{:S(2)}) collective-permute-start(f32[112,512]{1,0:T(8,128)S(1)} %get-tuple-element.33.rest_6_), channel_id=1, source_target_pairs={{0,7},{1,0},{2,1},{3,2},{4,3},{5,4},{6,5},{7,6},{8,15},{9,8},{10,9... | collective-permute-start | bytes 688136 | tf_op jit(solution)/shard_map/ppermute | solution.py:729
  11.6 17.6 %collective-permute-start.3 = (f32[96,512]{1,0:T(8,128)S(1)}, f32[96,512]{1,0:T(8,128)S(1)}, u32[]{:S(2)}, u32[]{:S(2)}) collective-permute-start(f32[96,512]{1,0:T(8,128)S(1)} %get-tuple-element.43), channel_id=1, source_target_pairs={{0,1},{1,2},{2,3},{3,4},{4,5},{5,6},{6,7},{7,0},{8,9},{9,10},{10,1... | collective-permute-start | bytes 589832 | tf_op jit(solution)/shard_map/ppermute | solution.py:729
  11.7 17.5 %collective-permute-start.4 = (f32[96,512]{1,0:T(8,128)S(1)}, f32[96,512]{1,0:T(8,128)S(1)}, u32[]{:S(2)}, u32[]{:S(2)}) collective-permute-start(f32[96,512]{1,0:T(8,128)S(1)} %get-tuple-element.44), channel_id=1, source_target_pairs={{0,7},{1,0},{2,1},{3,2},{4,3},{5,4},{6,5},{7,6},{8,15},{9,8},{10,9... | collective-permute-start | bytes 589832 | tf_op jit(solution)/shard_map/ppermute | solution.py:729
  16.4 5.6 %copy-start = (f32[8,24,512]{2,1,0:T(8,128)S(1)}, f32[8,24,512]{2,1,0:T(8,128)}, u32[]{:S(2)}) copy-start(f32[8,24,512]{2,1,0:T(8,128)} %inv.7) | copy-start | bytes 1179652
  16.4 5.6 %copy-start.2 = (f32[1,512]{1,0:T(1,128)S(1)}, f32[1,512]{1,0:T(1,128)}, u32[]{:S(2)}) copy-start(f32[1,512]{1,0:T(1,128)} %rest_2_.11) | copy-start | bytes 6148
  16.4 5.7 %copy-start.3 = (f32[1,512]{1,0:T(1,128)S(1)}, f32[1,512]{1,0:T(1,128)}, u32[]{:S(2)}) copy-start(f32[1,512]{1,0:T(1,128)} %rest_3_.11) | copy-start | bytes 6148
  16.4 5.7 %copy-start.4 = (f32[1,3]{1,0:T(1,128)S(1)}, f32[1,3]{1,0:T(1,128)}, u32[]{:S(2)}) copy-start(f32[1,3]{1,0:T(1,128)} %rest_0_.11) | copy-start | bytes 40
  16.4 5.7 %copy-start.5 = (f32[1,3]{1,0:T(1,128)S(1)}, f32[1,3]{1,0:T(1,128)}, u32[]{:S(2)}) copy-start(f32[1,3]{1,0:T(1,128)} %rest_1_.11) | copy-start | bytes 40
  22.5 10.5 %collective-permute-start.5 = (f32[96,512]{1,0:T(8,128)S(1)}, f32[96,512]{1,0:T(8,128)S(1)}, u32[]{:S(2)}, u32[]{:S(2)}) collective-permute-start(f32[96,512]{1,0:T(8,128)S(1)} %get-tuple-element.53), channel_id=1, source_target_pairs={{0,1},{1,2},{2,3},{3,4},{4,5},{5,6},{6,7},{7,0},{8,9},{9,10},{10,1... | collective-permute-start | bytes 589832 | tf_op jit(solution)/shard_map/ppermute | solution.py:729
  22.6 11.3 %collective-permute-start.6 = (f32[96,512]{1,0:T(8,128)S(1)}, f32[96,512]{1,0:T(8,128)S(1)}, u32[]{:S(2)}, u32[]{:S(2)}) collective-permute-start(f32[96,512]{1,0:T(8,128)S(1)} %get-tuple-element.54), channel_id=1, source_target_pairs={{0,7},{1,0},{2,1},{3,2},{4,3},{5,4},{6,5},{7,6},{8,15},{9,8},{10,9... | collective-permute-start | bytes 589832 | tf_op jit(solution)/shard_map/ppermute | solution.py:729
  27.7 1.3 %collective-permute-start.2 = (f32[24,512]{1,0:T(8,128)S(1)}, f32[24,512]{1,0:T(8,128)S(1)}, u32[]{:S(2)}, u32[]{:S(2)}) collective-permute-start(f32[24,512]{1,0:T(8,128)S(1)} %get-tuple-element.38.own), channel_id=1, source_target_pairs={{0,8},{8,0},{16,24},{24,16},{1,9},{9,1},{17,25},{25,17},{2,10},{10... | collective-permute-start | bytes 147464 | tf_op jit(solution)/shard_map/ppermute | solution.py:827
  33.0 6.7 %copy-start.1 = (f32[64,64]{1,0:T(8,128)S(1)}, f32[64,64]{1,0:T(8,128)}, u32[]{:S(2)}) copy-start(f32[64,64]{1,0:T(8,128)} %density.3) | copy-start | bytes 49156
  33.0 6.7 %copy-start.6 = (s32[1,8]{1,0:T(1,128)S(1)}, s32[1,8]{1,0:T(1,128)}, u32[]{:S(2)}) copy-start(s32[1,8]{1,0:T(1,128)} %mask.3) | copy-start | bytes 100
  33.0 6.7 %copy-start.7 = (s32[1,8]{1,0:T(1,128)S(1)}, s32[1,8]{1,0:T(1,128)}, u32[]{:S(2)}) copy-start(s32[1,8]{1,0:T(1,128)} %radius_map.1) | copy-start | bytes 100
  35.0 12.4 %all-to-all-start = ((f32[32,8,72]{2,1,0:T(8,128)}), f32[32,8,72]{2,1,0:T(8,128)S(1)}, u32[]{:S(2)}, u32[]{:S(2)}) async-start(f32[32,8,72]{2,1,0:T(8,128)} %bitcast), calls=%async_computation | async-start | bytes 262144 | tf_op jit(solution)/shard_map/all_to_all | solution.py:888

commit v5 on v4

--- a/solution.py
+++ b/solution.py
@@ -24,20 +24,17 @@
 HBM = pl.BlockSpec(memory_space=pltpu.HBM)
 ANY = pl.BlockSpec(memory_space=pl.ANY)
 GRANT = 8 * 1024 * 1024
-HALF = NZ // 2
-HALO = 4 * NZ + HALF
-
-
-def mark_at(width):
-    return (HALO, width) if 2 * width <= NY else (HALO + RMAX, 0)
+PART = NZ // FREQS
+HALO = 4 * NZ + PART
+
+
+def slot_at(index, width):
+    beside = NY // width
+    return (pl.ds(HALO + index // beside, 1), pl.ds(index % beside * width, width))
 
 
 def sent_rows(width):
-    return -(-(max(HALO + RMAX, mark_at(width)[0] + 1)) // 8) * 8
-
-
-def second_core():
-    return lax.rem(lax.axis_index("freq"), 2) == 1
+    return -(-(HALO + RMAX // (NY // width) + 1) // 8) * 8
 
 
 def neighbour(plane, axis, by):
@@ -202,14 +199,17 @@
     spread = jnp.zeros((1, width), jnp.float32)
     for k in range(mask.shape[1]):
         spread = jnp.where(at == k, chosen[:, k : k + 1].astype(jnp.float32), spread)
-    mark_row, mark_lane = mark_at(width)
-    tail = to_next.shape[0] - HALO
+    rest = pl.ds(4 * NZ, to_next.shape[0] - 4 * NZ)
+    group = lax.axis_index("freq")
     for side, (sent, first) in enumerate(((to_prior, 0), (to_next, density.shape[0] - RMAX))):
-        half = jnp.where(second_core(), inv[side, HALF:, :], inv[side, :HALF, :])
-        sent[pl.ds(4 * NZ, HALF), :] = half
-        sent[pl.ds(HALO, tail), :] = jnp.zeros((tail, NY), jnp.float32)
-        sent[pl.ds(HALO, RMAX), pl.ds(0, width)] = cells[pl.ds(first, RMAX), :]
-        sent[pl.ds(mark_row, 1), pl.ds(mark_lane, width)] = spread
+        part = inv[side, :PART, :]
+        for k in range(1, FREQS):
+            part = jnp.where(group == k, inv[side, k * PART : (k + 1) * PART, :], part)
+        sent[rest, :] = jnp.zeros((to_next.shape[0] - 4 * NZ, NY), jnp.float32)
+        sent[pl.ds(4 * NZ, PART), :] = part
+        for k in range(RMAX):
+            sent[slot_at(k, width)] = cells[pl.ds(first + k, 1), :]
+        sent[slot_at(RMAX, width)] = spread
     for run in range(2):
         copies[run].wait()
         planes = [rows_in[run, k] for k in range(6)]
@@ -369,12 +369,11 @@
     ]
 
 
-def respond(before, early, own, other, resp, scaled):
-    second = second_core()
+def respond(before, early, parts, resp, scaled):
     for side, flag in enumerate(flags()):
-        mine, theirs = (ref[pl.ds(side * HALF, HALF), :] for ref in (own, other))
-        scaled[side, pl.ds(0, HALF), :] = courant * flag * jnp.where(second, theirs, mine)
-        scaled[side, pl.ds(HALF, HALF), :] = courant * flag * jnp.where(second, mine, theirs)
+        for k in range(FREQS):
+            part = parts[k, pl.ds(side * PART, PART), :]
+            scaled[side, pl.ds(k * PART, PART), :] = courant * flag * part
     flagged = courant * flags()[0]
 
     def one_run(run, carry):
@@ -483,9 +482,10 @@
 
 
 def step_one(inv, *rest):
-    given, (before, prior_a, next_a, early, halves, share) = rest[:6], rest[6:]
+    given, (before, prior_a, next_a, early, parts, share) = rest[:6], rest[6:]
+    parts[...] = jnp.zeros_like(parts)
     for side, ref in enumerate((prior_a, next_a)):
-        halves[pl.ds(side * HALF, HALF), :] = ref[pl.ds(4 * NZ, HALF), :]
+        parts[pl.ds(side * PART, PART), :] = ref[pl.ds(4 * NZ, PART), :]
 
     def one_run(run, carry):
         state = State(lambda k, x: (before, x), lambda k, x: (early, min(x, 1)), ())
@@ -498,7 +498,7 @@
 
 
 def borders(inv, *rest):
-    given, (before, early, resp_in, scaled, share, ends, prior_b, next_b) = rest[:6], rest[6:14]
+    given, (before, early, resp_in, scaled, share, ends, next_b, prior_b) = rest[:6], rest[6:14]
     kept, inner, summed, waiting, fwd_out, adj_out, resp, total, sems = rest[14:]
     rows = inv.shape[0]
     last = rows - 1
@@ -679,14 +679,13 @@
 ):
     tile_rows, width = density.shape
     reach = padded.shape[1]
-    above, below = (ref[pl.ds(HALO, RMAX), :] for ref in (prior_a, next_a))
-    mark_row, mark_lane = mark_at(width)
-    rows_of[pl.ds(0, RMAX), :] = above[:, :width]
+    for side, (ref, first) in enumerate(((prior_a, 0), (next_a, RMAX + tile_rows))):
+        for k in range(RMAX):
+            rows_of[pl.ds(first + k, 1), :] = ref[slot_at(k, width)]
     rows_of[pl.ds(RMAX, tile_rows), :] = density[...]
-    rows_of[pl.ds(RMAX + tile_rows, RMAX), :] = below[:, :width]
     marks_of[...] = jnp.zeros_like(marks_of)
     for side, ref in enumerate((prior_a, next_a)):
-        marks_of[pl.ds(side, 1), :] = ref[pl.ds(mark_row, 1), pl.ds(mark_lane, width)]
+        marks_of[pl.ds(side, 1), :] = ref[slot_at(RMAX, width)]
     sides = marks_of[...].T
     first = lax.axis_index("slab") * tile_rows - RMAX
     at = lax.broadcasted_iota(jnp.int32, (width, reach), 1)
@@ -815,25 +814,25 @@
     )(inverse_permittivity, *waves, *planes, state, own)
     prior_c = around(to_next, "slab", 1)
     next_c = around(to_prior, "slab", -1)
-    early, halves, ends = kernel_call(
+    early, parts, ends = kernel_call(
         step_one,
-        (shaped(2, 6, 2, *PLANE), shaped(*PLANE), shaped(2, 8, NY)),
+        (shaped(2, 6, 2, *PLANE), shaped(-(-2 * PART // 8) * 8, NY), shaped(2, 8, NY)),
         [VMEM] + SOURCE_VALUES + [VMEM] * 3,
         (VMEM,) * 3,
         [],
         "step_one",
         micros=0,
     )(inverse_permittivity, *waves, *planes, state, prior_a, next_a)
-    other = lax.ppermute(halves, "freq", [(i, i ^ 1) for i in range(freqs)])
+    parts = lax.all_gather(parts, "freq")
     resp, scaled = kernel_call(
         respond,
         (shaped(2, 8, *PLANE), shaped(2, *PLANE)),
-        [VMEM] * 4,
+        [VMEM] * 3,
         (VMEM,) * 2,
         [],
         "respond",
         micros=0,
-    )(state, early, halves, other)
+    )(state, early, parts)
     padded, chosen, weights = kernel_call(
         filter_operands,
         (shaped(width, reach), shaped(width, reach), shaped(RINGS, width, tile_rows)),
@@ -855,7 +854,7 @@
         grant=2 * GRANT,
     )(
         inverse_permittivity, *waves, *planes, state, early, resp, scaled, share, ends,
-        prior_b, next_b,
+        next_b, prior_b,
     )
     forward_part, adjoint_part, done = kernel_call(
         write_borders,

time: 48.6 us -> 47.9 us (0.986)
  blocking collectives: 0 us -> 5.43 us
  starting transfers between devices: 20.3 us -> 16.3 us
  waiting for transfers between devices: 8.08 us -> 5.4 us
  Pallas kernels: 17.8 us -> 18.3 us
    all_gather x0 -> x1, blocking collectives: none -> 5.43 us  [on_device(): parts = lax.all_gather(parts, 'freq')]
    ppermute x6, starting transfers between devices: 15.6 us -> 13.4 us  [around(): lax.ppermute(shard, axis, [(i, (i + by) % count) for i in range(count)])]
    all_to_all x1, starting transfers between devices: 4.64 us -> 2.93 us  [on_device(): blocks = lax.all_to_all(blocks, ('freq', 'slab'), 0, 0, tiled=True)]
    ppermute x1 -> x0, waiting for transfers between devices: 1.22 us -> none  [on_device(): other = lax.ppermute(halves, 'freq', [(i, i ^ 1) for i in range(freqs)])]
    ppermute x6, waiting for transfers between devices: 0.91 us -> 0.02 us  [around(): lax.ppermute(shard, axis, [(i, (i + by) % count) for i in range(count)])]
    all_to_all x1, waiting for transfers between devices: 5.95 us -> 5.38 us  [on_device(): blocks = lax.all_to_all(blocks, ('freq', 'slab'), 0, 0, tiled=True)]
    pallas_call x1, Pallas kernels: 0.85 us -> 1.42 us  [on_device(): kernel_call(filter_operands, (shaped(width, reach), shaped(width, reach),...]
  transfers between devices with their start and end apart: 8 -> 7, of which waited for: 3 -> 1; matrix products, arithmetic and copies ran while one was open for 0% -> 0% of each run, Pallas kernels for 29% -> 31%
where the time goes in v5:
time: 47.9 us; the launch traced here: 47.6 us
  Pallas kernels  18.3 us (38%)
  starting transfers between devices  16.3 us (34%)
  blocking collectives  5.43 us (11%)
  waiting for transfers between devices  5.4 us (11%)
  between operations  2.15 us (4%)
    ppermute x6, starting transfers between devices, around(): lax.ppermute(shard, axis, [(i, (i + by) % count) for i in range(count)])  13.4 us
    pallas_call x1, Pallas kernels, on_device(): kernel_call(interior, (state_shape, shaped(rows, 8, NY)), [HBM] * 3 + SOU...  5.6 us
    all_gather x1, blocking collectives, on_device(): parts = lax.all_gather(parts, 'freq')  5.43 us
    all_to_all x1, waiting for transfers between devices, on_device(): blocks = lax.all_to_all(blocks, ('freq', 'slab'), 0, 0, tiled=True)  5.38 us
    all_to_all x1, starting transfers between devices, on_device(): blocks = lax.all_to_all(blocks, ('freq', 'slab'), 0, 0, tiled=True)  2.93 us
    pallas_call x1, Pallas kernels, on_device(): kernel_call(borders, (three, three, shaped(rows, NY), shaped(2, 8, *PLANE...  2.16 us
    pallas_call x1, Pallas kernels, on_device(): kernel_call(second_planes, (four, four, shaped(2, 9, *PLANE)), [HBM] * 3...  2.1 us
    pallas_call x1, Pallas kernels, on_device(): kernel_call(write_borders, (field_shape, field_shape, shaped(8, 128)), [H...  1.57 us
  transfers between devices with their start and end apart: 7, of which 1 were waited for; matrix products, arithmetic and copies ran while one was open for 0% of the time, Pallas kernels for 31%

profile of v5, /device:TPU:0, one launch (start us, length us, event | category | flops | bytes accessed | tf_op | source)
XLA Modules:
  0.0 47.6 jit_solution(10660889838637017019)
XLA Ops:
  0.6 1.4 %first_planes.1 = (f32[104,512]{1,0:T(8,128)S(1)}, f32[104,512]{1,0:T(8,128)S(1)}) custom-call(f32[1,6,8,24,512]{4,3,2,1,0:T(8,128)} %fwd.5, f32[1,6,8,24,512]{4,3,2,1,0:T(8,128)} %adj.5, f32[8,24,512]{2,1,0:T(8,128)} %inv.7, f32[64,64]{1,0:T(8,128)} %density.3, s32[1,8]{1,0:T(1,128)} %mask.3), custom_call_target="tpu_custom_call" | custom-call | flops 1000000000 | tf_op jit(solution)/shard_map/first_planes/pallas_call | solution.py:765
  2.0 3.0 %collective-permute-start = (f32[104,512]{1,0:T(8,128)S(1)}, f32[104,512]{1,0:T(8,128)S(1)}, u32[]{:S(2)}, u32[]{:S(2)}) collective-permute-start(f32[104,512]{1,0:T(8,128)S(1)} %get-tuple-element.36), channel_id=1, source_target_pairs={{0,1},{1,2},{2,3},{3,4},{4,5},{5,6},{6,7},{7,0},{8,9},{9,10},{10,1... | collective-permute-start | bytes 638984 | tf_op jit(solution)/shard_map/ppermute | solution.py:728
  5.0 3.1 %collective-permute-start.1 = (f32[104,512]{1,0:T(8,128)S(1)}, f32[104,512]{1,0:T(8,128)S(1)}, u32[]{:S(2)}, u32[]{:S(2)}) collective-permute-start(f32[104,512]{1,0:T(8,128)S(1)} %get-tuple-element.33.rest_6_), channel_id=1, source_target_pairs={{0,7},{1,0},{2,1},{3,2},{4,3},{5,4},{6,5},{7,6},{8,15},{9,8},{10,9... | collective-permute-start | bytes 638984 | tf_op jit(solution)/shard_map/ppermute | solution.py:728
  9.4 2.1 %second_planes.1 = (f32[96,512]{1,0:T(8,128)S(1)}, f32[96,512]{1,0:T(8,128)S(1)}, f32[2,9,24,512]{3,2,1,0:T(8,128)S(1)}) custom-call(f32[1,6,8,24,512]{4,3,2,1,0:T(8,128)} %fwd.5, f32[1,6,8,24,512]{4,3,2,1,0:T(8,128)} %adj.5, f32[8,24,512]{2,1,0:T(8,128)} %inv.7, f32[1,3]{1,0:T(1,128)} %rest_0_.11, f32[1,3]{1,0:T(1,128)} %rest_1_.11, f32[1,512]{1,0:T(1,128)} %rest_2_.11, ...), custom_call_target="tpu_custom_call" | custom-call | flops 2000000000 | tf_op jit(solution)/shard_map/second_planes/pallas_call | solution.py:781
  11.5 2.0 %collective-permute-start.2 = (f32[96,512]{1,0:T(8,128)S(1)}, f32[96,512]{1,0:T(8,128)S(1)}, u32[]{:S(2)}, u32[]{:S(2)}) collective-permute-start(f32[96,512]{1,0:T(8,128)S(1)} %get-tuple-element.43), channel_id=1, source_target_pairs={{0,7},{1,0},{2,1},{3,2},{4,3},{5,4},{6,5},{7,6},{8,15},{9,8},{10,9... | collective-permute-start | bytes 589832 | tf_op jit(solution)/shard_map/ppermute | solution.py:728
  13.5 0.1 collective-permute-start.3
  13.6 0.0 copy-start.5
  13.6 5.6 %interior.1 = (f32[2,6,8,24,512]{4,3,2,1,0:T(8,128)S(1)}, f32[8,8,512]{2,1,0:T(8,128)S(1)}) custom-call(f32[1,6,8,24,512]{4,3,2,1,0:T(8,128)} %fwd.5, f32[1,6,8,24,512]{4,3,2,1,0:T(8,128)} %adj.5, f32[8,24,512]{2,1,0:T(8,128)} %inv.7, f32[1,3]{1,0:T(1,128)} %rest_0_.11, f32[1,3]{1,0:T(1,128)} %rest_1_.11, f32[1,512]{1,0:T(1,128)} %rest_2_.11, ...), custom_call_target="tpu_custom_call" | custom-call | flops 8000000000 | tf_op jit(solution)/shard_map/interior/pallas_call | solution.py:798
  19.3 0.4 third_planes.1
  19.7 0.1 collective-permute-start.4
  19.8 5.2 %collective-permute-start.5 = (f32[96,512]{1,0:T(8,128)S(1)}, f32[96,512]{1,0:T(8,128)S(1)}, u32[]{:S(2)}, u32[]{:S(2)}) collective-permute-start(f32[96,512]{1,0:T(8,128)S(1)} %get-tuple-element.54), channel_id=1, source_target_pairs={{0,7},{1,0},{2,1},{3,2},{4,3},{5,4},{6,5},{7,6},{8,15},{9,8},{10,9... | collective-permute-start | bytes 589832 | tf_op jit(solution)/shard_map/ppermute | solution.py:728
  25.0 0.4 step_one.1
  25.4 5.4 %all-gather = f32[64,512]{1,0:T(8,128)S(1)} all-gather(f32[16,512]{1,0:T(8,128)S(1)} %get-tuple-element.38), channel_id=2, replica_groups=mesh['freq'=4,'slab'=8] {'freq'}, dimensions={0}, use_global_device_ids=true | all-gather | bytes 163840 | tf_op jit(solution)/shard_map/all_gather | solution.py:826
  30.8 0.2 respond.1
  31.0 2.2 %borders.1 = (f32[2,6,3,24,512]{4,3,2,1,0:T(8,128)S(1)}, f32[2,6,3,24,512]{4,3,2,1,0:T(8,128)S(1)}, f32[8,512]{1,0:T(8,128)S(1)}, f32[2,8,24,512]{3,2,1,0:T(8,12...) custom-call(f32[8,24,512]{2,1,0:T(8,128)S(1)} %copy-done, f32[1,3]{1,0:T(1,128)S(1)} %copy-done.4, ...), custom_call_target="tpu_custom_call" | custom-call | tf_op jit(solution)/shard_map/borders/pallas_call | solution.py:846
  33.2 1.6 %write_borders.1 = (f32[1,6,8,24,512]{4,3,2,1,0:T(8,128)}, f32[1,6,8,24,512]{4,3,2,1,0:T(8,128)}, f32[8,128]{1,0:T(8,128)S(1)}) custom-call(f32[1,6,8,24,512]{4,3,2,1,0:T(8,128)} %get-tuple-element.45.fwd, f32[1,6,8,24,512]{4,3,2,1,0:T(8,128)} %get-tuple-element.46.adj, ...), custom_call_target="tpu_custom_call", output_to_operand_aliasing={{0}: (0, {}), {1}: (1, {})} | custom-call | flops 1000000000 | tf_op jit(solution)/shard_map/write_borders/pallas_call | solution.py:859
  34.8 0.0 copy-start.1
  34.8 0.0 copy-start.6
  34.8 1.1 %last_planes.1 = (f32[4,8,8,72]{3,2,1,0:T(8,128)}, f32[2,7,1,24,512]{4,3,2,1,0:T(8,128)S(1)}) custom-call(f32[8,24,512]{2,1,0:T(8,128)S(1)} %copy-done, f32[1,3]{1,0:T(1,128)S(1)} %copy-done.4, f32[1,3]{1,0:T(1,128)S(1)} %copy-done.5, f32[1,512]{1,0:T(1,128)S(1)} %copy-done.2, f32[1,512]{1,0:T(1,128)S(1)} %copy-done.3, s32[1]{0:T(128)S(6)} %copy.23.rest_4_, ...), custom_call_target="tpu_custom_call" | custom-call | flops 1000000000 | tf_op jit(solution)/shard_map/last_planes/pallas_call | solution.py:868
  36.0 2.9 %all-to-all-start = ((f32[32,8,72]{2,1,0:T(8,128)}), f32[32,8,72]{2,1,0:T(8,128)S(1)}, u32[]{:S(2)}, u32[]{:S(2)}) async-start(f32[32,8,72]{2,1,0:T(8,128)} %bitcast.1), calls=%async_computation | async-start | bytes 262144 | tf_op jit(solution)/shard_map/all_to_all | solution.py:887
  39.0 1.4 %filter_operands.1 = (f32[64,72]{1,0:T(8,128)S(1)}, f32[64,72]{1,0:T(8,128)S(1)}, f32[15,64,64]{2,1,0:T(8,128)S(1)}) custom-call(f32[104,512]{1,0:T(8,128)S(1)} %collective-permute-done.rest_7_.prior_a, f32[104,512]{1,0:T(8,128)S(1)} %collective-permute-done.1.rest_8_.next_a, f32[64,64]{1,0:T(8,128)S(1)} %copy-done.1, s32[1,8]{1,0:T(1,128)S(1)} %copy-done.6, ...), custom_call_target="tpu_custom_call" | custom-call | tf_op jit(solution)/shard_map/filter_operands/pallas_call | solution.py:836
  40.4 0.9 %write_ends.1 = (f32[1,6,8,24,512]{4,3,2,1,0:T(8,128)}, f32[1,6,8,24,512]{4,3,2,1,0:T(8,128)}) custom-call(f32[1,6,8,24,512]{4,3,2,1,0:T(8,128)} %get-tuple-element.49.fwd, f32[1,6,8,24,512]{4,3,2,1,0:T(8,128)} %get-tuple-element.50.adj, f32[2,7,1,24,512]{4,3,2,1,0:T(8,128)S(1)} %get-tuple-element.56.ends), custom_call_target="tpu_custom_call", output_to_operand_aliasing={{0}: (0, {}), {1}: (1, {})} | custom-call | flops 1000000000 | tf_op jit(solution)/shard_map/write_ends/pallas_call | solution.py:876
  41.3 5.4 %all-to-all-done = f32[32,8,72]{2,1,0:T(8,128)S(1)} async-done(((f32[32,8,72]{2,1,0:T(8,128)}), f32[32,8,72]{2,1,0:T(8,128)S(1)}, u32[]{:S(2)}, u32[]{:S(2)}) %all-to-all-start) | async-done | bytes 73760 | tf_op jit(solution)/shard_map/all_to_all | solution.py:887
  46.7 1.0 %project.1 = f32[64,64]{1,0:T(8,128)} custom-call(f32[4,8,8,72]{3,2,1,0:T(8,128)S(1)} %bitcast.4, f32[64,72]{1,0:T(8,128)S(1)} %get-tuple-element.60.padded, f32[64,72]{1,0:T(8,128)S(1)} %get-tuple-element.61.chosen, f32[15,64,64]{2,1,0:T(8,128)S(1)} %get-tuple-element.62.weights), custom_call_target="tpu_custom_call" | custom-call | flops 1000000000 | tf_op jit(solution)/shard_map/project/pallas_call | solution.py:889
  (19 shorter events, 0.0 us)
Async XLA Ops:
  2.0 17.8 %collective-permute-start = (f32[104,512]{1,0:T(8,128)S(1)}, f32[104,512]{1,0:T(8,128)S(1)}, u32[]{:S(2)}, u32[]{:S(2)}) collective-permute-start(f32[104,512]{1,0:T(8,128)S(1)} %get-tuple-element.36), channel_id=1, source_target_pairs={{0,1},{1,2},{2,3},{3,4},{4,5},{5,6},{6,7},{7,0},{8,9},{9,10},{10,1... | collective-permute-start | bytes 638984 | tf_op jit(solution)/shard_map/ppermute | solution.py:728
  5.0 20.0 %collective-permute-start.1 = (f32[104,512]{1,0:T(8,128)S(1)}, f32[104,512]{1,0:T(8,128)S(1)}, u32[]{:S(2)}, u32[]{:S(2)}) collective-permute-start(f32[104,512]{1,0:T(8,128)S(1)} %get-tuple-element.33.rest_6_), channel_id=1, source_target_pairs={{0,7},{1,0},{2,1},{3,2},{4,3},{5,4},{6,5},{7,6},{8,15},{9,8},{10,9... | collective-permute-start | bytes 638984 | tf_op jit(solution)/shard_map/ppermute | solution.py:728
  11.5 19.5 %collective-permute-start.2 = (f32[96,512]{1,0:T(8,128)S(1)}, f32[96,512]{1,0:T(8,128)S(1)}, u32[]{:S(2)}, u32[]{:S(2)}) collective-permute-start(f32[96,512]{1,0:T(8,128)S(1)} %get-tuple-element.43), channel_id=1, source_target_pairs={{0,7},{1,0},{2,1},{3,2},{4,3},{5,4},{6,5},{7,6},{8,15},{9,8},{10,9... | collective-permute-start | bytes 589832 | tf_op jit(solution)/shard_map/ppermute | solution.py:728
  13.5 17.5 %collective-permute-start.3 = (f32[96,512]{1,0:T(8,128)S(1)}, f32[96,512]{1,0:T(8,128)S(1)}, u32[]{:S(2)}, u32[]{:S(2)}) collective-permute-start(f32[96,512]{1,0:T(8,128)S(1)} %get-tuple-element.44), channel_id=1, source_target_pairs={{0,1},{1,2},{2,3},{3,4},{4,5},{5,6},{6,7},{7,0},{8,9},{9,10},{10,1... | collective-permute-start | bytes 589832 | tf_op jit(solution)/shard_map/ppermute | solution.py:728
  13.6 5.6 %copy-start = (f32[8,24,512]{2,1,0:T(8,128)S(1)}, f32[8,24,512]{2,1,0:T(8,128)}, u32[]{:S(2)}) copy-start(f32[8,24,512]{2,1,0:T(8,128)} %inv.7) | copy-start | bytes 1179652
  13.6 5.6 %copy-start.2 = (f32[1,512]{1,0:T(1,128)S(1)}, f32[1,512]{1,0:T(1,128)}, u32[]{:S(2)}) copy-start(f32[1,512]{1,0:T(1,128)} %rest_2_.11) | copy-start | bytes 6148
  13.6 5.7 %copy-start.3 = (f32[1,512]{1,0:T(1,128)S(1)}, f32[1,512]{1,0:T(1,128)}, u32[]{:S(2)}) copy-start(f32[1,512]{1,0:T(1,128)} %rest_3_.11) | copy-start | bytes 6148
  13.6 5.7 %copy-start.4 = (f32[1,3]{1,0:T(1,128)S(1)}, f32[1,3]{1,0:T(1,128)}, u32[]{:S(2)}) copy-start(f32[1,3]{1,0:T(1,128)} %rest_0_.11) | copy-start | bytes 40
  13.6 5.7 %copy-start.5 = (f32[1,3]{1,0:T(1,128)S(1)}, f32[1,3]{1,0:T(1,128)}, u32[]{:S(2)}) copy-start(f32[1,3]{1,0:T(1,128)} %rest_1_.11) | copy-start | bytes 40
  19.7 15.1 %collective-permute-start.4 = (f32[96,512]{1,0:T(8,128)S(1)}, f32[96,512]{1,0:T(8,128)S(1)}, u32[]{:S(2)}, u32[]{:S(2)}) collective-permute-start(f32[96,512]{1,0:T(8,128)S(1)} %get-tuple-element.53), channel_id=1, source_target_pairs={{0,1},{1,2},{2,3},{3,4},{4,5},{5,6},{6,7},{7,0},{8,9},{9,10},{10,1... | collective-permute-start | bytes 589832 | tf_op jit(solution)/shard_map/ppermute | solution.py:728
  19.8 15.0 %collective-permute-start.5 = (f32[96,512]{1,0:T(8,128)S(1)}, f32[96,512]{1,0:T(8,128)S(1)}, u32[]{:S(2)}, u32[]{:S(2)}) collective-permute-start(f32[96,512]{1,0:T(8,128)S(1)} %get-tuple-element.54), channel_id=1, source_target_pairs={{0,7},{1,0},{2,1},{3,2},{4,3},{5,4},{6,5},{7,6},{8,15},{9,8},{10,9... | collective-permute-start | bytes 589832 | tf_op jit(solution)/shard_map/ppermute | solution.py:728
  34.8 4.1 %copy-start.1 = (f32[64,64]{1,0:T(8,128)S(1)}, f32[64,64]{1,0:T(8,128)}, u32[]{:S(2)}) copy-start(f32[64,64]{1,0:T(8,128)} %density.3) | copy-start | bytes 49156
  34.8 4.1 %copy-start.6 = (s32[1,8]{1,0:T(1,128)S(1)}, s32[1,8]{1,0:T(1,128)}, u32[]{:S(2)}) copy-start(s32[1,8]{1,0:T(1,128)} %mask.3) | copy-start | bytes 100
  34.8 4.1 %copy-start.7 = (s32[1,8]{1,0:T(1,128)S(1)}, s32[1,8]{1,0:T(1,128)}, u32[]{:S(2)}) copy-start(s32[1,8]{1,0:T(1,128)} %radius_map.1) | copy-start | bytes 100
  36.0 10.7 %all-to-all-start = ((f32[32,8,72]{2,1,0:T(8,128)}), f32[32,8,72]{2,1,0:T(8,128)S(1)}, u32[]{:S(2)}, u32[]{:S(2)}) async-start(f32[32,8,72]{2,1,0:T(8,128)} %bitcast.1), calls=%async_computation | async-start | bytes 262144 | tf_op jit(solution)/shard_map/all_to_all | solution.py:887

commit v6 on v5

--- a/solution.py
+++ b/solution.py
@@ -357,14 +357,14 @@
     return has_prior, has_next
 
 
-def write_copies(parts, fields, sems):
+def write_copies(parts, fields, sems, runs=(0, 1)):
     return [
         pltpu.make_async_copy(
             ref.at[run, *(pl.ds(at, n) for at, n in zip(source, count))],
             fields[run].at[0, *(pl.ds(at, n) for at, n in zip(target, count))],
             sems.at[len(parts) * run + part],
         )
-        for run in range(2)
+        for run in runs
         for part, (ref, source, count, target) in enumerate(parts)
     ]
 
@@ -482,7 +482,7 @@
 
 
 def step_one(inv, *rest):
-    given, (before, prior_a, next_a, early, parts, share) = rest[:6], rest[6:]
+    given, (before, next_a, prior_a, early, parts, share) = rest[:6], rest[6:]
     parts[...] = jnp.zeros_like(parts)
     for side, ref in enumerate((prior_a, next_a)):
         parts[pl.ds(side * PART, PART), :] = ref[pl.ds(4 * NZ, PART), :]
@@ -499,7 +499,7 @@
 
 def borders(inv, *rest):
     given, (before, early, resp_in, scaled, share, ends, next_b, prior_b) = rest[:6], rest[6:14]
-    kept, inner, summed, waiting, fwd_out, adj_out, resp, total, sems = rest[14:]
+    kept, summed, waiting, fwd_out, adj_out, inner, resp, total, inside_sems, sems = rest[14:]
     rows = inv.shape[0]
     last = rows - 1
     inside = rows - 2 * STEPS
@@ -509,9 +509,18 @@
             (before, (3, STEPS - 1), (3, inside + 1), (3, STEPS - 1)),
         ),
         (fwd_out, adj_out),
-        sems,
+        inside_sems,
     )
     start_all(out)
+    rows_done = (
+        (inner, (0, 0), (6, 1), (0, 1)),
+        (inner, (0, 1), (3, 1), (0, 2)),
+        (inner, (0, 2), (6, 1), (0, last - 2)),
+        (kept, (0, 1), (6, 1), (0, last - 1)),
+        (kept, (0, 0), (1, 1), (0, 0)),
+        (kept, (3, 0), (3, 1), (3, 0)),
+        (kept, (3, 2), (1, 1), (3, last)),
+    )
     homes = {0: (kept, 0), last - 1: (kept, 1), last: (kept, 2)}
     homes |= {1: (inner, 0), 2: (inner, 1), last - 2: (inner, 2)}
 
@@ -535,7 +544,14 @@
             seen[:] = [state.written]
             return carry
 
-        lax.fori_loop(0, 2, one_run, 0)
+        if whole:
+            lax.fori_loop(0, 2, one_run, 0)
+        else:
+            for run in range(2):
+                one_run(run, 0)
+                mine = write_copies(rows_done, (fwd_out, adj_out), sems, (run,))
+                start_all(mine)
+                out = out + mine
         written = seen[0]
         reached = list(range(turn + 1)) + list(range(last - turn, last + 1))
         for x in reached if whole else reached[1:-1]:
@@ -551,7 +567,7 @@
 
 
 def last_planes(inv, *rest):
-    given, (kept, summed, waiting, prior_c, next_c, _, blocks, ends) = rest[:6], rest[6:]
+    given, (kept, summed, waiting, prior_c, next_c, blocks, ends) = rest[:6], rest[6:]
     last = inv.shape[0] - 1
     has_prior, has_next = flags()
 
@@ -598,26 +614,6 @@
         turned = pltpu.roll(full, (RMAX - k * (NY // slabs)) % NY, 1)
         for f in range(blocks.shape[0]):
             blocks[f, k] = turned[:, :width]
-
-
-def write_borders(fwd, adj, kept, inner, fwd_out, adj_out, done, sems):
-    last = fwd.shape[2] - 1
-    done[...] = jnp.zeros_like(done)
-    out = write_copies(
-        (
-            (inner, (0, 0), (6, 1), (0, 1)),
-            (inner, (0, 1), (3, 1), (0, 2)),
-            (inner, (0, 2), (6, 1), (0, last - 2)),
-            (kept, (0, 1), (6, 1), (0, last - 1)),
-            (kept, (0, 0), (1, 1), (0, 0)),
-            (kept, (3, 0), (3, 1), (3, 0)),
-            (kept, (3, 2), (1, 1), (3, last)),
-        ),
-        (fwd_out, adj_out),
-        sems,
-    )
-    start_all(out)
-    wait_all(out)
 
 
 def write_ends(fwd, adj, ends, fwd_out, adj_out, sems):
@@ -822,7 +818,7 @@
         [],
         "step_one",
         micros=0,
-    )(inverse_permittivity, *waves, *planes, state, prior_a, next_a)
+    )(inverse_permittivity, *waves, *planes, state, next_a, prior_a)
     parts = lax.all_gather(parts, "freq")
     resp, scaled = kernel_call(
         respond,
@@ -843,12 +839,18 @@
         micros=0,
     )(prior_a, next_a, design_density, design_mask, radius_map)
     three = shaped(2, 6, 3, *PLANE)
-    kept, inner, summed, waiting, forward_part, adjoint_part = kernel_call(
+    kept, summed, waiting, forward_part, adjoint_part = kernel_call(
         borders,
-        (three, three, shaped(rows, NY), shaped(2, 8, *PLANE), field_shape, field_shape),
+        (three, shaped(rows, NY), shaped(2, 8, *PLANE), field_shape, field_shape),
         [VMEM] + SOURCE_VALUES + [VMEM] * 8,
-        (VMEM,) * 4 + (HBM,) * 2,
-        [vmem(2, 8, *PLANE), vmem(rows, 8, NY), dma((4,))],
+        (VMEM,) * 3 + (HBM,) * 2,
+        [
+            vmem(2, 6, 3, *PLANE),
+            vmem(2, 8, *PLANE),
+            vmem(rows, 8, NY),
+            dma((4,)),
+            dma((14,)),
+        ],
         "borders",
         micros=0,
         grant=2 * GRANT,
@@ -856,23 +858,14 @@
         inverse_permittivity, *waves, *planes, state, early, resp, scaled, share, ends,
         next_b, prior_b,
     )
-    forward_part, adjoint_part, done = kernel_call(
-        write_borders,
-        (field_shape, field_shape, shaped(8, 128)),
-        [HBM] * 2 + [VMEM] * 2,
-        (HBM, HBM, VMEM),
-        [dma((14,))],
-        "write_borders",
-        input_output_aliases={0: 0, 1: 1},
-    )(forward_part, adjoint_part, kept, inner)
     blocks, ends = kernel_call(
         last_planes,
         (shaped(freqs, slabs, rows, reach), shaped(2, 7, 1, *PLANE)),
-        [VMEM] + SOURCE_VALUES + [VMEM] * 6,
+        [VMEM] + SOURCE_VALUES + [VMEM] * 5,
         (VMEM, VMEM),
         [],
         "last_planes",
-    )(inverse_permittivity, *waves, *planes, kept, summed, waiting, prior_c, next_c, done)
+    )(inverse_permittivity, *waves, *planes, kept, summed, waiting, prior_c, next_c)
     forward_out, adjoint_out = kernel_call(
         write_ends,
         (field_shape, field_shape),

time: 47.9 us -> 47.9 us (level)
    pallas_call x2 -> x1, Pallas kernels: 3.74 us -> 3.34 us  [on_device(): kernel_call(borders, (three, shaped(rows, NY), shaped(2, 8, *PLANE), fiel...]
  transfers between devices with their start and end apart: 7 -> 7, of which waited for: 1 -> 1; matrix products, arithmetic and copies ran while one was open for 0% -> 0% of each run, Pallas kernels for 31% -> 30%
where the time goes in v6:
time: 47.9 us; the launch traced here: 47.7 us
  Pallas kernels  17.9 us (37%)
  starting transfers between devices  16.7 us (35%)
  blocking collectives  5.43 us (11%)
  waiting for transfers between devices  5.4 us (11%)
  between operations  2.15 us (4%)
    ppermute x6, starting transfers between devices, around(): lax.ppermute(shard, axis, [(i, (i + by) % count) for i in range(count)])  13.4 us
    pallas_call x1, Pallas kernels, on_device(): kernel_call(interior, (state_shape, shaped(rows, 8, NY)), [HBM] * 3 + SOU...  5.6 us
    all_gather x1, blocking collectives, on_device(): parts = lax.all_gather(parts, 'freq')  5.43 us
    all_to_all x1, waiting for transfers between devices, on_device(): blocks = lax.all_to_all(blocks, ('freq', 'slab'), 0, 0, tiled=True)  5.38 us
    pallas_call x1, Pallas kernels, on_device(): kernel_call(borders, (three, shaped(rows, NY), shaped(2, 8, *PLANE), fiel...  3.34 us
    all_to_all x1, starting transfers between devices, on_device(): blocks = lax.all_to_all(blocks, ('freq', 'slab'), 0, 0, tiled=True)  3.33 us
    pallas_call x1, Pallas kernels, on_device(): kernel_call(second_planes, (four, four, shaped(2, 9, *PLANE)), [HBM] * 3...  2.1 us
    pallas_call x1, Pallas kernels, on_device(): kernel_call(filter_operands, (shaped(width, reach), shaped(width, reach),...  1.42 us
  transfers between devices with their start and end apart: 7, of which 1 were waited for; matrix products, arithmetic and copies ran while one was open for 0% of the time, Pallas kernels for 30%

profile of v6, /device:TPU:0, one launch (start us, length us, event | category | flops | bytes accessed | tf_op | source)
XLA Modules:
  0.0 47.7 jit_solution(11130866814998921408)
XLA Ops:
  0.6 1.4 %first_planes.1 = (f32[104,512]{1,0:T(8,128)S(1)}, f32[104,512]{1,0:T(8,128)S(1)}) custom-call(f32[1,6,8,24,512]{4,3,2,1,0:T(8,128)} %fwd.5, f32[1,6,8,24,512]{4,3,2,1,0:T(8,128)} %adj.5, f32[8,24,512]{2,1,0:T(8,128)} %inv.7, f32[64,64]{1,0:T(8,128)} %density.3, s32[1,8]{1,0:T(1,128)} %mask.3), custom_call_target="tpu_custom_call" | custom-call | flops 1000000000 | tf_op jit(solution)/shard_map/first_planes/pallas_call | solution.py:761
  2.0 3.0 %collective-permute-start.1 = (f32[104,512]{1,0:T(8,128)S(1)}, f32[104,512]{1,0:T(8,128)S(1)}, u32[]{:S(2)}, u32[]{:S(2)}) collective-permute-start(f32[104,512]{1,0:T(8,128)S(1)} %get-tuple-element.32), channel_id=1, source_target_pairs={{0,1},{1,2},{2,3},{3,4},{4,5},{5,6},{6,7},{7,0},{8,9},{9,10},{10,1... | collective-permute-start | bytes 638984 | tf_op jit(solution)/shard_map/ppermute | solution.py:724
  5.0 3.1 %collective-permute-start = (f32[104,512]{1,0:T(8,128)S(1)}, f32[104,512]{1,0:T(8,128)S(1)}, u32[]{:S(2)}, u32[]{:S(2)}) collective-permute-start(f32[104,512]{1,0:T(8,128)S(1)} %get-tuple-element.29.rest_6_), channel_id=1, source_target_pairs={{0,7},{1,0},{2,1},{3,2},{4,3},{5,4},{6,5},{7,6},{8,15},{9,8},{10,9... | collective-permute-start | bytes 638984 | tf_op jit(solution)/shard_map/ppermute | solution.py:724
  9.4 2.1 %second_planes.1 = (f32[96,512]{1,0:T(8,128)S(1)}, f32[96,512]{1,0:T(8,128)S(1)}, f32[2,9,24,512]{3,2,1,0:T(8,128)S(1)}) custom-call(f32[1,6,8,24,512]{4,3,2,1,0:T(8,128)} %fwd.5, f32[1,6,8,24,512]{4,3,2,1,0:T(8,128)} %adj.5, f32[8,24,512]{2,1,0:T(8,128)} %inv.7, f32[1,3]{1,0:T(1,128)} %rest_0_.11, f32[1,3]{1,0:T(1,128)} %rest_1_.11, f32[1,512]{1,0:T(1,128)} %rest_2_.11, ...), custom_call_target="tpu_custom_call" | custom-call | flops 2000000000 | tf_op jit(solution)/shard_map/second_planes/pallas_call | solution.py:777
  11.5 2.0 %collective-permute-start.2 = (f32[96,512]{1,0:T(8,128)S(1)}, f32[96,512]{1,0:T(8,128)S(1)}, u32[]{:S(2)}, u32[]{:S(2)}) collective-permute-start(f32[96,512]{1,0:T(8,128)S(1)} %get-tuple-element.39), channel_id=1, source_target_pairs={{0,7},{1,0},{2,1},{3,2},{4,3},{5,4},{6,5},{7,6},{8,15},{9,8},{10,9... | collective-permute-start | bytes 589832 | tf_op jit(solution)/shard_map/ppermute | solution.py:724
  13.5 0.1 collective-permute-start.3
  13.6 0.0 copy-start.5
  13.6 5.6 %interior.1 = (f32[2,6,8,24,512]{4,3,2,1,0:T(8,128)S(1)}, f32[8,8,512]{2,1,0:T(8,128)S(1)}) custom-call(f32[1,6,8,24,512]{4,3,2,1,0:T(8,128)} %fwd.5, f32[1,6,8,24,512]{4,3,2,1,0:T(8,128)} %adj.5, f32[8,24,512]{2,1,0:T(8,128)} %inv.7, f32[1,3]{1,0:T(1,128)} %rest_0_.11, f32[1,3]{1,0:T(1,128)} %rest_1_.11, f32[1,512]{1,0:T(1,128)} %rest_2_.11, ...), custom_call_target="tpu_custom_call" | custom-call | flops 8000000000 | tf_op jit(solution)/shard_map/interior/pallas_call | solution.py:794
  19.3 0.4 third_planes.1
  19.7 0.1 collective-permute-start.4
  19.8 5.2 %collective-permute-start.5 = (f32[96,512]{1,0:T(8,128)S(1)}, f32[96,512]{1,0:T(8,128)S(1)}, u32[]{:S(2)}, u32[]{:S(2)}) collective-permute-start(f32[96,512]{1,0:T(8,128)S(1)} %get-tuple-element.47), channel_id=1, source_target_pairs={{0,7},{1,0},{2,1},{3,2},{4,3},{5,4},{6,5},{7,6},{8,15},{9,8},{10,9... | collective-permute-start | bytes 589832 | tf_op jit(solution)/shard_map/ppermute | solution.py:724
  25.0 0.4 step_one.1
  25.4 5.4 %all-gather = f32[64,512]{1,0:T(8,128)S(1)} all-gather(f32[16,512]{1,0:T(8,128)S(1)} %get-tuple-element.34), channel_id=2, replica_groups=mesh['freq'=4,'slab'=8] {'freq'}, dimensions={0}, use_global_device_ids=true | all-gather | bytes 163840 | tf_op jit(solution)/shard_map/all_gather | solution.py:822
  30.8 0.2 respond.1
  31.0 3.3 %borders.1 = (f32[2,6,3,24,512]{4,3,2,1,0:T(8,128)S(1)}, f32[8,512]{1,0:T(8,128)S(1)}, f32[2,8,24,512]{3,2,1,0:T(8,128)S(1)}, f32[1,6,8,24,512]{4,3,2,1,0:T(8,128)}, f32[1,6,8,24,512]{4,3,2,1,0:T(8,128)}) custom-call(f32[8,24,512]{2,1,0:T(8,128)S(1)} %copy-done, f32[1,3]{1,0:T(1,128)S(1)} %copy-done.4, f32[1,3]{1,0:T(1,128)S(1)} %copy-done.5, ...), custom_call_target="tpu_custom_call" | custom-call | tf_op jit(solution)/shard_map/borders/pallas_call | solution.py:842
  34.4 0.0 copy-start.1
  34.4 0.0 copy-start.6
  34.4 0.0 copy-start.7
  34.4 1.2 %last_planes.1 = (f32[4,8,8,72]{3,2,1,0:T(8,128)}, f32[2,7,1,24,512]{4,3,2,1,0:T(8,128)S(1)}) custom-call(f32[8,24,512]{2,1,0:T(8,128)S(1)} %copy-done, f32[1,3]{1,0:T(1,128)S(1)} %copy-done.4, f32[1,3]{1,0:T(1,128)S(1)} %copy-done.5, f32[1,512]{1,0:T(1,128)S(1)} %copy-done.2, f32[1,512]{1,0:T(1,128)S(1)} %copy-done.3, s32[1]{0:T(128)S(6)} %copy.19.rest_4_, ...), custom_call_target="tpu_custom_call" | custom-call | flops 1000000000 | tf_op jit(solution)/shard_map/last_planes/pallas_call | solution.py:861
  35.6 3.3 %all-to-all-start = ((f32[32,8,72]{2,1,0:T(8,128)}), f32[32,8,72]{2,1,0:T(8,128)S(1)}, u32[]{:S(2)}, u32[]{:S(2)}) async-start(f32[32,8,72]{2,1,0:T(8,128)} %bitcast.1), calls=%async_computation | async-start | bytes 262144 | tf_op jit(solution)/shard_map/all_to_all | solution.py:880
  39.0 1.4 %filter_operands.1 = (f32[64,72]{1,0:T(8,128)S(1)}, f32[64,72]{1,0:T(8,128)S(1)}, f32[15,64,64]{2,1,0:T(8,128)S(1)}) custom-call(f32[104,512]{1,0:T(8,128)S(1)} %collective-permute-done.1.rest_8_.prior_a, f32[104,512]{1,0:T(8,128)S(1)} %collective-permute-done.rest_7_.next_a, f32[64,64]{1,0:T(8,128)S(1)} %copy-done.1, s32[1,8]{1,0:T(1,128)S(1)} %copy-done.6, ...), custom_call_target="tpu_custom_call" | custom-call | tf_op jit(solution)/shard_map/filter_operands/pallas_call | solution.py:832
  40.4 0.9 %write_ends.1 = (f32[1,6,8,24,512]{4,3,2,1,0:T(8,128)}, f32[1,6,8,24,512]{4,3,2,1,0:T(8,128)}) custom-call(f32[1,6,8,24,512]{4,3,2,1,0:T(8,128)} %get-tuple-element.41.fwd, f32[1,6,8,24,512]{4,3,2,1,0:T(8,128)} %get-tuple-element.42.adj, f32[2,7,1,24,512]{4,3,2,1,0:T(8,128)S(1)} %get-tuple-element.48.ends), custom_call_target="tpu_custom_call", output_to_operand_aliasing={{0}: (0, {}), {1}: (1, {})} | custom-call | flops 1000000000 | tf_op jit(solution)/shard_map/write_ends/pallas_call | solution.py:869
  41.3 5.4 %all-to-all-done = f32[32,8,72]{2,1,0:T(8,128)S(1)} async-done(((f32[32,8,72]{2,1,0:T(8,128)}), f32[32,8,72]{2,1,0:T(8,128)S(1)}, u32[]{:S(2)}, u32[]{:S(2)}) %all-to-all-start) | async-done | bytes 73760 | tf_op jit(solution)/shard_map/all_to_all | solution.py:880
  46.7 1.0 %project.1 = f32[64,64]{1,0:T(8,128)} custom-call(f32[4,8,8,72]{3,2,1,0:T(8,128)S(1)} %bitcast.4, f32[64,72]{1,0:T(8,128)S(1)} %get-tuple-element.52.padded, f32[64,72]{1,0:T(8,128)S(1)} %get-tuple-element.53.chosen, f32[15,64,64]{2,1,0:T(8,128)S(1)} %get-tuple-element.54.weights), custom_call_target="tpu_custom_call" | custom-call | flops 1000000000 | tf_op jit(solution)/shard_map/project/pallas_call | solution.py:882
  (18 shorter events, 0.0 us)
Async XLA Ops:
  2.0 17.8 %collective-permute-start.1 = (f32[104,512]{1,0:T(8,128)S(1)}, f32[104,512]{1,0:T(8,128)S(1)}, u32[]{:S(2)}, u32[]{:S(2)}) collective-permute-start(f32[104,512]{1,0:T(8,128)S(1)} %get-tuple-element.32), channel_id=1, source_target_pairs={{0,1},{1,2},{2,3},{3,4},{4,5},{5,6},{6,7},{7,0},{8,9},{9,10},{10,1... | collective-permute-start | bytes 638984 | tf_op jit(solution)/shard_map/ppermute | solution.py:724
  5.0 20.0 %collective-permute-start = (f32[104,512]{1,0:T(8,128)S(1)}, f32[104,512]{1,0:T(8,128)S(1)}, u32[]{:S(2)}, u32[]{:S(2)}) collective-permute-start(f32[104,512]{1,0:T(8,128)S(1)} %get-tuple-element.29.rest_6_), channel_id=1, source_target_pairs={{0,7},{1,0},{2,1},{3,2},{4,3},{5,4},{6,5},{7,6},{8,15},{9,8},{10,9... | collective-permute-start | bytes 638984 | tf_op jit(solution)/shard_map/ppermute | solution.py:724
  11.5 19.5 %collective-permute-start.2 = (f32[96,512]{1,0:T(8,128)S(1)}, f32[96,512]{1,0:T(8,128)S(1)}, u32[]{:S(2)}, u32[]{:S(2)}) collective-permute-start(f32[96,512]{1,0:T(8,128)S(1)} %get-tuple-element.39), channel_id=1, source_target_pairs={{0,7},{1,0},{2,1},{3,2},{4,3},{5,4},{6,5},{7,6},{8,15},{9,8},{10,9... | collective-permute-start | bytes 589832 | tf_op jit(solution)/shard_map/ppermute | solution.py:724
  13.5 17.5 %collective-permute-start.3 = (f32[96,512]{1,0:T(8,128)S(1)}, f32[96,512]{1,0:T(8,128)S(1)}, u32[]{:S(2)}, u32[]{:S(2)}) collective-permute-start(f32[96,512]{1,0:T(8,128)S(1)} %get-tuple-element.40), channel_id=1, source_target_pairs={{0,1},{1,2},{2,3},{3,4},{4,5},{5,6},{6,7},{7,0},{8,9},{9,10},{10,1... | collective-permute-start | bytes 589832 | tf_op jit(solution)/shard_map/ppermute | solution.py:724
  13.6 5.6 %copy-start = (f32[8,24,512]{2,1,0:T(8,128)S(1)}, f32[8,24,512]{2,1,0:T(8,128)}, u32[]{:S(2)}) copy-start(f32[8,24,512]{2,1,0:T(8,128)} %inv.7) | copy-start | bytes 1179652
  13.6 5.6 %copy-start.2 = (f32[1,512]{1,0:T(1,128)S(1)}, f32[1,512]{1,0:T(1,128)}, u32[]{:S(2)}) copy-start(f32[1,512]{1,0:T(1,128)} %rest_2_.11) | copy-start | bytes 6148
  13.6 5.7 %copy-start.3 = (f32[1,512]{1,0:T(1,128)S(1)}, f32[1,512]{1,0:T(1,128)}, u32[]{:S(2)}) copy-start(f32[1,512]{1,0:T(1,128)} %rest_3_.11) | copy-start | bytes 6148
  13.6 5.7 %copy-start.4 = (f32[1,3]{1,0:T(1,128)S(1)}, f32[1,3]{1,0:T(1,128)}, u32[]{:S(2)}) copy-start(f32[1,3]{1,0:T(1,128)} %rest_0_.11) | copy-start | bytes 40
  13.6 5.7 %copy-start.5 = (f32[1,3]{1,0:T(1,128)S(1)}, f32[1,3]{1,0:T(1,128)}, u32[]{:S(2)}) copy-start(f32[1,3]{1,0:T(1,128)} %rest_1_.11) | copy-start | bytes 40
  19.7 14.7 %collective-permute-start.4 = (f32[96,512]{1,0:T(8,128)S(1)}, f32[96,512]{1,0:T(8,128)S(1)}, u32[]{:S(2)}, u32[]{:S(2)}) collective-permute-start(f32[96,512]{1,0:T(8,128)S(1)} %get-tuple-element.46), channel_id=1, source_target_pairs={{0,1},{1,2},{2,3},{3,4},{4,5},{5,6},{6,7},{7,0},{8,9},{9,10},{10,1... | collective-permute-start | bytes 589832 | tf_op jit(solution)/shard_map/ppermute | solution.py:724
  19.8 14.6 %collective-permute-start.5 = (f32[96,512]{1,0:T(8,128)S(1)}, f32[96,512]{1,0:T(8,128)S(1)}, u32[]{:S(2)}, u32[]{:S(2)}) collective-permute-start(f32[96,512]{1,0:T(8,128)S(1)} %get-tuple-element.47), channel_id=1, source_target_pairs={{0,7},{1,0},{2,1},{3,2},{4,3},{5,4},{6,5},{7,6},{8,15},{9,8},{10,9... | collective-permute-start | bytes 589832 | tf_op jit(solution)/shard_map/ppermute | solution.py:724
  34.4 4.6 %copy-start.1 = (f32[64,64]{1,0:T(8,128)S(1)}, f32[64,64]{1,0:T(8,128)}, u32[]{:S(2)}) copy-start(f32[64,64]{1,0:T(8,128)} %density.3) | copy-start | bytes 49156
  34.4 4.6 %copy-start.6 = (s32[1,8]{1,0:T(1,128)S(1)}, s32[1,8]{1,0:T(1,128)}, u32[]{:S(2)}) copy-start(s32[1,8]{1,0:T(1,128)} %mask.3) | copy-start | bytes 100
  34.4 4.6 %copy-start.7 = (s32[1,8]{1,0:T(1,128)S(1)}, s32[1,8]{1,0:T(1,128)}, u32[]{:S(2)}) copy-start(s32[1,8]{1,0:T(1,128)} %radius_map.1) | copy-start | bytes 100
  35.6 11.1 %all-to-all-start = ((f32[32,8,72]{2,1,0:T(8,128)}), f32[32,8,72]{2,1,0:T(8,128)S(1)}, u32[]{:S(2)}, u32[]{:S(2)}) async-start(f32[32,8,72]{2,1,0:T(8,128)} %bitcast.1), calls=%async_computation | async-start | bytes 262144 | tf_op jit(solution)/shard_map/all_to_all | solution.py:880

commit v7 on v6

--- a/solution.py
+++ b/solution.py
@@ -567,7 +567,9 @@
 
 
 def last_planes(inv, *rest):
-    given, (kept, summed, waiting, prior_c, next_c, blocks, ends) = rest[:6], rest[6:]
+    given, (kept, summed, waiting, prior_c, next_c, blocks, ends, built, sems) = (
+        rest[:6], rest[6:]
+    )
     last = inv.shape[0] - 1
     has_prior, has_next = flags()
 
@@ -612,8 +614,12 @@
     slabs, width = blocks.shape[1], blocks.shape[3]
     for k in range(slabs):
         turned = pltpu.roll(full, (RMAX - k * (NY // slabs)) % NY, 1)
-        for f in range(blocks.shape[0]):
-            blocks[f, k] = turned[:, :width]
+        built[k] = turned[:, :width]
+    out = [
+        pltpu.make_async_copy(built, blocks.at[f], sems.at[f]) for f in range(blocks.shape[0])
+    ]
+    start_all(out)
+    wait_all(out)
 
 
 def write_ends(fwd, adj, ends, fwd_out, adj_out, sems):
@@ -862,8 +868,8 @@
         last_planes,
         (shaped(freqs, slabs, rows, reach), shaped(2, 7, 1, *PLANE)),
         [VMEM] + SOURCE_VALUES + [VMEM] * 5,
-        (VMEM, VMEM),
-        [],
+        (HBM, VMEM),
+        [vmem(slabs, rows, reach), dma((freqs,))],
         "last_planes",
     )(inverse_permittivity, *waves, *planes, kept, summed, waiting, prior_c, next_c)
     forward_out, adjoint_out = kernel_call(

time: 47.9 us -> 48 us (level)
  no operation moved by 1% of the time
where the time goes in v7:
time: 48 us; the launch traced here: 47.7 us
  Pallas kernels  18 us (38%)
  starting transfers between devices  16.7 us (35%)
  blocking collectives  5.43 us (11%)
  waiting for transfers between devices  5.4 us (11%)
  between operations  2.15 us (4%)
    ppermute x6, starting transfers between devices, around(): lax.ppermute(shard, axis, [(i, (i + by) % count) for i in range(count)])  13.4 us
    pallas_call x1, Pallas kernels, on_device(): kernel_call(interior, (state_shape, shaped(rows, 8, NY)), [HBM] * 3 + SOU...  5.6 us
    all_gather x1, blocking collectives, on_device(): parts = lax.all_gather(parts, 'freq')  5.43 us
    all_to_all x1, waiting for transfers between devices, on_device(): blocks = lax.all_to_all(blocks, ('freq', 'slab'), 0, 0, tiled=True)  5.38 us
    all_to_all x1, starting transfers between devices, on_device(): blocks = lax.all_to_all(blocks, ('freq', 'slab'), 0, 0, tiled=True)  3.34 us
    pallas_call x1, Pallas kernels, on_device(): kernel_call(borders, (three, shaped(rows, NY), shaped(2, 8, *PLANE), fiel...  3.34 us
    pallas_call x1, Pallas kernels, on_device(): kernel_call(second_planes, (four, four, shaped(2, 9, *PLANE)), [HBM] * 3...  2.1 us
    pallas_call x1, Pallas kernels, on_device(): kernel_call(filter_operands, (shaped(width, reach), shaped(width, reach),...  1.42 us
  transfers between devices with their start and end apart: 7, of which 1 were waited for; matrix products, arithmetic and copies ran while one was open for 0% of the time, Pallas kernels for 30%

profile of v7, /device:TPU:0, one launch (start us, length us, event | category | flops | bytes accessed | tf_op | source)
XLA Modules:
  0.0 47.7 jit_solution(15634096398271285739)
XLA Ops:
  0.6 1.4 %first_planes.1 = (f32[104,512]{1,0:T(8,128)S(1)}, f32[104,512]{1,0:T(8,128)S(1)}) custom-call(f32[1,6,8,24,512]{4,3,2,1,0:T(8,128)} %fwd.5, f32[1,6,8,24,512]{4,3,2,1,0:T(8,128)} %adj.5, f32[8,24,512]{2,1,0:T(8,128)} %inv.7, f32[64,64]{1,0:T(8,128)} %density.3, s32[1,8]{1,0:T(1,128)} %mask.3), custom_call_target="tpu_custom_call" | custom-call | flops 1000000000 | tf_op jit(solution)/shard_map/first_planes/pallas_call | solution.py:767
  2.0 3.0 %collective-permute-start.1 = (f32[104,512]{1,0:T(8,128)S(1)}, f32[104,512]{1,0:T(8,128)S(1)}, u32[]{:S(2)}, u32[]{:S(2)}) collective-permute-start(f32[104,512]{1,0:T(8,128)S(1)} %get-tuple-element.32), channel_id=1, source_target_pairs={{0,1},{1,2},{2,3},{3,4},{4,5},{5,6},{6,7},{7,0},{8,9},{9,10},{10,1... | collective-permute-start | bytes 638984 | tf_op jit(solution)/shard_map/ppermute | solution.py:730
  5.0 3.1 %collective-permute-start = (f32[104,512]{1,0:T(8,128)S(1)}, f32[104,512]{1,0:T(8,128)S(1)}, u32[]{:S(2)}, u32[]{:S(2)}) collective-permute-start(f32[104,512]{1,0:T(8,128)S(1)} %get-tuple-element.29.rest_6_), channel_id=1, source_target_pairs={{0,7},{1,0},{2,1},{3,2},{4,3},{5,4},{6,5},{7,6},{8,15},{9,8},{10,9... | collective-permute-start | bytes 638984 | tf_op jit(solution)/shard_map/ppermute | solution.py:730
  9.4 2.1 %second_planes.1 = (f32[96,512]{1,0:T(8,128)S(1)}, f32[96,512]{1,0:T(8,128)S(1)}, f32[2,9,24,512]{3,2,1,0:T(8,128)S(1)}) custom-call(f32[1,6,8,24,512]{4,3,2,1,0:T(8,128)} %fwd.5, f32[1,6,8,24,512]{4,3,2,1,0:T(8,128)} %adj.5, f32[8,24,512]{2,1,0:T(8,128)} %inv.7, f32[1,3]{1,0:T(1,128)} %rest_0_.11, f32[1,3]{1,0:T(1,128)} %rest_1_.11, f32[1,512]{1,0:T(1,128)} %rest_2_.11, ...), custom_call_target="tpu_custom_call" | custom-call | flops 2000000000 | tf_op jit(solution)/shard_map/second_planes/pallas_call | solution.py:783
  11.5 2.0 %collective-permute-start.2 = (f32[96,512]{1,0:T(8,128)S(1)}, f32[96,512]{1,0:T(8,128)S(1)}, u32[]{:S(2)}, u32[]{:S(2)}) collective-permute-start(f32[96,512]{1,0:T(8,128)S(1)} %get-tuple-element.39), channel_id=1, source_target_pairs={{0,7},{1,0},{2,1},{3,2},{4,3},{5,4},{6,5},{7,6},{8,15},{9,8},{10,9... | collective-permute-start | bytes 589832 | tf_op jit(solution)/shard_map/ppermute | solution.py:730
  13.5 0.1 collective-permute-start.3
  13.6 0.0 copy-start.5
  13.6 5.6 %interior.1 = (f32[2,6,8,24,512]{4,3,2,1,0:T(8,128)S(1)}, f32[8,8,512]{2,1,0:T(8,128)S(1)}) custom-call(f32[1,6,8,24,512]{4,3,2,1,0:T(8,128)} %fwd.5, f32[1,6,8,24,512]{4,3,2,1,0:T(8,128)} %adj.5, f32[8,24,512]{2,1,0:T(8,128)} %inv.7, f32[1,3]{1,0:T(1,128)} %rest_0_.11, f32[1,3]{1,0:T(1,128)} %rest_1_.11, f32[1,512]{1,0:T(1,128)} %rest_2_.11, ...), custom_call_target="tpu_custom_call" | custom-call | flops 8000000000 | tf_op jit(solution)/shard_map/interior/pallas_call | solution.py:800
  19.3 0.4 third_planes.1
  19.7 0.1 collective-permute-start.4
  19.8 5.2 %collective-permute-start.5 = (f32[96,512]{1,0:T(8,128)S(1)}, f32[96,512]{1,0:T(8,128)S(1)}, u32[]{:S(2)}, u32[]{:S(2)}) collective-permute-start(f32[96,512]{1,0:T(8,128)S(1)} %get-tuple-element.47), channel_id=1, source_target_pairs={{0,7},{1,0},{2,1},{3,2},{4,3},{5,4},{6,5},{7,6},{8,15},{9,8},{10,9... | collective-permute-start | bytes 589832 | tf_op jit(solution)/shard_map/ppermute | solution.py:730
  25.0 0.4 step_one.1
  25.4 5.4 %all-gather = f32[64,512]{1,0:T(8,128)S(1)} all-gather(f32[16,512]{1,0:T(8,128)S(1)} %get-tuple-element.34), channel_id=2, replica_groups=mesh['freq'=4,'slab'=8] {'freq'}, dimensions={0}, use_global_device_ids=true | all-gather | bytes 163840 | tf_op jit(solution)/shard_map/all_gather | solution.py:828
  30.8 0.2 respond.1
  31.0 3.3 %borders.1 = (f32[2,6,3,24,512]{4,3,2,1,0:T(8,128)S(1)}, f32[8,512]{1,0:T(8,128)S(1)}, f32[2,8,24,512]{3,2,1,0:T(8,128)S(1)}, f32[1,6,8,24,512]{4,3,2,1,0:T(8,128)}, f32[1,6,8,24,512]{4,3,2,1,0:T(8,128)}) custom-call(f32[8,24,512]{2,1,0:T(8,128)S(1)} %copy-done, f32[1,3]{1,0:T(1,128)S(1)} %copy-done.4, f32[1,3]{1,0:T(1,128)S(1)} %copy-done.5, ...), custom_call_target="tpu_custom_call" | custom-call | tf_op jit(solution)/shard_map/borders/pallas_call | solution.py:848
  34.4 0.0 copy-start.1
  34.4 0.0 copy-start.6
  34.4 0.0 copy-start.7
  34.4 1.2 %last_planes.1 = (f32[4,8,8,72]{3,2,1,0:T(8,128)}, f32[2,7,1,24,512]{4,3,2,1,0:T(8,128)S(1)}) custom-call(f32[8,24,512]{2,1,0:T(8,128)S(1)} %copy-done, f32[1,3]{1,0:T(1,128)S(1)} %copy-done.4, f32[1,3]{1,0:T(1,128)S(1)} %copy-done.5, f32[1,512]{1,0:T(1,128)S(1)} %copy-done.2, f32[1,512]{1,0:T(1,128)S(1)} %copy-done.3, s32[1]{0:T(128)S(6)} %copy.19.rest_4_, ...), custom_call_target="tpu_custom_call" | custom-call | flops 1000000000 | tf_op jit(solution)/shard_map/last_planes/pallas_call | solution.py:867
  35.6 3.3 %all-to-all-start = ((f32[32,8,72]{2,1,0:T(8,128)}), f32[32,8,72]{2,1,0:T(8,128)S(1)}, u32[]{:S(2)}, u32[]{:S(2)}) async-start(f32[32,8,72]{2,1,0:T(8,128)} %bitcast.1), calls=%async_computation | async-start | bytes 262144 | tf_op jit(solution)/shard_map/all_to_all | solution.py:886
  39.0 1.4 %filter_operands.1 = (f32[64,72]{1,0:T(8,128)S(1)}, f32[64,72]{1,0:T(8,128)S(1)}, f32[15,64,64]{2,1,0:T(8,128)S(1)}) custom-call(f32[104,512]{1,0:T(8,128)S(1)} %collective-permute-done.1.rest_8_.prior_a, f32[104,512]{1,0:T(8,128)S(1)} %collective-permute-done.rest_7_.next_a, f32[64,64]{1,0:T(8,128)S(1)} %copy-done.1, s32[1,8]{1,0:T(1,128)S(1)} %copy-done.6, ...), custom_call_target="tpu_custom_call" | custom-call | tf_op jit(solution)/shard_map/filter_operands/pallas_call | solution.py:838
  40.5 0.9 %write_ends.1 = (f32[1,6,8,24,512]{4,3,2,1,0:T(8,128)}, f32[1,6,8,24,512]{4,3,2,1,0:T(8,128)}) custom-call(f32[1,6,8,24,512]{4,3,2,1,0:T(8,128)} %get-tuple-element.41.fwd, f32[1,6,8,24,512]{4,3,2,1,0:T(8,128)} %get-tuple-element.42.adj, f32[2,7,1,24,512]{4,3,2,1,0:T(8,128)S(1)} %get-tuple-element.48.ends), custom_call_target="tpu_custom_call", output_to_operand_aliasing={{0}: (0, {}), {1}: (1, {})} | custom-call | flops 1000000000 | tf_op jit(solution)/shard_map/write_ends/pallas_call | solution.py:875
  41.4 5.4 %all-to-all-done = f32[32,8,72]{2,1,0:T(8,128)S(1)} async-done(((f32[32,8,72]{2,1,0:T(8,128)}), f32[32,8,72]{2,1,0:T(8,128)S(1)}, u32[]{:S(2)}, u32[]{:S(2)}) %all-to-all-start) | async-done | bytes 73760 | tf_op jit(solution)/shard_map/all_to_all | solution.py:886
  46.7 1.0 %project.1 = f32[64,64]{1,0:T(8,128)} custom-call(f32[4,8,8,72]{3,2,1,0:T(8,128)S(1)} %bitcast.4, f32[64,72]{1,0:T(8,128)S(1)} %get-tuple-element.52.padded, f32[64,72]{1,0:T(8,128)S(1)} %get-tuple-element.53.chosen, f32[15,64,64]{2,1,0:T(8,128)S(1)} %get-tuple-element.54.weights), custom_call_target="tpu_custom_call" | custom-call | flops 1000000000 | tf_op jit(solution)/shard_map/project/pallas_call | solution.py:888
  (18 shorter events, 0.0 us)
Async XLA Ops:
  2.0 17.8 %collective-permute-start.1 = (f32[104,512]{1,0:T(8,128)S(1)}, f32[104,512]{1,0:T(8,128)S(1)}, u32[]{:S(2)}, u32[]{:S(2)}) collective-permute-start(f32[104,512]{1,0:T(8,128)S(1)} %get-tuple-element.32), channel_id=1, source_target_pairs={{0,1},{1,2},{2,3},{3,4},{4,5},{5,6},{6,7},{7,0},{8,9},{9,10},{10,1... | collective-permute-start | bytes 638984 | tf_op jit(solution)/shard_map/ppermute | solution.py:730
  5.0 20.0 %collective-permute-start = (f32[104,512]{1,0:T(8,128)S(1)}, f32[104,512]{1,0:T(8,128)S(1)}, u32[]{:S(2)}, u32[]{:S(2)}) collective-permute-start(f32[104,512]{1,0:T(8,128)S(1)} %get-tuple-element.29.rest_6_), channel_id=1, source_target_pairs={{0,7},{1,0},{2,1},{3,2},{4,3},{5,4},{6,5},{7,6},{8,15},{9,8},{10,9... | collective-permute-start | bytes 638984 | tf_op jit(solution)/shard_map/ppermute | solution.py:730
  11.5 19.5 %collective-permute-start.2 = (f32[96,512]{1,0:T(8,128)S(1)}, f32[96,512]{1,0:T(8,128)S(1)}, u32[]{:S(2)}, u32[]{:S(2)}) collective-permute-start(f32[96,512]{1,0:T(8,128)S(1)} %get-tuple-element.39), channel_id=1, source_target_pairs={{0,7},{1,0},{2,1},{3,2},{4,3},{5,4},{6,5},{7,6},{8,15},{9,8},{10,9... | collective-permute-start | bytes 589832 | tf_op jit(solution)/shard_map/ppermute | solution.py:730
  13.5 17.5 %collective-permute-start.3 = (f32[96,512]{1,0:T(8,128)S(1)}, f32[96,512]{1,0:T(8,128)S(1)}, u32[]{:S(2)}, u32[]{:S(2)}) collective-permute-start(f32[96,512]{1,0:T(8,128)S(1)} %get-tuple-element.40), channel_id=1, source_target_pairs={{0,1},{1,2},{2,3},{3,4},{4,5},{5,6},{6,7},{7,0},{8,9},{9,10},{10,1... | collective-permute-start | bytes 589832 | tf_op jit(solution)/shard_map/ppermute | solution.py:730
  13.6 5.6 %copy-start = (f32[8,24,512]{2,1,0:T(8,128)S(1)}, f32[8,24,512]{2,1,0:T(8,128)}, u32[]{:S(2)}) copy-start(f32[8,24,512]{2,1,0:T(8,128)} %inv.7) | copy-start | bytes 1179652
  13.6 5.6 %copy-start.2 = (f32[1,512]{1,0:T(1,128)S(1)}, f32[1,512]{1,0:T(1,128)}, u32[]{:S(2)}) copy-start(f32[1,512]{1,0:T(1,128)} %rest_2_.11) | copy-start | bytes 6148
  13.6 5.7 %copy-start.3 = (f32[1,512]{1,0:T(1,128)S(1)}, f32[1,512]{1,0:T(1,128)}, u32[]{:S(2)}) copy-start(f32[1,512]{1,0:T(1,128)} %rest_3_.11) | copy-start | bytes 6148
  13.6 5.7 %copy-start.4 = (f32[1,3]{1,0:T(1,128)S(1)}, f32[1,3]{1,0:T(1,128)}, u32[]{:S(2)}) copy-start(f32[1,3]{1,0:T(1,128)} %rest_0_.11) | copy-start | bytes 40
  13.6 5.7 %copy-start.5 = (f32[1,3]{1,0:T(1,128)S(1)}, f32[1,3]{1,0:T(1,128)}, u32[]{:S(2)}) copy-start(f32[1,3]{1,0:T(1,128)} %rest_1_.11) | copy-start | bytes 40
  19.7 14.7 %collective-permute-start.4 = (f32[96,512]{1,0:T(8,128)S(1)}, f32[96,512]{1,0:T(8,128)S(1)}, u32[]{:S(2)}, u32[]{:S(2)}) collective-permute-start(f32[96,512]{1,0:T(8,128)S(1)} %get-tuple-element.46), channel_id=1, source_target_pairs={{0,1},{1,2},{2,3},{3,4},{4,5},{5,6},{6,7},{7,0},{8,9},{9,10},{10,1... | collective-permute-start | bytes 589832 | tf_op jit(solution)/shard_map/ppermute | solution.py:730
  19.8 14.6 %collective-permute-start.5 = (f32[96,512]{1,0:T(8,128)S(1)}, f32[96,512]{1,0:T(8,128)S(1)}, u32[]{:S(2)}, u32[]{:S(2)}) collective-permute-start(f32[96,512]{1,0:T(8,128)S(1)} %get-tuple-element.47), channel_id=1, source_target_pairs={{0,7},{1,0},{2,1},{3,2},{4,3},{5,4},{6,5},{7,6},{8,15},{9,8},{10,9... | collective-permute-start | bytes 589832 | tf_op jit(solution)/shard_map/ppermute | solution.py:730
  34.4 4.6 %copy-start.1 = (f32[64,64]{1,0:T(8,128)S(1)}, f32[64,64]{1,0:T(8,128)}, u32[]{:S(2)}) copy-start(f32[64,64]{1,0:T(8,128)} %density.3) | copy-start | bytes 49156
  34.4 4.6 %copy-start.6 = (s32[1,8]{1,0:T(1,128)S(1)}, s32[1,8]{1,0:T(1,128)}, u32[]{:S(2)}) copy-start(s32[1,8]{1,0:T(1,128)} %mask.3) | copy-start | bytes 100
  34.4 4.6 %copy-start.7 = (s32[1,8]{1,0:T(1,128)S(1)}, s32[1,8]{1,0:T(1,128)}, u32[]{:S(2)}) copy-start(s32[1,8]{1,0:T(1,128)} %radius_map.1) | copy-start | bytes 100
  35.6 11.1 %all-to-all-start = ((f32[32,8,72]{2,1,0:T(8,128)}), f32[32,8,72]{2,1,0:T(8,128)S(1)}, u32[]{:S(2)}, u32[]{:S(2)}) async-start(f32[32,8,72]{2,1,0:T(8,128)} %bitcast.1), calls=%async_computation | async-start | bytes 262144 | tf_op jit(solution)/shard_map/all_to_all | solution.py:886
